TPU v7x, 32 devices: a whole 2x2x4 slice. The times are simulated.
32 devices in a mesh: groups: 2 (over x), seq: 16 (over z, y, core).
Axes of the slice: x: 2, y: 2, z: 4, core: 2. Of those that a mesh axis runs over, the one named last changes fastest.
Arguments:
- projected: bfloat16 [4096, 3072], P(('groups', 'seq')), parts along dimension 0, may hold values from -6 to 6
- decay_log: bfloat16 [4096, 8], P(('groups', 'seq')), parts along dimension 0, may hold values from -0.7 to 0
- destination: int32 [4096], P(('groups', 'seq')), parts along dimension 0, may hold values from 0 to 2047, as said below
- source: int32 [4096], P(('groups', 'seq')), parts along dimension 0, may hold values from 0 to 2047, as said below
- starts: int32 [4096], P(('groups', 'seq')), parts along dimension 0, may hold values from 0 to 1, as said below
- upstream: bfloat16 [4096, 2048], P(('groups', 'seq')), parts along dimension 0, may hold values from -6 to 6
- out_weight: bfloat16 [1024, 2048], replicated, may hold values from -0.1875 to 0.1875
Outputs:
- grad_projected: bfloat16 [4096, 3072], P(('groups', 'seq')), parts along dimension 0
- grad_weight: bfloat16 [32768, 2048], P(('groups', 'seq')), parts along dimension 0
There are 2 independent parts, one for each index of `groups`. A program takes and returns all parts, laid end to end along the dimension named above; an argument that names none is the same for every part. Nothing has to cross between parts.
Inputs may be any that keep to these rules, and one draw needn't show every extreme that they name: `destination`: each rollout, padded to a whole number of groups of 16 packed rows, is dealt row by row to the owners in turn, starting at a first owner of its own; the i-th row of owner o goes to packed position i * 16 + (o - that rollout's first owner) mod 16. So every position is named once, each owner holds its rows in packed order, and each owner sends exactly 8 rows to each shard. source[destination[o]] = o for every owner row o. `starts`: 1 marks the first packed row of a rollout and the first row of the padding at a rollout's end, if it has any; each rollout with its padding covers a whole number of groups of 16 rows, and its padding fewer than 16 rows.
All inputs are finite; a program needn't handle non-finite values.
Results may differ from a plain program's by a relative error of at most 0.0064.
Values may be sent and summed in bfloat16 or wider, within the bound.
No kernel may reach another device: no remote copies, remote signals or barrier semaphores. Data moves between devices by JAX's collectives and lax.ppermute only.
A program may use at most 320 MiB of HBM per device.

v0:
```python
import jax
import jax.numpy as jnp
from jax import lax
from jax.sharding import PartitionSpec as P

norm_eps = 1e-06
highest = lax.Precision.HIGHEST


def prefix(value, axis, join, neutral, backward):
    count, mine = (lax.axis_size(axis), lax.axis_index(axis))
    pieces = jax.tree.map(lambda part: lax.all_gather(part, axis), value)
    if backward:
        pieces = jax.tree.map(lambda part: part[::-1], pieces)
        mine = count - 1 - mine
    subtotal = jax.tree.map(
        lambda part, zero: jnp.full_like(part, 0) + jnp.asarray(zero, part.dtype), value, neutral
    )

    def hop(position, subtotal):
        longer = join(subtotal, jax.tree.map(lambda part: part[position], pieces))
        return jax.tree.map(lambda new, old: jnp.where(position < mine, new, old), longer, subtotal)

    return lax.fori_loop(0, count - 1, hop, subtotal)


def combine_states(earlier, later):
    return (earlier[0] * later[0], later[0][:, None, None] * earlier[1] + later[1])


def within_rank(group_ids, order_keys):
    same = group_ids[:, None] == group_ids[None, :]
    before = order_keys[None, :] < order_keys[:, None]
    return jnp.sum((same & before).astype(jnp.int32), axis=1)


def decay_terms(log_decay, begin_flags):
    row_count = log_decay.shape[0]
    segment = jnp.cumsum(begin_flags, dtype=jnp.int32)
    running = jnp.cumsum(log_decay, axis=0).T
    position = jnp.arange(row_count, dtype=jnp.int32)
    same = (segment[:, None] == segment[None, :]) & (position[None, :] <= position[:, None])
    spread_gap = jnp.minimum(running[:, :, None] - running[:, None, :], 0.0)
    decay_mix = jnp.where(same[None, :, :], jnp.exp(spread_gap), 0.0)
    enter_decay = jnp.where(segment[None, :] == 0, jnp.exp(running), 0.0)
    leave_decay = jnp.where(
        segment[None, :] == segment[-1], jnp.exp(jnp.minimum(running[:, -1:] - running, 0.0)), 0.0
    )
    return (decay_mix, enter_decay, leave_decay)


def shards(projected, decay_log, destination, source, starts, upstream, out_weight):
    row_count = projected.shape[0]
    inner_width = projected.shape[1] // 3
    head_count = decay_log.shape[1]
    head_width = inner_width // head_count
    peers = lax.axis_size("seq")
    capacity = row_count // peers
    position = jnp.arange(row_count, dtype=jnp.int32)
    target = destination // row_count
    send_slot = target * capacity + within_rank(target, position)
    anchor = source // row_count
    take_slot = anchor * capacity + within_rank(anchor, source)

    def spread(payload, slots):
        buffer = (
            jnp.zeros((peers * capacity, payload.shape[1]), payload.dtype).at[slots].set(payload)
        )
        return buffer.reshape(peers, capacity, payload.shape[1])

    def collect(arrived, slots):
        return arrived.reshape(peers * capacity, arrived.shape[2])[slots]

    arrived, arrived_decay = (
        lax.all_to_all(
            spread(projected[:, inner_width:], send_slot),
            "seq",
            split_axis=0,
            concat_axis=0,
            tiled=True,
        ),
        lax.all_to_all(
            spread(decay_log, send_slot), "seq", split_axis=0, concat_axis=0, tiled=True
        ),
    )
    pair_rows = collect(arrived, take_slot)
    log_rows = collect(arrived_decay, take_slot).astype(jnp.float32)
    decay_mix, enter_decay, leave_decay = decay_terms(log_rows, starts)
    key_rows = pair_rows[:, :inner_width].reshape(row_count, head_count, head_width)
    value_rows = pair_rows[:, inner_width:].reshape(row_count, head_count, head_width)
    key_wide = key_rows.astype(jnp.float32)
    value_wide = value_rows.astype(jnp.float32)
    local_state = jnp.einsum(
        "shd,she->hde", key_wide * leave_decay.T[:, :, None], value_wide, precision=highest
    )
    total_decay = enter_decay[:, -1]
    identity = (jnp.ones_like(total_decay), jnp.zeros_like(local_state))
    state_in = prefix((total_decay, local_state), "seq", combine_states, identity, False)[1]
    query_rows = collect(
        lax.all_to_all(
            spread(projected[:, :inner_width], send_slot),
            "seq",
            split_axis=0,
            concat_axis=0,
            tiled=True,
        ),
        take_slot,
    )
    queries = query_rows.reshape(row_count, head_count, head_width)
    query_wide = queries.astype(jnp.float32)
    scores = jnp.einsum("ihd,shd->his", queries, key_rows, preferred_element_type=jnp.float32)
    weights = (scores * decay_mix).astype(jnp.bfloat16)
    output = jnp.einsum("his,she->ihe", weights, value_rows, preferred_element_type=jnp.float32)
    output = output + enter_decay.T[:, :, None] * jnp.einsum(
        "ihd,hde->ihe", query_wide, state_in, precision=highest
    )
    norm_scale = jnp.sqrt(jnp.mean(output * output, axis=2, keepdims=True) + norm_eps)
    normed = output / norm_scale
    normed_low = normed.astype(jnp.bfloat16).reshape(row_count, inner_width)
    grad_weight = lax.dot_general(
        normed_low, upstream, (((0,), (0,)), ((), ())), preferred_element_type=jnp.float32
    ).astype(jnp.bfloat16)
    grad_normed = lax.dot_general(
        upstream, out_weight, (((1,), (1,)), ((), ())), preferred_element_type=jnp.float32
    )
    grad_normed = grad_normed.reshape(row_count, head_count, head_width)
    grad_output = (
        (grad_normed - normed * jnp.mean(grad_normed * normed, axis=2, keepdims=True)) / norm_scale
    ).astype(jnp.bfloat16)
    grad_wide = grad_output.astype(jnp.float32)
    grad_mix = (
        jnp.einsum("ihe,she->his", grad_output, value_rows, preferred_element_type=jnp.float32)
        * decay_mix
    ).astype(jnp.bfloat16)
    grad_query = jnp.einsum("his,shd->ihd", grad_mix, key_rows, preferred_element_type=jnp.float32)
    grad_query = grad_query + enter_decay.T[:, :, None] * jnp.einsum(
        "ihe,hde->ihd", grad_wide, state_in, precision=highest
    )
    query_low = grad_query.reshape(row_count, inner_width).astype(jnp.bfloat16)
    reverse_local = jnp.einsum(
        "thd,the->hde", query_wide * enter_decay.T[:, :, None], grad_wide, precision=highest
    )
    state_back = prefix((total_decay, reverse_local), "seq", combine_states, identity, True)[1]
    grad_key = jnp.einsum("his,ihd->shd", grad_mix, queries, preferred_element_type=jnp.float32)
    grad_key = grad_key + leave_decay.T[:, :, None] * jnp.einsum(
        "hde,she->shd", state_back, value_wide, precision=highest
    )
    grad_value = jnp.einsum(
        "his,ihe->she", weights, grad_output, preferred_element_type=jnp.float32
    )
    grad_value = grad_value + leave_decay.T[:, :, None] * jnp.einsum(
        "hde,shd->she", state_back, key_wide, precision=highest
    )
    pair_low = jnp.concatenate(
        [grad_key.reshape(row_count, inner_width), grad_value.reshape(row_count, inner_width)],
        axis=1,
    ).astype(jnp.bfloat16)
    grad_rows = jnp.concatenate([query_low, pair_low], axis=1)
    grad_projected = collect(
        lax.all_to_all(
            spread(grad_rows, take_slot), "seq", split_axis=0, concat_axis=0, tiled=True
        ),
        send_slot,
    )
    return (grad_projected, grad_weight)


def solution(mesh):
    placed = (
        P(("groups", "seq"), None),
        P(("groups", "seq"), None),
        P(("groups", "seq")),
        P(("groups", "seq")),
        P(("groups", "seq")),
        P(("groups", "seq"), None),
        P(),
    )
    return jax.shard_map(
        shards,
        mesh=mesh,
        in_specs=placed,
        out_specs=(P(("groups", "seq"), None), P(("groups", "seq"), None)),
        check_vma=False,
    )
```

profile of v0, /device:TPU:18, one launch (start us, length us, event | category | flops | bytes accessed | tf_op | source)
XLA Modules:
  0.0 285.0 jit_solution(12024699350426141128)
XLA Ops:
  9.6 1.4 scatter_custom_fusion.2
  11.0 6.2 %all-to-all-start.2 = ((bf16[16,8,8]{2,1,0:T(8,128)(2,1)}), bf16[16,8,8]{2,1,0:T(8,128)(2,1)S(1)}, u32[]{:S(2)}, u32[]{:S(2)}) async-start(bf16[16,8,8]{2,1,0:T(8,128)(2,1)} %bitcast.8), calls=%async_computation.2 | async-start | bytes 65536 | tf_op jit(solution)/shard_map/all_to_all | solution.py:82
  20.4 2.7 scatter_custom_fusion
  23.1 6.0 %all-to-all-start = ((bf16[16,8,2048]{2,1,0:T(8,128)(2,1)}), bf16[16,8,2048]{2,1,0:T(8,128)(2,1)S(1)}, u32[]{:S(2)}, u32[]{:S(2)}) async-start(bf16[16,8,2048]{2,1,0:T(8,128)(2,1)} %bitcast), calls=%async_computation | async-start | bytes 1048576 | tf_op jit(solution)/shard_map/all_to_all | solution.py:75
  31.6 11.4 %all-to-all-done = bf16[16,8,2048]{2,1,0:T(8,128)(2,1)S(1)} async-done(((bf16[16,8,2048]{2,1,0:T(8,128)(2,1)}), bf16[16,8,2048]{2,1,0:T(8,128)(2,1)S(1)}, u32[]{:S(2)}, u32[]{:S(2)}) %all-to-all-start) | async-done | bytes 524320 | tf_op jit(solution)/shard_map/all_to_all | solution.py:75
  44.3 1.5 fusion.18
  45.8 2.2 scatter_custom_fusion.1
  48.0 4.7 %all-to-all-start.1 = ((bf16[16,8,1024]{2,1,0:T(8,128)(2,1)}), bf16[16,8,1024]{2,1,0:T(8,128)(2,1)S(1)}, u32[]{:S(2)}, u32[]{:S(2)}) async-start(bf16[16,8,1024]{2,1,0:T(8,128)(2,1)} %bitcast.4), calls=%async_computation.1 | async-start | bytes 524288 | tf_op jit(solution)/shard_map/all_to_all | solution.py:100
  55.4 29.7 %all-reduce = f32[128]{0:T(128)S(1)} all-reduce(f32[128]{0:T(128)S(1)} %fusion.36), channel_id=2, replica_groups=mesh['groups'=2,'seq'=16] {'seq'}, use_global_device_ids=true, to_apply=%add | all-reduce | flops 128 | bytes 1024
  86.7 37.5 %all-gather.6.cloned.1.call-done = f32[128,128,128]{2,1,0:T(8,128)} async-done(((f32[8,128,128]{2,1,0:T(8,128)}), f32[128,128,128]{2,1,0:T(8,128)}) %all-gather.6.cloned.1.call-update) | async-done | bytes 8388624 | tf_op jit(solution)/shard_map/all_gather | solution.py:12
  124.1 18.2 %while.28 = (s32[]{:T(128)}, f32[8,128,128]{2,1,0:T(8,128)S(1)}, s32[]{:T(128)}, f32[16,8]{1,0:T(8,128)S(1)}, f32[16,8,128,128]{3,2,1,0:T(8,128)}, /*index=5*/s32[]{:T(128)}, s32[]{:T(128)}) while((s32[]{:T(128)}, f32[8,128,128]{2,1,0:T(8,128)S(1)}, s32[]{:T(128)}, f32[16,8]{1,0:T(8,128)S(1)}, f32[16,8,128,128]{3,2,1,0:T(8,128)}, ...), condition=%wide.region_8.9_spmd.clone, body=%wide.region_7.8_spmd.clone.sunk | while | flops 524292 | bytes 1573065 | solution.py:24
  125.4 1.2 fusion.67
  126.6 1.2 fusion.67
  127.8 1.2 fusion.67
  130.2 1.2 fusion.67
  132.6 1.2 fusion.67
  135.1 1.2 fusion.67
  137.5 1.2 fusion.67
  139.9 1.2 fusion.67
  143.3 3.5 %multiply_reduce_fusion = (f32[128,8]{0,1:T(8,128)S(1)}, f32[128,1024]{0,1:T(8,128)S(1)}) fusion(f32[128,8,128]{0,2,1:T(8,128)S(1)} %get-tuple-element.257, f32[128,8]{0,1:T(8,128)S(1)} %add_sqrt_fusion, bf16[128,2048]{1,0:T(8,128)(2,1)S(1)} %copy-done, bf16[1024,2048]{1,0:T(8,128)(2,1)} %param.17), kind=kOutput, calls=%fused_computation.43 | convolution fusion | flops 537263104 | bytes 5775360 | tf_op jit(solution)/shard_map/reshape | solution.py:126
  146.9 1.5 fusion.15
  150.1 71.6 %all-gather.8.cloned.1.call-done = f32[128,128,128]{2,1,0:T(8,128)} async-done(((f32[8,128,128]{2,1,0:T(8,128)}), f32[128,128,128]{2,1,0:T(8,128)}) %all-gather.8.cloned.1.call-update) | async-done | bytes 8388624 | tf_op jit(solution)/shard_map/all_gather | solution.py:12
  221.7 7.7 %rev.7 = f32[16,8,128,128]{3,2,1,0:T(8,128)} reverse(f32[16,8,128,128]{3,2,1,0:T(8,128)} %bitcast.116), dimensions={0} | reverse | bytes 16777216 | tf_op jit(solution)/shard_map/rev | solution.py:14
  229.4 18.2 %while.29 = (s32[]{:T(128)}, f32[8,128,128]{2,1,0:T(8,128)S(1)}, s32[]{:T(128)}, f32[16,8]{1,0:T(8,128)S(1)}, f32[16,8,128,128]{3,2,1,0:T(8,128)}, /*index=5*/s32[]{:T(128)}, s32[]{:T(128)}) while((s32[]{:T(128)}, f32[8,128,128]{2,1,0:T(8,128)S(1)}, s32[]{:T(128)}, f32[16,8]{1,0:T(8,128)S(1)}, f32[16,8,128,128]{3,2,1,0:T(8,128)}, ...), condition=%wide.region_12.13_spmd.clone, body=%wide.region_11.12_spmd.clone.sunk | while | flops 524292 | bytes 1573065 | solution.py:24
  231.8 1.2 fusion.68
  233.0 1.2 fusion.68
  234.2 1.2 fusion.68
  249.4 2.6 scatter_custom_fusion.3
  251.9 4.8 %all-to-all-start.3 = ((bf16[16,8,3072]{2,1,0:T(8,128)(2,1)}), bf16[16,8,3072]{2,1,0:T(8,128)(2,1)S(1)}, u32[]{:S(2)}, u32[]{:S(2)}) async-start(bf16[16,8,3072]{2,1,0:T(8,128)(2,1)} %bitcast.28), calls=%async_computation.3 | async-start | bytes 1572864 | tf_op jit(solution)/shard_map/all_to_all | solution.py:160
  256.8 3.3 %convolution_convert_fusion = bf16[1024,2048]{1,0:T(8,128)(2,1)} fusion(bf16[128,1024]{0,1:T(8,128)(2,1)S(1)} %bitcast.131, bf16[128,2048]{1,0:T(8,128)(2,1)S(1)} %copy-done), kind=kOutput, calls=%fused_computation.14 | convolution fusion | flops 538968064 | bytes 4980736 | tf_op jit(solution)/shard_map/dot_general | solution.py:120
  260.0 16.3 %all-to-all-done.3 = bf16[16,8,3072]{2,1,0:T(8,128)(2,1)S(1)} async-done(((bf16[16,8,3072]{2,1,0:T(8,128)(2,1)}), bf16[16,8,3072]{2,1,0:T(8,128)(2,1)S(1)}, u32[]{:S(2)}, u32[]{:S(2)}) %all-to-all-start.3) | async-done | bytes 786464 | tf_op jit(solution)/shard_map/all_to_all | solution.py:160
  276.3 1.9 gather_fusion.3
  (112 shorter events, 40.1 us)
Async XLA Ops:
  7.2 136.1 %copy-start = (bf16[128,2048]{1,0:T(8,128)(2,1)S(1)}, bf16[128,2048]{1,0:T(8,128)(2,1)}, u32[]{:S(2)}) copy-start(bf16[128,2048]{1,0:T(8,128)(2,1)} %param.16) | copy-start | bytes 1572868
  11.0 12.1 %all-to-all-start.2 = ((bf16[16,8,8]{2,1,0:T(8,128)(2,1)}), bf16[16,8,8]{2,1,0:T(8,128)(2,1)S(1)}, u32[]{:S(2)}, u32[]{:S(2)}) async-start(bf16[16,8,8]{2,1,0:T(8,128)(2,1)} %bitcast.8), calls=%async_computation.2 | async-start | bytes 65536 | tf_op jit(solution)/shard_map/all_to_all | solution.py:82
  23.1 19.9 %all-to-all-start = ((bf16[16,8,2048]{2,1,0:T(8,128)(2,1)}), bf16[16,8,2048]{2,1,0:T(8,128)(2,1)S(1)}, u32[]{:S(2)}, u32[]{:S(2)}) async-start(bf16[16,8,2048]{2,1,0:T(8,128)(2,1)} %bitcast), calls=%async_computation | async-start | bytes 1048576 | tf_op jit(solution)/shard_map/all_to_all | solution.py:75
  29.1 95.1 %all-gather.6.cloned.1.call-start = ((), (), s32[]{:S(2)}) async-start(), calls=%async_computation.4 | async-start | bytes 8912896 | tf_op jit(solution)/shard_map/all_gather | solution.py:12
  43.0 10.4 %copy-start.2 = (u32[32]{0:T(128)S(1)}, u32[32]{0:T(128)}, u32[]{:S(2)}) copy-start(u32[32]{0:T(128)} %constant.103) | copy-start | bytes 388
  48.0 37.3 %all-to-all-start.1 = ((bf16[16,8,1024]{2,1,0:T(8,128)(2,1)}), bf16[16,8,1024]{2,1,0:T(8,128)(2,1)S(1)}, u32[]{:S(2)}, u32[]{:S(2)}) async-start(bf16[16,8,1024]{2,1,0:T(8,128)(2,1)} %bitcast.4), calls=%async_computation.1 | async-start | bytes 524288 | tf_op jit(solution)/shard_map/all_to_all | solution.py:100
  52.7 169.0 %all-gather.8.cloned.1.call-start = ((), (), s32[]{:S(2)}) async-start(), calls=%async_computation.5 | async-start | bytes 8912896 | tf_op jit(solution)/shard_map/all_gather | solution.py:12
  247.6 1.5 copy-start.1
  251.9 24.3 %all-to-all-start.3 = ((bf16[16,8,3072]{2,1,0:T(8,128)(2,1)}), bf16[16,8,3072]{2,1,0:T(8,128)(2,1)S(1)}, u32[]{:S(2)}, u32[]{:S(2)}) async-start(bf16[16,8,3072]{2,1,0:T(8,128)(2,1)} %bitcast.28), calls=%async_computation.3 | async-start | bytes 1572864 | tf_op jit(solution)/shard_map/all_to_all | solution.py:160
Sparse Core Ops, SparseCore 0:
  45.9 78.1 all-gather.5
  148.5 73.1 all-gather.7
where the time goes:
time: 288 us; the launch traced here: 285 us
  waiting for transfers between devices  137 us (48%)
  other arithmetic  41.3 us (14%)
  blocking collectives  29.7 us (10%)
  local copies, waits for them, and re-layouts  25.8 us (9%)
  starting transfers between devices  21.8 us (8%)
  between operations  14.9 us (5%)
  matrix products  14 us (5%)
    all_gather x2, waiting for transfers between devices, prefix(): pieces = jax.tree.map(lambda part: lax.all_gather(part, axis), value)  109 us
    select_n x30, other arithmetic, hop(): jnp.where(position < mine, new, old)  35.2 us
    unnamed x1, blocking collectives  29.7 us
    all_to_all x1, waiting for transfers between devices, shards(): lax.all_to_all(spread(grad_rows, take_slot), 'seq', split_axis=0, concat_...  16.3 us
    all_to_all x1, waiting for transfers between devices, shards(): lax.all_to_all(spread(projected[:, inner_width:], send_slot), 'seq', spli...  11.4 us
    scatter x4, local copies, waits for them, and re-layouts, spread(): jnp.zeros((peers * capacity, payload.shape[1]), payload.dtype).at[slots]  8.91 us
    rev x2, local copies, waits for them, and re-layouts, prefix(): pieces = jax.tree.map(lambda part: part[::-1], pieces)  7.72 us
    all_to_all x1, starting transfers between devices, shards(): lax.all_to_all(spread(decay_log, send_slot), 'seq', split_axis=0, concat_...  6.18 us
  transfers between devices with their start and end apart: 6, of which 4 were waited for; matrix products, arithmetic and copies ran while one was open for 7% of the time, Pallas kernels for 0%

commit v1 on v0

v1 whole, which is shorter than its diff:
```python
import functools

import jax
import jax.numpy as jnp
from jax import lax
from jax.experimental import pallas as pl
from jax.experimental.pallas import tpu as pltpu
from jax.sharding import PartitionSpec as P

norm_eps = 1e-06
LANES = 128
CHUNK = 256
META = 8
bf16 = jnp.bfloat16
f32 = jnp.float32

VMEM = pl.BlockSpec(memory_space=pltpu.VMEM)
SMEM = pl.BlockSpec(memory_space=pltpu.SMEM)
PARAMS = pltpu.CompilerParams(vmem_limit_bytes=48 * 1024 * 1024)


def dot(a, b):
    return lax.dot_general(a, b, (((1,), (0,)), ((), ())), preferred_element_type=f32)


def dot_nt(a, b):
    return lax.dot_general(a, b, (((1,), (1,)), ((), ())), preferred_element_type=f32)


def dot_tn(a, b):
    return lax.dot_general(a, b, (((0,), (0,)), ((), ())), preferred_element_type=f32)


def halves(value):
    high = value.astype(bf16)
    return high, (value - high.astype(f32)).astype(bf16)


def wide(value):
    return jnp.concatenate([value] * (CHUNK // LANES), axis=1)


def iota(shape, dim):
    return lax.broadcasted_iota(jnp.int32, shape, dim)


def call(body, outs, ins, flops=0, moved=0, **more):
    return pl.pallas_call(
        body,
        out_shape=outs,
        compiler_params=PARAMS,
        cost_estimate=pl.CostEstimate(flops=flops, bytes_accessed=moved, transcendentals=0),
        **more,
    )(*ins)


def pack_kernel(heads, segments, rows_ref, decay_ref, starts_ref, out_ref):
    per = rows_ref.shape[0] // segments
    inner = heads * LANES
    eye = jnp.where(iota((LANES, LANES), 0) == iota((LANES, LANES), 1), 1.0, 0.0).astype(bf16)
    decay_rows = dot_tn(decay_ref[...], eye)
    flags = starts_ref[...].astype(f32)
    line = iota((META, LANES), 0)
    for head in range(heads):
        meta = jnp.where(line == 0, decay_rows[head : head + 1, :], jnp.where(line == 1, flags, 0.0))
        for segment in range(segments):
            to = segment * heads + head
            for part in range(3):
                at = part * inner + head * LANES
                out_ref[to, part * per : (part + 1) * per, :] = rows_ref[
                    segment * per : (segment + 1) * per, at : at + LANES
                ]
            out_ref[to, 3 * per :, :] = meta.astype(bf16)


def pack(projected, decay_log, starts, heads, segments):
    rows = projected.shape[0]
    per = rows // segments
    peers = heads * segments
    if per % 16 == 0:
        return call(
            functools.partial(pack_kernel, heads, segments),
            jax.ShapeDtypeStruct((peers, 3 * per + META, LANES), bf16),
            (projected, decay_log, starts.reshape(1, rows)),
            moved=4 * projected.size,
            in_specs=[VMEM] * 3,
            out_specs=VMEM,
        )
    body = projected.reshape(segments, per, 3, heads, LANES).transpose(0, 3, 2, 1, 4)
    body = body.reshape(peers, 3 * per, LANES)
    flags = jnp.broadcast_to(starts.astype(bf16)[None, None, :], (heads, 1, rows))
    meta = jnp.concatenate(
        [decay_log.T[:, None, :], flags, jnp.zeros((heads, META - 2, rows), bf16)], axis=1
    )
    meta = jnp.broadcast_to(meta[None], (segments, heads, META, LANES)).reshape(peers, META, LANES)
    return jnp.concatenate([body, meta], axis=1)


def unpack_kernel(heads, segments, in_ref, out_ref):
    per = out_ref.shape[0] // segments
    inner = heads * LANES
    for segment in range(segments):
        for head in range(heads):
            for part in range(3):
                at = part * inner + head * LANES
                out_ref[segment * per : (segment + 1) * per, at : at + LANES] = in_ref[
                    segment * heads + head, part * per : (part + 1) * per, :
                ]


def unpack(arrived, rows, heads, segments):
    per = rows // segments
    if per % 16 == 0:
        return call(
            functools.partial(unpack_kernel, heads, segments),
            jax.ShapeDtypeStruct((rows, 3 * heads * LANES), bf16),
            (arrived,),
            moved=4 * arrived.size,
            in_specs=[VMEM],
            out_specs=VMEM,
        )
    body = arrived.reshape(segments, heads, 3, per, LANES).transpose(0, 3, 2, 1, 4)
    return body.reshape(rows, 3 * heads * LANES)


def grad_normed_kernel(up_ref, order_ref, weight_ref, out_ref, turned_ref):
    @pl.when(pl.program_id(0) == 0)
    def _():
        rows = up_ref.shape[0]
        pick = iota((rows, rows), 1).astype(f32) == order_ref[...]
        turned_ref[...] = dot(jnp.where(pick, 1.0, 0.0).astype(bf16), up_ref[...]).astype(bf16)

    out_ref[0] = dot_nt(turned_ref[...], weight_ref[...])


def grad_normed_of(upstream, order, out_weight, heads):
    rows, width = upstream.shape
    return call(
        grad_normed_kernel,
        (
            jax.ShapeDtypeStruct((heads, rows, LANES), f32),
            jax.ShapeDtypeStruct((rows, width), bf16),
        ),
        (upstream, order, out_weight),
        flops=2 * rows * out_weight.size,
        moved=2 * (2 * upstream.size + out_weight.size),
        grid=(heads,),
        in_specs=[
            pl.BlockSpec((rows, width), lambda i: (0, 0)),
            pl.BlockSpec((rows, LANES), lambda i: (0, 0)),
            pl.BlockSpec((LANES, width), lambda i: (i, 0)),
        ],
        out_specs=[
            pl.BlockSpec((1, rows, LANES), lambda i: (i, 0, 0)),
            pl.BlockSpec((rows, width), lambda i: (0, 0)),
        ],
    )


def grad_weight_kernel(normed_ref, up_ref, out_ref):
    out_ref[...] = dot_tn(normed_ref[0], up_ref[...]).astype(bf16)


def grad_weight_of(normed, upstream):
    heads, rows, _ = normed.shape
    width = upstream.shape[1]
    return call(
        grad_weight_kernel,
        jax.ShapeDtypeStruct((heads * LANES, width), bf16),
        (normed, upstream),
        flops=2 * rows * heads * LANES * width,
        moved=2 * (upstream.size + normed.size + heads * LANES * width),
        grid=(heads,),
        in_specs=[
            pl.BlockSpec((1, rows, LANES), lambda i: (i, 0, 0)),
            pl.BlockSpec((rows, width), lambda i: (0, 0)),
        ],
        out_specs=pl.BlockSpec((LANES, width), lambda i: (i, 0)),
    )


def part_rows(ref, part, chunk):
    per = ref.shape[1] // 3
    if ref.shape[1] % 16:
        per = (ref.shape[1] - META) // 3
    at = part * per + chunk * 16
    return ref[:, at : at + 16, :].reshape(CHUNK, LANES)


def masks(column_ref, line_ref, chunk):
    column = wide(column_ref[chunk])
    line = line_ref[chunk, 0:1, :]
    return column, line


def forward_kernel(
    chunks, per_seg, where_ref, rows_ref, meta_ref, column_ref, line_ref,
    mix_ref, weights_ref, enter_ref, leave_ref, inner_ref, before_ref, state_ref, last_ref, gains_ref,
):
    owners = meta_ref.shape[0]
    per = CHUNK // owners
    segment = where_ref[0]
    first_block = where_ref[1]
    group = CHUNK // LANES
    meta = meta_ref[...].astype(f32).reshape(owners * META, LANES).astype(bf16)
    row = iota((CHUNK, owners * META), 0)
    pick = jnp.where(iota((CHUNK, owners * META), 1) == (row // per) * META, 1.0, 0.0).astype(bf16)
    all_decay = dot(pick, meta)
    lane = iota((CHUNK, LANES), 1)
    slot = iota((CHUNK, LANES), 0) % per
    ones = jnp.ones((LANES, LANES), bf16)
    place = iota((CHUNK, CHUNK), 1).astype(f32)
    state = jnp.zeros((LANES, LANES), f32)
    before = jnp.ones((1, LANES), f32)
    for chunk in range(chunks):
        column, line = masks(column_ref, line_ref, chunk)
        order = line <= column
        chosen = lane == segment * per_seg + chunk * per + slot
        decay = dot(jnp.where(chosen, all_decay, 0.0).astype(bf16), ones).astype(bf16)
        running = dot(jnp.where(order, 1.0, 0.0).astype(bf16), decay)
        flags = jnp.concatenate(
            [
                meta_ref[first_block + chunk * group + i].astype(f32)[1:2, :]
                for i in range(group)
            ],
            axis=1,
        )
        flags = jnp.broadcast_to(flags, (LANES, CHUNK)).astype(bf16)
        count = dot_nt(jnp.where(place <= column, 1.0, 0.0).astype(bf16), flags)
        turned = jnp.where(lane == 0, running, count).T
        gap = jnp.minimum(wide(running) - turned[0:1, :], 0.0)
        same = order & (wide(count) == turned[1:2, :])
        mix = jnp.where(same, jnp.exp(gap), 0.0)
        last_run = jnp.min(running, axis=0, keepdims=True)
        last_count = jnp.max(count, axis=0, keepdims=True)
        enter = jnp.where(count == 0.0, jnp.exp(running), 0.0)
        leave = jnp.where(
            count == last_count, jnp.exp(jnp.minimum(last_run - running, 0.0)), 0.0
        )
        total = jnp.where(last_count == 0.0, jnp.exp(last_run), 0.0)
        query, key, value = (part_rows(rows_ref, part, chunk) for part in range(3))
        weights = (dot_nt(query, key) * mix).astype(bf16)
        high, low = halves(key.astype(f32) * leave)
        local = dot_tn(high, value) + dot_tn(low, value)
        mix_ref[chunk] = mix
        weights_ref[chunk] = weights
        enter_ref[chunk] = enter
        leave_ref[chunk] = leave
        inner_ref[chunk] = dot(weights, value)
        gains_ref[chunk] = jnp.broadcast_to(total, (8, LANES))
        before_ref[chunk] = jnp.broadcast_to(before, (8, LANES))
        state_ref[chunk] = state
        state = total * state + local
        before = total * before
    last_ref[...] = state
    before_ref[chunks] = jnp.broadcast_to(before, (8, LANES))


def middle_kernel(
    chunks, runs, rows_ref, mix_ref, weights_ref, enter_ref, inner_ref, before_ref,
    state_ref, gains_ref, came_ref, normal_ref,
    normed_ref, query_ref, key_ref, value_ref, back_ref, after_ref, last_ref,
):
    group = CHUNK // LANES
    back = jnp.zeros((LANES, LANES), f32)
    after = jnp.ones((1, LANES), f32)
    came = came_ref[...]
    for chunk in reversed(range(chunks)):
        query, key, value = (part_rows(rows_ref, part, chunk) for part in range(3))
        enter = enter_ref[chunk]
        mix = mix_ref[chunk]
        high, low = halves(state_ref[chunk] + before_ref[chunk, 0:1, :] * came)
        output = inner_ref[chunk] + enter * (dot(query, high) + dot(query, low))
        scale = lax.rsqrt(jnp.mean(output * output, axis=1, keepdims=True) + norm_eps)
        normed = output * scale
        split = normed.reshape(runs, group, CHUNK // (runs * group), LANES)
        for i in range(group):
            normed_ref[chunk * group + i] = split[:, i].reshape(LANES, LANES).astype(bf16)
        normal = jnp.concatenate(
            [
                normal_ref[chunk * group + i].reshape(runs, 1, CHUNK // (runs * group), LANES)
                for i in range(group)
            ],
            axis=1,
        ).reshape(CHUNK, LANES)
        grad = (
            (normal - normed * jnp.mean(normal * normed, axis=1, keepdims=True)) * scale
        ).astype(bf16)
        grad_mix = (dot_nt(grad, value) * mix).astype(bf16)
        grad_query = dot(grad_mix, key) + enter * (dot_nt(grad, high) + dot_nt(grad, low))
        query_ref[:, chunk * 16 : (chunk + 1) * 16, :] = (
            grad_query.astype(bf16).reshape(16, 16, LANES)
        )
        key_ref[chunk] = dot_tn(grad_mix, query)
        value_ref[chunk] = dot_tn(weights_ref[chunk], grad)
        high, low = halves(query.astype(f32) * enter)
        local = dot_tn(high, grad) + dot_tn(low, grad)
        back_ref[chunk] = back
        after_ref[chunk] = jnp.broadcast_to(after, (8, LANES))
        gain = gains_ref[chunk, 0:1, :]
        back = gain * back + local
        after = gain * after
    last_ref[...] = back


def backward_kernel(
    chunks, rows_ref, leave_ref, query_ref, key_ref, value_ref, back_ref, after_ref, came_ref, out_ref
):
    per = chunks * 16
    came = came_ref[...]
    out_ref[:, 0:per, :] = query_ref[...]
    for chunk in range(chunks):
        key, value = (part_rows(rows_ref, part, chunk) for part in (1, 2))
        leave = leave_ref[chunk]
        high, low = halves(back_ref[chunk] + after_ref[chunk, 0:1, :] * came)
        grad_key = key_ref[chunk] + leave * (dot_nt(value, high) + dot_nt(value, low))
        grad_value = value_ref[chunk] + leave * (dot(key, high) + dot(key, low))
        for part, grad in ((1, grad_key), (2, grad_value)):
            at = part * per + chunk * 16
            out_ref[:, at : at + 16, :] = grad.astype(bf16).reshape(16, 16, LANES)


def carried(last, gain, segments, heads, step):
    def shift(value, by):
        pairs = [
            (s * heads + h, (s + by * step) * heads + h)
            for s in range(segments)
            for h in range(heads)
            if 0 <= s + by * step < segments
        ]
        return lax.ppermute(value, "seq", pairs)

    state = shift(last, 1)
    if segments > 2:
        gain = shift(gain, 1)
        by = 1
        while by < segments - 1:
            state, gain = state + gain[0:1, :] * shift(state, by), gain * shift(gain, by)
            by *= 2
    return state


def shards(projected, decay_log, destination, source, starts, upstream, out_weight):
    rows = projected.shape[0]
    heads = decay_log.shape[1]
    peers = lax.axis_size("seq")
    segments = peers // heads
    per_seg = rows // segments
    chunks = heads * rows // CHUNK
    per = CHUNK // peers
    me = lax.axis_index("seq")
    segment = me // heads
    groups = [[s * heads + h for h in range(heads)] for s in range(segments)]

    mine = lax.dynamic_slice(destination, (segment * per_seg,), (per_seg,)).reshape(chunks, 1, per)
    owner = jnp.arange(peers, dtype=jnp.int32).reshape(1, peers, 1)
    spot = jnp.arange(per, dtype=jnp.int32).reshape(1, 1, per)
    position = spot * peers + (owner - me + mine) % peers
    position = position.reshape(chunks, CHUNK).astype(f32)
    column = jnp.broadcast_to(position[:, :, None], (chunks, CHUNK, LANES))
    line = jnp.broadcast_to(position[:, None, :], (chunks, 8, CHUNK))
    capacity = rows // peers
    mine = lax.dynamic_slice(destination, (me * capacity,), (capacity,)).reshape(1, capacity)
    spot = jnp.arange(capacity, dtype=jnp.int32).reshape(1, capacity)
    order = spot * peers + (owner[0] - me + mine) % peers
    order = jnp.broadcast_to(order.reshape(rows, 1).astype(f32), (rows, LANES))
    where = jnp.stack([segment, segment * heads]).astype(jnp.int32)

    def exchange(value):
        return lax.all_to_all(value, "seq", split_axis=0, concat_axis=0, tiled=True)

    arrived = exchange(pack(projected, decay_log, starts, heads, segments))
    normal, turned = grad_normed_of(upstream, order, out_weight, heads)
    meta = arrived[:, 3 * per_seg :, :]
    if per != 16:
        arrived = arrived[:, : 3 * per_seg, :].reshape(peers, 3, chunks, per, LANES)
        arrived = arrived.transpose(1, 2, 0, 3, 4).reshape(3, chunks, 16, 16, LANES)
        arrived = arrived.transpose(2, 0, 1, 3, 4).reshape(16, 3 * chunks * 16, LANES)

    def shape(*dims, dtype=f32):
        return jax.ShapeDtypeStruct(dims, dtype)

    tall = (chunks, CHUNK, LANES)
    square = (chunks, CHUNK, CHUNK)
    small = (chunks, 8, LANES)
    states = (chunks, LANES, LANES)
    mix, weights, enter, leave, inner, before, state, last, gains = call(
        functools.partial(forward_kernel, chunks, per_seg),
        (
            shape(*square), shape(*square, dtype=bf16), shape(*tall), shape(*tall), shape(*tall),
            shape(chunks + 1, 8, LANES), shape(*states), shape(LANES, LANES), shape(*small),
        ),
        (where, arrived, meta, column, line),
        flops=2 * chunks * CHUNK * LANES * 1024,
        moved=2 * arrived.size + 8 * chunks * CHUNK * CHUNK,
        in_specs=[SMEM] + [VMEM] * 4,
        out_specs=[VMEM] * 9,
    )
    came = carried(last, before[chunks], segments, heads, 1)
    normal = lax.all_to_all(
        normal, "seq", split_axis=0, concat_axis=0, tiled=True, axis_index_groups=groups
    )
    runs = peers if per == 16 else 1
    if per != 16:
        normal = normal.reshape(chunks, CHUNK // rows, peers, capacity, LANES)
        normal = normal.swapaxes(1, 2).reshape(heads, rows, LANES)
    normed, grad_query, grad_key, grad_value, back, after, last = call(
        functools.partial(middle_kernel, chunks, runs),
        (
            shape(heads, rows, LANES, dtype=bf16), shape(16, chunks * 16, LANES, dtype=bf16),
            shape(*tall), shape(*tall), shape(*states), shape(*small), shape(LANES, LANES),
        ),
        (arrived, mix, weights, enter, inner, before, state, gains, came, normal),
        flops=2 * chunks * CHUNK * LANES * 2048,
        moved=2 * arrived.size + 8 * chunks * CHUNK * CHUNK,
        in_specs=[VMEM] * 10,
        out_specs=[VMEM] * 7,
    )
    came = carried(last, before[chunks], segments, heads, -1)
    if per != 16:
        normed = normed.reshape(chunks, peers, CHUNK // rows, capacity, LANES)
        normed = normed.swapaxes(1, 2).reshape(heads, rows, LANES)
    normed = lax.all_to_all(
        normed, "seq", split_axis=0, concat_axis=0, tiled=True, axis_index_groups=groups
    )
    grads = call(
        functools.partial(backward_kernel, chunks),
        shape(16, 3 * chunks * 16, LANES, dtype=bf16),
        (arrived, leave, grad_query, grad_key, grad_value, back, after, came),
        flops=2 * chunks * CHUNK * LANES * 512,
        moved=4 * arrived.size,
        in_specs=[VMEM] * 8,
        out_specs=VMEM,
    )
    if per != 16:
        grads = grads.reshape(16, 3, chunks, 16, LANES).transpose(1, 2, 0, 3, 4)
        grads = grads.reshape(3, chunks, peers, per, LANES).transpose(2, 0, 1, 3, 4)
        grads = grads.reshape(peers, 3 * per_seg, LANES)
    grad_projected = unpack(exchange(grads), rows, heads, segments)
    grad_weight = grad_weight_of(normed, turned)
    return (grad_projected, grad_weight)


def solution(mesh):
    placed = (
        P(("groups", "seq"), None),
        P(("groups", "seq"), None),
        P(("groups", "seq")),
        P(("groups", "seq")),
        P(("groups", "seq")),
        P(("groups", "seq"), None),
        P(),
    )
    return jax.shard_map(
        shards,
        mesh=mesh,
        in_specs=placed,
        out_specs=(P(("groups", "seq"), None), P(("groups", "seq"), None)),
        check_vma=False,
    )
```

time: 288 us -> 106 us (0.37)
  waiting for transfers between devices: 137 us -> 34.8 us
  other arithmetic: 41.3 us -> 0.18 us
  blocking collectives: 29.7 us -> 0 us
  Pallas kernels: 0 us -> 20.6 us
  between operations: 14.9 us -> 0.79 us
  matrix products: 14 us -> 0 us
  starting transfers between devices: 21.8 us -> 26.5 us
  local copies, waits for them, and re-layouts: 25.8 us -> 21.6 us
    all_gather x2 -> x0, waiting for transfers between devices: 109 us -> none  [prefix(): pieces = jax.tree.map(lambda part: lax.all_gather(part, axis), value)]
    select_n x35 -> x0, other arithmetic: 38 us -> none  [the longest x30 35.2 us: hop(): jnp.where(position < mine, new, old)]
    unnamed x1 -> x0, blocking collectives: 29.7 us -> none
    pallas_call x0 -> x7, Pallas kernels: none -> 20.6 us  [call(): pl.pallas_call(body, out_shape=outs, compiler_params=PARAMS, cost_estimat...]
    unnamed x9 -> x45, local copies, waits for them, and re-layouts: 1.41 us -> 19.9 us
    dot_general x13 -> x0, matrix products: 10.5 us -> none  [the longest x1 3.25 us: shards(): lax.dot_general(normed_low, upstream, (((0,), (0,)), ((), ())), preferred...]
    scatter x4 -> x0, local copies, waits for them, and re-layouts: 8.91 us -> none  [spread(): jnp.zeros((peers * capacity, payload.shape[1]), payload.dtype).at[slots]]
    ppermute x0 -> x2, waiting for transfers between devices: none -> 8.08 us  [shift(): return lax.ppermute(value, 'seq', pairs)]
  transfers between devices with their start and end apart: 6 -> 6, of which waited for: 4 -> 5; matrix products, arithmetic and copies ran while one was open for 7% -> 2% of each run, Pallas kernels for 0% -> 14%
where the time goes in v1:
time: 106 us; the launch traced here: 104 us
  waiting for transfers between devices  34.8 us (33%)
  starting transfers between devices  26.5 us (25%)
  local copies, waits for them, and re-layouts  21.6 us (20%)
  Pallas kernels  20.6 us (19%)
    all_to_all x2, waiting for transfers between devices, exchange(): return lax.all_to_all(value, 'seq', split_axis=0, concat_axis=0, tiled=True)  26.3 us
    pallas_call x7, Pallas kernels, call(): pl.pallas_call(body, out_shape=outs, compiler_params=PARAMS, cost_estimat...  20.6 us
    unnamed x45, local copies, waits for them, and re-layouts  19.9 us
    all_to_all x2, starting transfers between devices, exchange(): return lax.all_to_all(value, 'seq', split_axis=0, concat_axis=0, tiled=True)  15 us
    ppermute x2, waiting for transfers between devices, shift(): return lax.ppermute(value, 'seq', pairs)  8.08 us
    all_to_all x1, starting transfers between devices, shards(): lax.all_to_all(normed, 'seq', split_axis=0, concat_axis=0, tiled=True, ax...  5.15 us
    all_to_all x1, starting transfers between devices, shards(): lax.all_to_all(normal, 'seq', split_axis=0, concat_axis=0, tiled=True, ax...  3.49 us
    ppermute x2, starting transfers between devices, shift(): return lax.ppermute(value, 'seq', pairs)  2.83 us
  transfers between devices with their start and end apart: 6, of which 5 were waited for; matrix products, arithmetic and copies ran while one was open for 2% of the time, Pallas kernels for 14%

profile of v1, /device:TPU:18, one launch (start us, length us, event | category | flops | bytes accessed | tf_op | source)
XLA Modules:
  0.0 104.5 jit_solution(16377010645820167470)
XLA Ops:
  0.6 0.8 copy.9.decay_ref
  1.4 1.1 %copy-done.2 = bf16[128,3072]{1,0:T(8,128)(2,1)S(1)} copy-done((bf16[128,3072]{1,0:T(8,128)(2,1)S(1)}, bf16[128,3072]{1,0:T(8,128)(2,1)}, u32[]{:S(2)}) %copy-start.2) | copy-done | bytes 786456
  3.2 1.1 %shard_map.77 = bf16[16,200,128]{2,1,0:T(8,128)(2,1)} custom-call(bf16[128,3072]{1,0:T(8,128)(2,1)S(1)} %copy-done.2, bf16[128,8]{1,0:T(8,128)(2,1)S(1)} %copy.9.decay_ref, s32[1,128]{1,0:T(1,128)S(1)} %bitcast.3), custom_call_target="tpu_custom_call" | custom-call | bytes 1572864 | tf_op jit(solution)/shard_map/pallas_call | solution.py:48
  4.3 6.3 %all-to-all-start = ((bf16[16,200,128]{2,1,0:T(8,128)(2,1)}), bf16[16,200,128]{2,1,0:T(8,128)(2,1)S(1)}, u32[]{:S(2)}, u32[]{:S(2)}) async-start(bf16[16,200,128]{2,1,0:T(8,128)(2,1)} %shard_map.77), calls=%async_computation | async-start | bytes 1638400 | tf_op jit(solution)/shard_map/all_to_all | solution.py:370
  10.7 0.7 dynamic_slice.7
  11.7 2.2 %copy-done = bf16[1024,2048]{1,0:T(8,128)(2,1)S(1)} copy-done((bf16[1024,2048]{1,0:T(8,128)(2,1)S(1)}, bf16[1024,2048]{1,0:T(8,128)(2,1)}, u32[]{:S(2)}) %copy-start) | copy-done | bytes 4194328
  13.9 1.0 copy-done.3
  14.9 4.3 %shard_map.79 = (f32[8,128,128]{2,1,0:T(8,128)}, bf16[128,2048]{1,0:T(8,128)(2,1)S(1)}) custom-call(bf16[128,2048]{1,0:T(8,128)(2,1)S(1)} %copy-done.3, f32[128,128]{1,0:T(8,128)S(1)} %broadcast_in_dim.8.order_ref, bf16[1024,2048]{1,0:T(8,128)(2,1)S(1)} %copy-done), custom_call_target="tpu_custom_call" | custom-call | flops 536870912 | bytes 5242880 | tf_op jit(solution)/shard_map/pallas_call | solution.py:48
  19.3 11.6 %all-to-all-done.rows_ref = bf16[16,200,128]{2,1,0:T(8,128)(2,1)S(1)} async-done(((bf16[16,200,128]{2,1,0:T(8,128)(2,1)}), bf16[16,200,128]{2,1,0:T(8,128)(2,1)S(1)}, u32[]{:S(2)}, u32[]{:S(2)}) %all-to-all-start) | async-done | bytes 819232 | tf_op jit(solution)/shard_map/all_to_all | solution.py:370
  30.9 3.5 %all-to-all-start.1 = ((f32[8,128,128]{2,1,0:T(8,128)}), f32[8,128,128]{2,1,0:T(8,128)S(1)}, u32[]{:S(2)}, u32[]{:S(2)}) async-start(f32[8,128,128]{2,1,0:T(8,128)} %get-tuple-element.29), calls=%async_computation.1 | async-start | bytes 1048576 | tf_op jit(solution)/shard_map/all_to_all | solution.py:400
  35.2 3.7 %shard_map.78 = (f32[4,256,256]{2,1,0:T(8,128)S(1)}, bf16[4,256,256]{2,1,0:T(8,128)(2,1)S(1)}, f32[4,256,128]{2,1,0:T(8,128)S(1)}, f32[4,256,128]{2,1,0:T(8,128)...) custom-call(s32[2]{0:T(128)S(1)} %pad_add_fusion.where_ref, ...), custom_call_target="tpu_custom_call" | custom-call | flops 268435456 | bytes 2916352 | tf_op jit(solution)/shard_map/pallas_call | solution.py:48
  38.9 1.0 copy-done.1
  39.9 0.8 copy-done.4
  41.4 1.3 %collective-permute-start = (f32[128,128]{1,0:T(8,128)}, f32[128,128]{1,0:T(8,128)S(1)}, u32[]{:S(2)}, u32[]{:S(2)}) collective-permute-start(f32[128,128]{1,0:T(8,128)} %get-tuple-element.28), channel_id=1, source_target_pairs={{0,8},{1,9},{2,10},{3,11},{4,12},{5,13},{6,14},{7,15},{16,24},{17,... | collective-permute-start | bytes 196616 | tf_op jit(solution)/shard_map/ppermute | solution.py:331
  43.1 5.8 %collective-permute-done.came_ref = f32[128,128]{1,0:T(8,128)S(1)} collective-permute-done((f32[128,128]{1,0:T(8,128)}, f32[128,128]{1,0:T(8,128)S(1)}, u32[]{:S(2)}, u32[]{:S(2)}) %collective-permute-start) | collective-permute-done | bytes 65568 | tf_op jit(solution)/shard_map/ppermute | solution.py:331
  48.9 0.9 copy-done.11
  49.8 4.2 %shard_map.80 = (bf16[8,128,128]{2,1,0:T(8,128)(2,1)S(1)}, bf16[16,64,128]{2,1,0:T(8,128)(2,1)S(1)}, f32[4,256,128]{2,1,0:T(8,128)S(1)}, f32[4,256,128]{2,1,0:T(...) custom-call(bf16[16,200,128]{2,1,0:T(8,128)(2,1)S(1)} %all-to-all-done.rows_ref, ...), custom_call_target="tpu_custom_call" | custom-call | flops 536870912 | bytes 2916352 | tf_op jit(solution)/shard_map/pallas_call | solution.py:48
  54.1 0.8 copy-done.6
  54.9 0.8 copy-done.8
  59.0 5.1 %all-to-all-start.3 = ((bf16[8,128,128]{2,1,0:T(8,128)(2,1)}), bf16[8,128,128]{2,1,0:T(8,128)(2,1)S(1)}, u32[]{:S(2)}, u32[]{:S(2)}) async-start(bf16[8,128,128]{2,1,0:T(8,128)(2,1)} %copy-done.12), calls=%async_computation.3 | async-start | bytes 524288 | tf_op jit(solution)/shard_map/all_to_all | solution.py:423
  64.1 1.5 %collective-permute-start.1 = (f32[128,128]{1,0:T(8,128)}, f32[128,128]{1,0:T(8,128)S(1)}, u32[]{:S(2)}, u32[]{:S(2)}) collective-permute-start(f32[128,128]{1,0:T(8,128)} %copy-done.20), channel_id=1, source_target_pairs={{8,0},{9,1},{10,2},{11,3},{12,4},{13,5},{14,6},{15,7},{24,16},{25,... | collective-permute-start | bytes 196616 | tf_op jit(solution)/shard_map/ppermute | solution.py:331
  65.7 2.3 %collective-permute-done.1.came_ref = f32[128,128]{1,0:T(8,128)S(1)} collective-permute-done((f32[128,128]{1,0:T(8,128)}, f32[128,128]{1,0:T(8,128)S(1)}, u32[]{:S(2)}, u32[]{:S(2)}) %collective-permute-start.1) | collective-permute-done | bytes 65568 | tf_op jit(solution)/shard_map/ppermute | solution.py:331
  68.0 1.0 copy-done.5
  69.1 1.0 copy-done.7
  70.1 1.0 copy-done.9
  71.1 0.9 copy-done.14
  72.1 0.9 copy-done.16
  73.8 1.3 %shard_map.81 = bf16[16,192,128]{2,1,0:T(8,128)(2,1)} custom-call(bf16[16,200,128]{2,1,0:T(8,128)(2,1)S(1)} %all-to-all-done.rows_ref, f32[4,256,128]{2,1,0:T(8,128)S(1)} %copy-done.5, bf16[16,64,128]{2,1,0:T(8,128)(2,1)S(1)} %copy-done.14, f32[4,256,128]{2,1,0:T(8,128)S(1)} %copy-done.7, f32[4,256,128]{2,1,0:T(8,128)S(1)} %copy-done.9, ...), custom_call_target="tpu_custom_call" | custom-call | flops 134217728 | bytes 1638400 | tf_op jit(solution)/shard_map/pallas_call | solution.py:48
  75.1 8.7 %all-to-all-start.2 = ((bf16[16,192,128]{2,1,0:T(8,128)(2,1)}), bf16[16,192,128]{2,1,0:T(8,128)(2,1)S(1)}, u32[]{:S(2)}, u32[]{:S(2)}) async-start(bf16[16,192,128]{2,1,0:T(8,128)(2,1)} %shard_map.81), calls=%async_computation.2 | async-start | bytes 1572864 | tf_op jit(solution)/shard_map/all_to_all | solution.py:370
  83.8 4.8 %shard_map.83 = bf16[1024,2048]{1,0:T(8,128)(2,1)} custom-call(bf16[8,128,128]{2,1,0:T(8,128)(2,1)S(1)} %all-to-all-done.3.normed_ref, bf16[128,2048]{1,0:T(8,128)(2,1)S(1)} %get-tuple-element.37.up_ref), custom_call_target="tpu_custom_call" | custom-call | flops 536870912 | bytes 4980736 | tf_op jit(solution)/shard_map/pallas_call | solution.py:48
  88.6 14.7 %all-to-all-done.2.in_ref = bf16[16,192,128]{2,1,0:T(8,128)(2,1)S(1)} async-done(((bf16[16,192,128]{2,1,0:T(8,128)(2,1)}), bf16[16,192,128]{2,1,0:T(8,128)(2,1)S(1)}, u32[]{:S(2)}, u32[]{:S(2)}) %all-to-all-start.2) | async-done | bytes 786464 | tf_op jit(solution)/shard_map/all_to_all | solution.py:370
  103.4 1.1 %shard_map.82 = bf16[128,3072]{1,0:T(8,128)(2,1)} custom-call(bf16[16,192,128]{2,1,0:T(8,128)(2,1)S(1)} %all-to-all-done.2.in_ref), custom_call_target="tpu_custom_call" | custom-call | bytes 1572864 | tf_op jit(solution)/shard_map/pallas_call | solution.py:48
  (55 shorter events, 7.0 us)
Async XLA Ops:
  1.4 1.1 %copy-start.2 = (bf16[128,3072]{1,0:T(8,128)(2,1)S(1)}, bf16[128,3072]{1,0:T(8,128)(2,1)}, u32[]{:S(2)}) copy-start(bf16[128,3072]{1,0:T(8,128)(2,1)} %rows_ref.1) | copy-start | bytes 2359300
  2.6 0.7 copy-start.19
  4.3 30.1 %copy-start.21 = (s32[128]{0:T(128)S(1)}, s32[128]{0:T(128)}, u32[]{:S(2)}) copy-start(s32[128]{0:T(128)} %param.9) | copy-start | bytes 1540
  4.3 26.6 %all-to-all-start = ((bf16[16,200,128]{2,1,0:T(8,128)(2,1)}), bf16[16,200,128]{2,1,0:T(8,128)(2,1)S(1)}, u32[]{:S(2)}, u32[]{:S(2)}) async-start(bf16[16,200,128]{2,1,0:T(8,128)(2,1)} %shard_map.77), calls=%async_computation | async-start | bytes 1638400 | tf_op jit(solution)/shard_map/all_to_all | solution.py:370
  11.7 2.2 %copy-start = (bf16[1024,2048]{1,0:T(8,128)(2,1)S(1)}, bf16[1024,2048]{1,0:T(8,128)(2,1)}, u32[]{:S(2)}) copy-start(bf16[1024,2048]{1,0:T(8,128)(2,1)} %weight_ref.1) | copy-start | bytes 12582916
  13.9 1.0 copy-start.3
  30.9 12.3 %all-to-all-start.1 = ((f32[8,128,128]{2,1,0:T(8,128)}), f32[8,128,128]{2,1,0:T(8,128)S(1)}, u32[]{:S(2)}, u32[]{:S(2)}) async-start(f32[8,128,128]{2,1,0:T(8,128)} %get-tuple-element.29), calls=%async_computation.1 | async-start | bytes 1048576 | tf_op jit(solution)/shard_map/all_to_all | solution.py:400
  38.9 1.0 copy-start.1
  39.9 0.8 copy-start.4
  40.7 0.7 copy-start.10
  41.4 7.5 %collective-permute-start = (f32[128,128]{1,0:T(8,128)}, f32[128,128]{1,0:T(8,128)S(1)}, u32[]{:S(2)}, u32[]{:S(2)}) collective-permute-start(f32[128,128]{1,0:T(8,128)} %get-tuple-element.28), channel_id=1, source_target_pairs={{0,8},{1,9},{2,10},{3,11},{4,12},{5,13},{6,14},{7,15},{16,24},{17,... | collective-permute-start | bytes 196616 | tf_op jit(solution)/shard_map/ppermute | solution.py:331
  48.9 1.0 copy-start.11
  54.1 0.8 copy-start.6
  54.9 0.8 copy-start.8
  55.6 0.7 copy-start.12
  56.4 0.7 copy-start.13
  57.1 0.7 copy-start.15
  57.8 0.6 copy-start.17
  58.4 0.6 copy-start.20
  59.0 16.1 %all-to-all-start.3 = ((bf16[8,128,128]{2,1,0:T(8,128)(2,1)}), bf16[8,128,128]{2,1,0:T(8,128)(2,1)S(1)}, u32[]{:S(2)}, u32[]{:S(2)}) async-start(bf16[8,128,128]{2,1,0:T(8,128)(2,1)} %copy-done.12), calls=%async_computation.3 | async-start | bytes 524288 | tf_op jit(solution)/shard_map/all_to_all | solution.py:423
  64.1 3.9 %collective-permute-start.1 = (f32[128,128]{1,0:T(8,128)}, f32[128,128]{1,0:T(8,128)S(1)}, u32[]{:S(2)}, u32[]{:S(2)}) collective-permute-start(f32[128,128]{1,0:T(8,128)} %copy-done.20), channel_id=1, source_target_pairs={{8,0},{9,1},{10,2},{11,3},{12,4},{13,5},{14,6},{15,7},{24,16},{25,... | collective-permute-start | bytes 196616 | tf_op jit(solution)/shard_map/ppermute | solution.py:331
  68.0 1.0 copy-start.5
  69.1 1.0 copy-start.7
  70.1 1.0 copy-start.9
  71.1 0.9 copy-start.14
  72.1 0.9 copy-start.16
  73.0 0.7 copy-start.18
  75.1 28.3 %all-to-all-start.2 = ((bf16[16,192,128]{2,1,0:T(8,128)(2,1)}), bf16[16,192,128]{2,1,0:T(8,128)(2,1)S(1)}, u32[]{:S(2)}, u32[]{:S(2)}) async-start(bf16[16,192,128]{2,1,0:T(8,128)(2,1)} %shard_map.81), calls=%async_computation.2 | async-start | bytes 1572864 | tf_op jit(solution)/shard_map/all_to_all | solution.py:370

commit v2 on v1

v2 whole, which is shorter than its diff:
```python
import functools

import jax
import jax.numpy as jnp
from jax import lax
from jax.experimental import pallas as pl
from jax.experimental.pallas import tpu as pltpu
from jax.sharding import PartitionSpec as P

norm_eps = 1e-06
LANES = 128
CHUNK = 256
META = 8
bf16 = jnp.bfloat16
f32 = jnp.float32

VMEM = pl.BlockSpec(memory_space=pltpu.VMEM)
SMEM = pl.BlockSpec(memory_space=pltpu.SMEM)
PARAMS = pltpu.CompilerParams(vmem_limit_bytes=24 * 1024 * 1024)
ANY = pl.BlockSpec(memory_space=pl.ANY)


def dot(a, b):
    return lax.dot_general(a, b, (((1,), (0,)), ((), ())), preferred_element_type=f32)


def dot_nt(a, b):
    return lax.dot_general(a, b, (((1,), (1,)), ((), ())), preferred_element_type=f32)


def dot_tn(a, b):
    return lax.dot_general(a, b, (((0,), (0,)), ((), ())), preferred_element_type=f32)


def halves(value):
    high = value.astype(bf16)
    return high, (value - high.astype(f32)).astype(bf16)


def wide(value):
    return jnp.concatenate([value] * (CHUNK // LANES), axis=1)


def iota(shape, dim):
    return lax.broadcasted_iota(jnp.int32, shape, dim)


def call(body, outs, ins, flops=0, moved=0, **more):
    return pl.pallas_call(
        body,
        out_shape=outs,
        compiler_params=PARAMS,
        cost_estimate=pl.CostEstimate(flops=flops, bytes_accessed=moved, transcendentals=0),
        **more,
    )(*ins)


def pack_kernel(heads, segments, rows_ref, decay_ref, starts_ref, out_ref):
    per = rows_ref.shape[0] // segments
    inner = heads * LANES
    decay_rows = decay_ref[...].astype(f32)
    flags = starts_ref[...].astype(f32)
    line = iota((META, LANES), 0)
    for head in range(heads):
        meta = jnp.where(line == 0, decay_rows[head : head + 1, :], jnp.where(line == 1, flags, 0.0))
        for segment in range(segments):
            to = segment * heads + head
            for part in range(3):
                at = part * inner + head * LANES
                out_ref[to, part * per : (part + 1) * per, :] = rows_ref[
                    segment * per : (segment + 1) * per, at : at + LANES
                ]
            out_ref[to, 3 * per :, :] = meta.astype(bf16)


def pack(projected, decay_log, starts, heads, segments):
    rows = projected.shape[0]
    per = rows // segments
    peers = heads * segments
    if per % 16 == 0:
        return call(
            functools.partial(pack_kernel, heads, segments),
            jax.ShapeDtypeStruct((peers, 3 * per + META, LANES), bf16),
            (projected, decay_log.T, starts.reshape(1, rows)),
            moved=4 * projected.size,
            in_specs=[VMEM] * 3,
            out_specs=VMEM,
        )
    body = projected.reshape(segments, per, 3, heads, LANES).transpose(0, 3, 2, 1, 4)
    body = body.reshape(peers, 3 * per, LANES)
    flags = jnp.broadcast_to(starts.astype(bf16)[None, None, :], (heads, 1, rows))
    meta = jnp.concatenate(
        [decay_log.T[:, None, :], flags, jnp.zeros((heads, META - 2, rows), bf16)], axis=1
    )
    meta = jnp.broadcast_to(meta[None], (segments, heads, META, LANES)).reshape(peers, META, LANES)
    return jnp.concatenate([body, meta], axis=1)


def unpack_kernel(heads, segments, in_ref, out_ref):
    per = out_ref.shape[0] // segments
    inner = heads * LANES
    for segment in range(segments):
        for head in range(heads):
            for part in range(3):
                at = part * inner + head * LANES
                out_ref[segment * per : (segment + 1) * per, at : at + LANES] = in_ref[
                    segment * heads + head, part * per : (part + 1) * per, :
                ]


def unpack(arrived, rows, heads, segments):
    per = rows // segments
    if per % 16 == 0:
        return call(
            functools.partial(unpack_kernel, heads, segments),
            jax.ShapeDtypeStruct((rows, 3 * heads * LANES), bf16),
            (arrived,),
            moved=4 * arrived.size,
            in_specs=[VMEM],
            out_specs=VMEM,
        )
    body = arrived.reshape(segments, heads, 3, per, LANES).transpose(0, 3, 2, 1, 4)
    return body.reshape(rows, 3 * heads * LANES)


def turns_of(destination_ref, peers):
    turn = jnp.bitwise_and(destination_ref[...], peers - 1).astype(f32)
    return jnp.broadcast_to(turn, (LANES, LANES)).astype(bf16)


def wrapped(value, peers):
    return jnp.where(value < 0.0, value + peers, jnp.where(value >= peers, value - peers, value))


def places(turns, peers, first, count, rows):
    me = lax.axis_index("seq").astype(f32)
    down = iota((rows, LANES), 0)
    chosen = iota((rows, LANES), 1) == first + down % count
    pick = jnp.where(chosen, 1.0, 0.0).astype(bf16)
    turn = dot_nt(pick, turns) + (down // count).astype(f32) - me
    column = (down % count * peers).astype(f32) + wrapped(turn, peers)
    along = iota((8, rows), 1)
    turn = dot_nt(turns[0:8, :], pick) + (along // count).astype(f32) - me
    line = (along % count * peers).astype(f32) + wrapped(turn, peers)
    return chosen, column, line


def grad_normed_kernel(heads, peers, up_ref, destination_ref, weight_ref, even_ref, odd_ref, turned_ref):
    rows = up_ref.shape[0]
    me = lax.axis_index("seq")
    capacity = rows // peers
    turns = turns_of(destination_ref, peers)
    _, column, _ = places(turns, peers, me * capacity, capacity, rows)
    pick = iota((rows, rows), 1).astype(f32) == column
    turned = dot(jnp.where(pick, 1.0, 0.0).astype(bf16), up_ref[...]).astype(bf16)
    turned_ref[...] = turned
    for step in range(heads):
        head = jnp.bitwise_xor(lax.rem(me, heads), step)
        at = pl.multiple_of(head * LANES, LANES)
        out_ref = odd_ref if step % 2 else even_ref
        out_ref[step // 2] = dot_nt(turned, weight_ref[pl.ds(at, LANES), :])


def grad_normed_of(upstream, destination, out_weight, heads, peers):
    rows, width = upstream.shape
    return call(
        functools.partial(grad_normed_kernel, heads, peers),
        (
            jax.ShapeDtypeStruct((heads // 2, rows, LANES), f32),
            jax.ShapeDtypeStruct((heads // 2, rows, LANES), f32),
            jax.ShapeDtypeStruct((rows, width), bf16),
        ),
        (upstream, destination, out_weight),
        flops=2 * rows * out_weight.size,
        moved=2 * (2 * upstream.size + out_weight.size),
        in_specs=[VMEM] * 3,
        out_specs=[VMEM] * 3,
    )


def grad_weight_kernel(mine_ref, normed_ref, up_ref, out_ref):
    out_ref[...] = dot_tn(normed_ref[0], up_ref[...]).astype(bf16)


def grad_weight_of(normed, upstream, mine):
    heads, rows, _ = normed.shape
    width = upstream.shape[1]
    return call(
        grad_weight_kernel,
        jax.ShapeDtypeStruct((heads * LANES, width), bf16),
        (mine.reshape(1), normed, upstream),
        flops=2 * rows * heads * LANES * width,
        moved=2 * (upstream.size + normed.size + heads * LANES * width),
        grid_spec=pltpu.PrefetchScalarGridSpec(
            num_scalar_prefetch=1,
            grid=(heads,),
            in_specs=[
                pl.BlockSpec((1, rows, LANES), lambda i, mine: (i, 0, 0)),
                pl.BlockSpec((rows, width), lambda i, mine: (0, 0)),
            ],
            out_specs=pl.BlockSpec((LANES, width), lambda i, mine: (jnp.bitwise_xor(mine[0], i), 0)),
        ),
    )


def part_rows(ref, part, chunk):
    per = ref.shape[1] // 3
    if ref.shape[1] % 16:
        per = (ref.shape[1] - META) // 3
    at = part * per + chunk * 16
    return ref[:, at : at + 16, :].reshape(CHUNK, LANES)


class Terms:
    def __init__(self, heads, chunks, meta_ref, destination_ref):
        self.meta_ref = meta_ref
        self.peers = meta_ref.shape[0]
        self.per = CHUNK // self.peers
        self.first_row = lax.axis_index("seq") // heads * self.per * chunks
        self.first_block = lax.axis_index("seq") // heads * heads
        self.turns = turns_of(destination_ref, self.peers)
        lines = self.peers * META
        meta = meta_ref[:, -META:, :].astype(f32).reshape(lines, LANES).astype(bf16)
        row = iota((CHUNK, lines), 0)
        pick = jnp.where(iota((CHUNK, lines), 1) == row // self.per * META, 1.0, 0.0)
        self.decays = dot(pick.astype(bf16), meta)

    def of(self, chunk):
        group = CHUNK // LANES
        chosen, column, line = places(
            self.turns, self.peers, self.first_row + chunk * self.per, self.per, CHUNK
        )
        ones = jnp.ones((LANES, LANES), bf16)
        decay = dot(jnp.where(chosen, self.decays, 0.0).astype(bf16), ones).astype(bf16)
        column = wide(column)
        order = line[0:1, :] <= column
        running = dot(jnp.where(order, 1.0, 0.0).astype(bf16), decay)
        flags = [
            self.meta_ref[self.first_block + chunk * group + i, -META:, :].astype(f32)[1:2, :]
            for i in range(group)
        ]
        flags = jnp.broadcast_to(jnp.concatenate(flags, axis=1), (LANES, CHUNK)).astype(bf16)
        reached = iota((CHUNK, CHUNK), 1).astype(f32) <= column
        count = dot_nt(jnp.where(reached, 1.0, 0.0).astype(bf16), flags)
        last_run = jnp.min(running, axis=0, keepdims=True)
        last_count = jnp.max(count, axis=0, keepdims=True)
        leave = jnp.exp(jnp.minimum(last_run - running, 0.0))
        leave = jnp.where(count == last_count, leave, 0.0)
        total = jnp.where(last_count == 0.0, jnp.exp(last_run), 0.0)
        return order, running, count, leave, total


def state_kernel(heads, chunks, rows_ref, meta_ref, destination_ref, last_ref, keep_ref, gain_ref):
    terms = Terms(heads, chunks, meta_ref, destination_ref)
    state = jnp.zeros((LANES, LANES), f32)
    before = jnp.ones((1, LANES), f32)
    line = iota((8, LANES), 0)
    for chunk in range(chunks):
        _, _, _, leave, total = terms.of(chunk)
        key, value = (part_rows(rows_ref, part, chunk) for part in (1, 2))
        high, low = halves(key.astype(f32) * leave)
        keep_ref[chunk, 0:LANES, :] = state
        keep_ref[chunk, LANES:, :] = jnp.where(line == 0, before, total)
        state = total * state + dot_tn(high, value) + dot_tn(low, value)
        before = total * before
    last_ref[...] = state
    gain_ref[...] = jnp.broadcast_to(before, (8, LANES))


def inner_kernel(
    heads, chunks, rows_ref, meta_ref, destination_ref, mix_ref, weights_ref, inner_ref, ends_ref
):
    terms = Terms(heads, chunks, meta_ref, destination_ref)
    lane = iota((CHUNK, LANES), 1)
    for chunk in range(chunks):
        order, running, count, leave, _ = terms.of(chunk)
        turned = jnp.where(lane == 0, running, count).T
        same = order & (wide(count) == turned[1:2, :])
        gap = jnp.minimum(wide(running) - turned[0:1, :], 0.0)
        mix = jnp.where(same, jnp.exp(gap), 0.0)
        enter = jnp.where(count == 0.0, jnp.exp(running), 0.0)
        query, key, value = (part_rows(rows_ref, part, chunk) for part in range(3))
        weights = (dot_nt(query, key) * mix).astype(bf16)
        mix_ref[chunk] = mix
        weights_ref[chunk] = weights
        inner_ref[chunk] = dot(weights, value)
        ends_ref[chunk] = jnp.where(lane == 0, enter, leave)


def entering(keep_ref, chunk, came):
    keep = keep_ref[chunk]
    return halves(keep[0:LANES, :] + keep[LANES : LANES + 1, :] * came), keep[LANES + 1 : LANES + 2, :]


def output_kernel(
    heads, chunks, runs, rows_ref, inner_ref, ends_ref, keep_ref, came_ref, *refs
):
    given, (grad_ref, block_ref, back_ref, last_ref, normal_ref, sems) = refs[:-6], refs[-6:]
    mine = lax.rem(lax.axis_index("seq"), heads)
    sources = [given[0].at[0], given[1].at[0]]
    for pair in given[2:]:
        sources += [pair.at[0], pair.at[1]]
    copies = [
        pltpu.make_async_copy(
            source, normal_ref.at[jnp.bitwise_xor(mine, step)], sems.at[step]
        )
        for step, source in enumerate(sources)
    ]
    for copy in copies:
        copy.start()
    group = CHUNK // LANES
    back = jnp.zeros((LANES, LANES), f32)
    after = jnp.ones((1, LANES), f32)
    line = iota((8, LANES), 0)
    came = came_ref[...]
    normed_rows = []
    for chunk in range(chunks):
        query = part_rows(rows_ref, 0, chunk)
        enter = ends_ref[chunk][:, 0:1]
        (high, low), _ = entering(keep_ref, chunk, came)
        output = inner_ref[chunk] + enter * (dot(query, high) + dot(query, low))
        scale = lax.rsqrt(jnp.mean(output * output, axis=1, keepdims=True) + norm_eps)
        normed = output * scale
        split = normed.reshape(runs, group, CHUNK // (runs * group), LANES)
        for i in range(group):
            step = jnp.bitwise_xor(mine, chunk * group + i)
            at = jnp.bitwise_and(step, 1) * (heads // 2) + lax.div(step, 2)
            block_ref[at] = split[:, i].reshape(LANES, LANES).astype(bf16)
        normed_rows.append((normed, scale))
    for copy in copies:
        copy.wait()
    for chunk in reversed(range(chunks)):
        normed, scale = normed_rows[chunk]
        query = part_rows(rows_ref, 0, chunk)
        enter = ends_ref[chunk][:, 0:1]
        normal = jnp.concatenate(
            [
                normal_ref[chunk * group + i].reshape(runs, 1, CHUNK // (runs * group), LANES)
                for i in range(group)
            ],
            axis=1,
        ).reshape(CHUNK, LANES)
        grad = (
            (normal - normed * jnp.mean(normal * normed, axis=1, keepdims=True)) * scale
        ).astype(bf16)
        grad_ref[chunk] = grad
        gain = keep_ref[chunk, LANES + 1 : LANES + 2, :]
        back_ref[chunk, 0:LANES, :] = back
        back_ref[chunk, LANES:, :] = jnp.where(line == 0, after, gain)
        high, low = halves(query.astype(f32) * enter)
        back = gain * back + dot_tn(high, grad) + dot_tn(low, grad)
        after = gain * after
    last_ref[...] = back


def local_kernel(
    chunks, rows_ref, mix_ref, weights_ref, ends_ref, keep_ref, came_ref, grad_ref, query_ref, part_ref
):
    came = came_ref[...]
    for chunk in range(chunks):
        query, key, value = (part_rows(rows_ref, part, chunk) for part in range(3))
        grad = grad_ref[chunk]
        (high, low), _ = entering(keep_ref, chunk, came)
        grad_mix = (dot_nt(grad, value) * mix_ref[chunk]).astype(bf16)
        grad_query = dot_nt(grad, high) + dot_nt(grad, low)
        grad_query = dot(grad_mix, key) + ends_ref[chunk][:, 0:1] * grad_query
        query_ref[:, chunk * 16 : (chunk + 1) * 16, :] = (
            grad_query.astype(bf16).reshape(16, 16, LANES)
        )
        part_ref[0, chunk] = dot_tn(grad_mix, query)
        part_ref[1, chunk] = dot_tn(weights_ref[chunk], grad)


def final_kernel(chunks, rows_ref, ends_ref, query_ref, part_ref, back_ref, came_ref, out_ref):
    per = chunks * 16
    came = came_ref[...]
    out_ref[:, 0:per, :] = query_ref[...]
    for chunk in range(chunks):
        key, value = (part_rows(rows_ref, part, chunk) for part in (1, 2))
        leave = ends_ref[chunk][:, 1:2]
        (high, low), _ = entering(back_ref, chunk, came)
        grad_key = part_ref[0, chunk] + leave * (dot_nt(value, high) + dot_nt(value, low))
        grad_value = part_ref[1, chunk] + leave * (dot(key, high) + dot(key, low))
        for part, grad in ((1, grad_key), (2, grad_value)):
            at = part * per + chunk * 16
            out_ref[:, at : at + 16, :] = grad.astype(bf16).reshape(16, 16, LANES)


def carried(last, gain, segments, heads, step):
    def shift(value, by):
        pairs = [
            (s * heads + h, (s + by * step) * heads + h)
            for s in range(segments)
            for h in range(heads)
            if 0 <= s + by * step < segments
        ]
        return lax.ppermute(value, "seq", pairs)

    state = shift(last, 1)
    if segments > 2:
        gain = shift(gain, 1)
        by = 1
        while by < segments - 1:
            state, gain = state + gain[0:1, :] * shift(state, by), gain * shift(gain, by)
            by *= 2
    return state


def shards(projected, decay_log, destination, source, starts, upstream, out_weight):
    rows = projected.shape[0]
    heads = decay_log.shape[1]
    peers = lax.axis_size("seq")
    segments = peers // heads
    per_seg = rows // segments
    chunks = heads * rows // CHUNK
    per = CHUNK // peers
    me = lax.axis_index("seq")
    segment = me // heads
    groups = [[s * heads + h for h in range(heads)] for s in range(segments)]

    def exchange(value):
        return lax.all_to_all(value, "seq", split_axis=0, concat_axis=0, tiled=True)

    def among_heads(value):
        return lax.all_to_all(
            value, "seq", split_axis=0, concat_axis=0, tiled=True, axis_index_groups=groups
        )

    place = destination.reshape(1, rows)
    arrived = exchange(pack(projected, decay_log, starts, heads, segments))
    even, odd, turned = grad_normed_of(upstream, place, out_weight, heads, peers)
    mine = me % heads
    steps = [jnp.bitwise_xor(mine, step) for step in range(heads)]

    def swap(value, step):
        return lax.ppermute(value, "seq", [(i, i ^ step) for i in range(peers)])

    def deal(even, odd):
        other = swap(odd, 1)
        pairs = [
            swap(jnp.stack([even[step], other[step]]), 2 * step) for step in range(1, heads // 2)
        ]
        return [even[0:1], other[0:1], *pairs]

    if per == 16:
        runs = peers
        meta = arrived
        normal = deal(even, odd)
    else:
        runs = 1
        meta = arrived[:, 3 * per_seg :, :]
        arrived = arrived[:, : 3 * per_seg, :].reshape(peers, 3, chunks, per, LANES)
        arrived = arrived.transpose(1, 2, 0, 3, 4).reshape(3, chunks, 16, 16, LANES)
        arrived = arrived.transpose(2, 0, 1, 3, 4).reshape(16, 3 * chunks * 16, LANES)
        normal = jnp.stack([even, odd], axis=1).reshape(heads, rows, LANES)
        normal = among_heads(jnp.stack([normal[step] for step in steps]))
        normal = normal.reshape(chunks, CHUNK // rows, peers, rows // peers, LANES)
        normal = normal.swapaxes(1, 2).reshape(heads, rows, LANES)
        normal = jnp.stack([normal[step] for step in steps])
        normal = [normal[0:1], normal[1:2], *(normal[i : i + 2] for i in range(2, heads, 2))]

    def shape(*dims, dtype=f32):
        return jax.ShapeDtypeStruct(dims, dtype)

    tall = (chunks, CHUNK, LANES)
    square = (chunks, CHUNK, CHUNK)
    states = (chunks, LANES + 8, LANES)
    low = (16, chunks * 16, LANES)
    unit = 2 * chunks * CHUNK * LANES
    last, keep, gain = call(
        functools.partial(state_kernel, heads, chunks),
        (shape(LANES, LANES), shape(*states), shape(8, LANES)),
        (arrived, meta, place),
        flops=unit * 512,
        moved=2 * arrived.size,
        in_specs=[VMEM] * 3,
        out_specs=[VMEM] * 3,
    )
    came = carried(last, gain, segments, heads, 1)
    mix, weights, inner, ends = call(
        functools.partial(inner_kernel, heads, chunks),
        (shape(*square), shape(*square, dtype=bf16), shape(*tall), shape(*tall)),
        (arrived, meta, place),
        flops=unit * 1024,
        moved=2 * arrived.size + 8 * chunks * CHUNK * CHUNK,
        in_specs=[VMEM] * 3,
        out_specs=[VMEM] * 4,
    )
    grad, normed, back, last = call(
        functools.partial(output_kernel, heads, chunks, runs),
        (
            shape(*tall, dtype=bf16), shape(heads, rows, LANES, dtype=bf16), shape(*states),
            shape(LANES, LANES),
        ),
        (arrived, inner, ends, keep, came, *normal),
        flops=unit * 1024,
        moved=2 * arrived.size + 8 * chunks * CHUNK * LANES,
        in_specs=[VMEM] * 5 + [ANY] * len(normal),
        out_specs=[VMEM] * 4,
        scratch_shapes=[
            pltpu.VMEM((heads, rows, LANES), f32),
            pltpu.SemaphoreType.DMA((heads,)),
        ],
    )
    came_back = carried(last, gain, segments, heads, -1)
    grad_query, part = call(
        functools.partial(local_kernel, chunks),
        (shape(*low, dtype=bf16), shape(2, *tall)),
        (arrived, mix, weights, ends, keep, came, grad),
        flops=unit * 1024,
        moved=2 * arrived.size + 8 * chunks * CHUNK * CHUNK,
        in_specs=[VMEM] * 7,
        out_specs=[VMEM] * 2,
    )
    grads = call(
        functools.partial(final_kernel, chunks),
        shape(16, 3 * chunks * 16, LANES, dtype=bf16),
        (arrived, ends, grad_query, part, back, came_back),
        flops=unit * 512,
        moved=4 * arrived.size,
        in_specs=[VMEM] * 6,
        out_specs=VMEM,
    )
    normed, grads = lax.optimization_barrier((normed, grads))
    if per == 16:
        normed = jnp.concatenate(deal(normed[: heads // 2], normed[heads // 2 :]))
    else:
        normed = normed.reshape(2, heads // 2, rows, LANES).swapaxes(0, 1)
        normed = normed.reshape(heads, rows, LANES)
        normed = jnp.stack([normed[step] for step in steps])
        normed = normed.reshape(chunks, peers, CHUNK // rows, rows // peers, LANES)
        normed = among_heads(normed.swapaxes(1, 2).reshape(heads, rows, LANES))
        normed = jnp.stack([normed[step] for step in steps])
        grads = grads.reshape(16, 3, chunks, 16, LANES).transpose(1, 2, 0, 3, 4)
        grads = grads.reshape(3, chunks, peers, per, LANES).transpose(2, 0, 1, 3, 4)
        grads = grads.reshape(peers, 3 * per_seg, LANES)
    grad_projected = unpack(exchange(grads), rows, heads, segments)
    grad_weight = grad_weight_of(normed, turned, mine)
    return (grad_projected, grad_weight)


def solution(mesh):
    placed = (
        P(("groups", "seq"), None),
        P(("groups", "seq"), None),
        P(("groups", "seq")),
        P(("groups", "seq")),
        P(("groups", "seq")),
        P(("groups", "seq"), None),
        P(),
    )
    return jax.shard_map(
        shards,
        mesh=mesh,
        in_specs=placed,
        out_specs=(P(("groups", "seq"), None), P(("groups", "seq"), None)),
        check_vma=False,
    )
```

time: 106 us -> 79.8 us (0.75)
  local copies, waits for them, and re-layouts: 21.6 us -> 6.46 us
  waiting for transfers between devices: 34.8 us -> 29.9 us
  Pallas kernels: 20.6 us -> 18.1 us
  starting transfers between devices: 26.5 us -> 24.1 us
    all_to_all x2, waiting for transfers between devices: 26.3 us -> 9.98 us  [exchange(): return lax.all_to_all(value, 'seq', split_axis=0, concat_axis=0, tiled=True)]
    ppermute x0 -> x8, waiting for transfers between devices: none -> 15.8 us  [swap(): return lax.ppermute(value, 'seq', [(i, i ^ step) for i in range(peers)])]
    unnamed x45 -> x16, local copies, waits for them, and re-layouts: 19.9 us -> 6.37 us
    all_to_all x2 -> x0, starting transfers between devices: 8.64 us -> none  [the longest x1 5.15 us: shards(): lax.all_to_all(normed, 'seq', split_axis=0, concat_axis=0, tiled=True, ax...]
    ppermute x0 -> x8, starting transfers between devices: none -> 7.79 us  [swap(): return lax.ppermute(value, 'seq', [(i, i ^ step) for i in range(peers)])]
    ppermute x2, waiting for transfers between devices: 8.08 us -> 4.09 us  [shift(): return lax.ppermute(value, 'seq', pairs)]
    pallas_call x7 -> x9, Pallas kernels: 20.6 us -> 18.1 us  [call(): pl.pallas_call(body, out_shape=outs, compiler_params=PARAMS, cost_estimat...]
    all_to_all x2, starting transfers between devices: 15 us -> 13 us  [exchange(): return lax.all_to_all(value, 'seq', split_axis=0, concat_axis=0, tiled=True)]
  transfers between devices with their start and end apart: 6 -> 12, of which waited for: 5 -> 7; matrix products, arithmetic and copies ran while one was open for 2% -> 0% of each run, Pallas kernels for 14% -> 16%
where the time goes in v2:
time: 79.8 us; the launch traced here: 79.3 us
  waiting for transfers between devices  29.9 us (37%)
  starting transfers between devices  24.1 us (30%)
  Pallas kernels  18.1 us (23%)
  local copies, waits for them, and re-layouts  6.46 us (8%)
    pallas_call x9, Pallas kernels, call(): pl.pallas_call(body, out_shape=outs, compiler_params=PARAMS, cost_estimat...  18.1 us
    ppermute x8, waiting for transfers between devices, swap(): return lax.ppermute(value, 'seq', [(i, i ^ step) for i in range(peers)])  15.8 us
    all_to_all x2, starting transfers between devices, exchange(): return lax.all_to_all(value, 'seq', split_axis=0, concat_axis=0, tiled=True)  13 us
    all_to_all x2, waiting for transfers between devices, exchange(): return lax.all_to_all(value, 'seq', split_axis=0, concat_axis=0, tiled=True)  9.98 us
    ppermute x8, starting transfers between devices, swap(): return lax.ppermute(value, 'seq', [(i, i ^ step) for i in range(peers)])  7.79 us
    unnamed x16, local copies, waits for them, and re-layouts  6.37 us
    ppermute x2, waiting for transfers between devices, shift(): return lax.ppermute(value, 'seq', pairs)  4.09 us
    ppermute x2, starting transfers between devices, shift(): return lax.ppermute(value, 'seq', pairs)  3.23 us
  transfers between devices with their start and end apart: 12, of which 7 were waited for; matrix products, arithmetic and copies ran while one was open for 0% of the time, Pallas kernels for 16%

profile of v2, /device:TPU:18, one launch (start us, length us, event | category | flops | bytes accessed | tf_op | source)
XLA Modules:
  0.0 79.3 jit_solution(16765699363061789907)
XLA Ops:
  0.6 1.1 %copy-done.1 = bf16[128,3072]{1,0:T(8,128)(2,1)S(1)} copy-done((bf16[128,3072]{1,0:T(8,128)(2,1)S(1)}, bf16[128,3072]{1,0:T(8,128)(2,1)}, u32[]{:S(2)}) %copy-start.1) | copy-done | bytes 786456
  1.8 0.7 copy-done.5
  2.4 0.7 copy-done.6
  3.1 1.0 %shard_map.77 = bf16[16,200,128]{2,1,0:T(8,128)(2,1)} custom-call(bf16[128,3072]{1,0:T(8,128)(2,1)S(1)} %copy-done.1, bf16[8,128]{1,0:T(8,128)(2,1)S(1)} %bitcast.7, s32[1,128]{1,0:T(1,128)S(1)} %bitcast.8), custom_call_target="tpu_custom_call" | custom-call | bytes 1572864 | tf_op jit(solution)/shard_map/pallas_call | solution.py:49
  4.1 6.3 %all-to-all-start = ((bf16[16,200,128]{2,1,0:T(8,128)(2,1)}), bf16[16,200,128]{2,1,0:T(8,128)(2,1)S(1)}, u32[]{:S(2)}, u32[]{:S(2)}) async-start(bf16[16,200,128]{2,1,0:T(8,128)(2,1)} %shard_map.77), calls=%async_computation | async-start | bytes 1638400 | tf_op jit(solution)/shard_map/all_to_all | solution.py:422
  10.5 2.2 %copy-done = bf16[1024,2048]{1,0:T(8,128)(2,1)S(1)} copy-done((bf16[1024,2048]{1,0:T(8,128)(2,1)S(1)}, bf16[1024,2048]{1,0:T(8,128)(2,1)}, u32[]{:S(2)}) %copy-start) | copy-done | bytes 4194328
  12.6 1.0 %copy-done.2 = bf16[128,2048]{1,0:T(8,128)(2,1)S(1)} copy-done((bf16[128,2048]{1,0:T(8,128)(2,1)S(1)}, bf16[128,2048]{1,0:T(8,128)(2,1)}, u32[]{:S(2)}) %copy-start.2) | copy-done | bytes 524312
  13.7 0.7 copy-done.3
  14.3 1.5 %shard_map.80 = (f32[4,128,128]{2,1,0:T(8,128)S(1)}, f32[4,128,128]{2,1,0:T(8,128)S(1)}, bf16[128,2048]{1,0:T(8,128)(2,1)S(1)}) custom-call(bf16[128,2048]{1,0:T(8,128)(2,1)S(1)} %copy-done.2, s32[1,128]{1,0:T(1,128)S(1)} %bitcast.4, bf16[1024,2048]{1,0:T(8,128)(2,1)S(1)} %copy-done), custom_call_target="tpu_custom_call" | custom-call | flops 536870912 | bytes 5242880 | tf_op jit(solution)/shard_map/pallas_call | solution.py:49
  16.1 1.4 %collective-permute-done.1 = f32[4,128,128]{2,1,0:T(8,128)S(1)} collective-permute-done((f32[4,128,128]{2,1,0:T(8,128)S(1)}, f32[4,128,128]{2,1,0:T(8,128)S(1)}, u32[]{:S(2)}, u32[]{:S(2)}) %collective-permute-start.1) | collective-permute-done | bytes 262176 | tf_op jit(solution)/shard_map/ppermute | solution.py:436
  17.5 1.5 %collective-permute-start.2 = (f32[2,128,128]{2,1,0:T(8,128)S(1)}, f32[2,128,128]{2,1,0:T(8,128)S(1)}, u32[]{:S(2)}, u32[]{:S(2)}) collective-permute-start(f32[2,128,128]{2,1,0:T(8,128)S(1)} %pad_maximum_fusion), channel_id=1, source_target_pairs={{0,2},{1,3},{2,0},{3,1},{4,6},{5,7},{6,4},{7,5},{8,10},{9,11},{10,... | collective-permute-start | bytes 393224 | tf_op jit(solution)/shard_map/ppermute | solution.py:436
  19.1 1.5 %collective-permute-start.3 = (f32[2,128,128]{2,1,0:T(8,128)S(1)}, f32[2,128,128]{2,1,0:T(8,128)S(1)}, u32[]{:S(2)}, u32[]{:S(2)}) collective-permute-start(f32[2,128,128]{2,1,0:T(8,128)S(1)} %pad_maximum_fusion.1), channel_id=1, source_target_pairs={{0,4},{1,5},{2,6},{3,7},{4,0},{5,1},{6,2},{7,3},{8,12},{9,13},{10,... | collective-permute-start | bytes 393224 | tf_op jit(solution)/shard_map/ppermute | solution.py:436
  20.6 0.6 collective-permute-start.4
  21.2 10.0 %all-to-all-done.rows_ref.meta_ref = bf16[16,200,128]{2,1,0:T(8,128)(2,1)S(1)} async-done(((bf16[16,200,128]{2,1,0:T(8,128)(2,1)}), bf16[16,200,128]{2,1,0:T(8,128)(2,1)S(1)}, u32[]{:S(2)}, u32[]{:S(2)}) %all-to-all-start) | async-done | bytes 819232 | tf_op jit(solution)/shard_map/all_to_all | solution.py:422
  31.2 2.6 %shard_map.79 = (f32[128,128]{1,0:T(8,128)S(1)}, f32[4,136,128]{2,1,0:T(8,128)S(1)}, f32[8,128]{1,0:T(8,128)}) custom-call(bf16[16,200,128]{2,1,0:T(8,128)(2,1)S(1)} %all-to-all-done.rows_ref.meta_ref, bf16[16,200,128]{2,1,0:T(8,128)(2,1)S(1)} %all-to-all-done.rows_ref.meta_ref, s32[1,128]{1,0:T(1,128)S(1)} %bitcast.5), custom_call_target="tpu_custom_call" | custom-call | flops 134217728 | bytes 819200 | tf_op jit(solution)/shard_map/pallas_call | solution.py:49
  33.9 1.3 %collective-permute-start = (f32[128,128]{1,0:T(8,128)S(1)}, f32[128,128]{1,0:T(8,128)S(1)}, u32[]{:S(2)}, u32[]{:S(2)}) collective-permute-start(f32[128,128]{1,0:T(8,128)S(1)} %get-tuple-element.22), channel_id=1, source_target_pairs={{0,8},{1,9},{2,10},{3,11},{4,12},{5,13},{6,14},{7,15},{16,24},{17,... | collective-permute-start | bytes 196616 | tf_op jit(solution)/shard_map/ppermute | solution.py:397
  35.1 2.2 %shard_map.78 = (f32[4,256,256]{2,1,0:T(8,128)S(1)}, bf16[4,256,256]{2,1,0:T(8,128)(2,1)S(1)}, f32[4,256,128]{2,1,0:T(8,128)S(1)}, f32[4,256,128]{2,1,0:T(8,128)S(1)}) custom-call(bf16[16,200,128]{2,1,0:T(8,128)(2,1)S(1)} %all-to-all-done.rows_ref.meta_ref, bf16[16,200,128]{2,1,0:T(8,128)(2,1)S(1)} %all-to-all-done.rows_ref.meta_ref, s32[1,128]{1,0:T(1,128)S(1)} %bitcast.6), custom_call_target="tpu_custom_call" | custom-call | flops 268435456 | bytes 2916352 | tf_op jit(solution)/shard_map/pallas_call | solution.py:49
  37.3 3.6 %collective-permute-done.came_ref = f32[128,128]{1,0:T(8,128)S(1)} collective-permute-done((f32[128,128]{1,0:T(8,128)S(1)}, f32[128,128]{1,0:T(8,128)S(1)}, u32[]{:S(2)}, u32[]{:S(2)}) %collective-permute-start) | collective-permute-done | bytes 65568 | tf_op jit(solution)/shard_map/ppermute | solution.py:397
  40.9 2.1 %shard_map.81 = (bf16[4,256,128]{2,1,0:T(8,128)(2,1)S(1)}, bf16[8,128,128]{2,1,0:T(8,128)(2,1)S(1)}, f32[4,136,128]{2,1,0:T(8,128)S(1)}, f32[128,128]{1,0:T(8,128)S(1)}) custom-call(bf16[16,200,128]{2,1,0:T(8,128)(2,1)S(1)} %all-to-all-done.rows_ref.meta_ref, f32[4,256,128]{2,1,0:T(8,128)S(1)} %get-tuple-element.19.inner_ref, ...), custom_call_target="tpu_custom_call" | custom-call | flops 268435456 | bytes 1867776 | tf_op jit(solution)/shard_map/pallas_call | solution.py:49
  43.0 2.0 %collective-permute-start.5 = (f32[128,128]{1,0:T(8,128)S(1)}, f32[128,128]{1,0:T(8,128)S(1)}, u32[]{:S(2)}, u32[]{:S(2)}) collective-permute-start(f32[128,128]{1,0:T(8,128)S(1)} %get-tuple-element.32), channel_id=1, source_target_pairs={{8,0},{9,1},{10,2},{11,3},{12,4},{13,5},{14,6},{15,7},{24,16},{25,... | collective-permute-start | bytes 196616 | tf_op jit(solution)/shard_map/ppermute | solution.py:397
  45.0 1.3 %shard_map.82 = (bf16[16,64,128]{2,1,0:T(8,128)(2,1)S(1)}, f32[2,4,256,128]{3,2,1,0:T(8,128)S(1)}) custom-call(bf16[16,200,128]{2,1,0:T(8,128)(2,1)S(1)} %all-to-all-done.rows_ref.meta_ref, f32[4,256,256]{2,1,0:T(8,128)S(1)} %get-tuple-element.26.mix_ref, bf16[4,256,256]{2,1,0:T(8,128)(2,1)S(1)} %get-tuple-element.27.weights_ref, ...), custom_call_target="tpu_custom_call" | custom-call | flops 268435456 | bytes 2916352 | tf_op jit(solution)/shard_map/pallas_call | solution.py:49
  46.3 0.5 collective-permute-done.5.came_ref
  46.9 1.3 %shard_map.83 = bf16[16,192,128]{2,1,0:T(8,128)(2,1)} custom-call(bf16[16,200,128]{2,1,0:T(8,128)(2,1)S(1)} %all-to-all-done.rows_ref.meta_ref, f32[4,256,128]{2,1,0:T(8,128)S(1)} %get-tuple-element.20.ends_ref, bf16[16,64,128]{2,1,0:T(8,128)(2,1)S(1)} %get-tuple-element.29.query_ref, f32[2,4,256,128]{3,2,1,0:T(8,128)S(1)} %get-tuple-element.30.part_ref, ...), custom_call_target="tpu_custom_call" | custom-call | flops 134217728 | bytes 1638400 | tf_op jit(solution)/shard_map/pallas_call | solution.py:49
  48.2 6.7 %all-to-all-start.1 = ((bf16[16,192,128]{2,1,0:T(8,128)(2,1)}), bf16[16,192,128]{2,1,0:T(8,128)(2,1)S(1)}, u32[]{:S(2)}, u32[]{:S(2)}) async-start(bf16[16,192,128]{2,1,0:T(8,128)(2,1)} %shard_map.83), calls=%async_computation.1 | async-start | bytes 1572864 | tf_op jit(solution)/shard_map/all_to_all | solution.py:422
  55.1 1.2 %collective-permute-done.6 = bf16[4,128,128]{2,1,0:T(8,128)(2,1)S(1)} collective-permute-done((bf16[4,128,128]{2,1,0:T(8,128)(2,1)S(1)}, bf16[4,128,128]{2,1,0:T(8,128)(2,1)S(1)}, u32[]{:S(2)}, u32[]{:S(2)}) %collective-permute-start.6) | collective-permute-done | bytes 131104 | tf_op jit(solution)/shard_map/ppermute | solution.py:436
  56.4 2.5 %collective-permute-start.9 = (bf16[2,128,128]{2,1,0:T(8,128)(2,1)S(1)}, bf16[2,128,128]{2,1,0:T(8,128)(2,1)S(1)}, u32[]{:S(2)}, u32[]{:S(2)}) collective-permute-start(bf16[2,128,128]{2,1,0:T(8,128)(2,1)S(1)} %pad_maximum_fusion.5), channel_id=1, source_target_pairs={{0,6},{1,7},{2,4},{3,5},{4,2},{5,3},{6,0},{7,1},{8,14},{9,15},{10,... | collective-permute-start | bytes 196616 | tf_op jit(solution)/shard_map/ppermute | solution.py:436
  58.8 0.6 collective-permute-start.7
  59.5 0.6 collective-permute-start.8
  60.1 3.7 %collective-permute-done.7 = bf16[2,128,128]{2,1,0:T(8,128)(2,1)S(1)} collective-permute-done((bf16[2,128,128]{2,1,0:T(8,128)(2,1)S(1)}, bf16[2,128,128]{2,1,0:T(8,128)(2,1)S(1)}, u32[]{:S(2)}, u32[]{:S(2)}) %collective-permute-start.7) | collective-permute-done | bytes 65568 | tf_op jit(solution)/shard_map/ppermute | solution.py:436
  63.8 9.5 %collective-permute-done.8 = bf16[2,128,128]{2,1,0:T(8,128)(2,1)S(1)} collective-permute-done((bf16[2,128,128]{2,1,0:T(8,128)(2,1)S(1)}, bf16[2,128,128]{2,1,0:T(8,128)(2,1)S(1)}, u32[]{:S(2)}, u32[]{:S(2)}) %collective-permute-start.8) | collective-permute-done | bytes 65568 | tf_op jit(solution)/shard_map/ppermute | solution.py:436
  73.4 4.8 %shard_map.85 = bf16[1024,2048]{1,0:T(8,128)(2,1)} custom-call(s32[1]{0:T(128)} %bitcast.3.mine_ref, bf16[8,128,128]{2,1,0:T(8,128)(2,1)S(1)} %constant_dynamic-update-slice_fusion.normed_ref, bf16[128,2048]{1,0:T(8,128)(2,1)S(1)} %get-tuple-element.35.up_ref), custom_call_target="tpu_custom_call" | custom-call | flops 536870912 | bytes 4980736 | tf_op jit(solution)/shard_map/pallas_call | solution.py:49
  78.2 1.1 %shard_map.84 = bf16[128,3072]{1,0:T(8,128)(2,1)} custom-call(bf16[16,192,128]{2,1,0:T(8,128)(2,1)S(1)} %all-to-all-done.1.in_ref), custom_call_target="tpu_custom_call" | custom-call | bytes 1572864 | tf_op jit(solution)/shard_map/pallas_call | solution.py:49
  (29 shorter events, 0.6 us)
Async XLA Ops:
  0.6 1.1 %copy-start.1 = (bf16[128,3072]{1,0:T(8,128)(2,1)S(1)}, bf16[128,3072]{1,0:T(8,128)(2,1)}, u32[]{:S(2)}) copy-start(bf16[128,3072]{1,0:T(8,128)(2,1)} %rows_ref.1) | copy-start | bytes 2359300
  1.8 0.7 copy-start.5
  2.4 0.7 copy-start.6
  4.1 27.1 %copy-start.4 = (s32[128]{0:T(128)S(1)}, s32[128]{0:T(128)}, u32[]{:S(2)}) copy-start(s32[128]{0:T(128)} %param.9) | copy-start | bytes 1540
  4.1 27.1 %all-to-all-start = ((bf16[16,200,128]{2,1,0:T(8,128)(2,1)}), bf16[16,200,128]{2,1,0:T(8,128)(2,1)S(1)}, u32[]{:S(2)}, u32[]{:S(2)}) async-start(bf16[16,200,128]{2,1,0:T(8,128)(2,1)} %shard_map.77), calls=%async_computation | async-start | bytes 1638400 | tf_op jit(solution)/shard_map/all_to_all | solution.py:422
  10.5 2.2 %copy-start = (bf16[1024,2048]{1,0:T(8,128)(2,1)S(1)}, bf16[1024,2048]{1,0:T(8,128)(2,1)}, u32[]{:S(2)}) copy-start(bf16[1024,2048]{1,0:T(8,128)(2,1)} %weight_ref.1) | copy-start | bytes 12582916
  12.6 1.0 %copy-start.2 = (bf16[128,2048]{1,0:T(8,128)(2,1)S(1)}, bf16[128,2048]{1,0:T(8,128)(2,1)}, u32[]{:S(2)}) copy-start(bf16[128,2048]{1,0:T(8,128)(2,1)} %up_ref.1) | copy-start | bytes 1572868
  13.7 0.7 copy-start.3
  15.9 1.6 %collective-permute-start.1 = (f32[4,128,128]{2,1,0:T(8,128)S(1)}, f32[4,128,128]{2,1,0:T(8,128)S(1)}, u32[]{:S(2)}, u32[]{:S(2)}) collective-permute-start(f32[4,128,128]{2,1,0:T(8,128)S(1)} %get-tuple-element.24), channel_id=1, source_target_pairs={{0,1},{1,0},{2,3},{3,2},{4,5},{5,4},{6,7},{7,6},{8,9},{9,8},{10,11... | collective-permute-start | bytes 786440 | tf_op jit(solution)/shard_map/ppermute | solution.py:436
  17.5 19.8 %collective-permute-start.2 = (f32[2,128,128]{2,1,0:T(8,128)S(1)}, f32[2,128,128]{2,1,0:T(8,128)S(1)}, u32[]{:S(2)}, u32[]{:S(2)}) collective-permute-start(f32[2,128,128]{2,1,0:T(8,128)S(1)} %pad_maximum_fusion), channel_id=1, source_target_pairs={{0,2},{1,3},{2,0},{3,1},{4,6},{5,7},{6,4},{7,5},{8,10},{9,11},{10,... | collective-permute-start | bytes 393224 | tf_op jit(solution)/shard_map/ppermute | solution.py:436
  19.1 18.3 %collective-permute-start.3 = (f32[2,128,128]{2,1,0:T(8,128)S(1)}, f32[2,128,128]{2,1,0:T(8,128)S(1)}, u32[]{:S(2)}, u32[]{:S(2)}) collective-permute-start(f32[2,128,128]{2,1,0:T(8,128)S(1)} %pad_maximum_fusion.1), channel_id=1, source_target_pairs={{0,4},{1,5},{2,6},{3,7},{4,0},{5,1},{6,2},{7,3},{8,12},{9,13},{10,... | collective-permute-start | bytes 393224 | tf_op jit(solution)/shard_map/ppermute | solution.py:436
  20.6 16.7 %collective-permute-start.4 = (f32[2,128,128]{2,1,0:T(8,128)S(1)}, f32[2,128,128]{2,1,0:T(8,128)S(1)}, u32[]{:S(2)}, u32[]{:S(2)}) collective-permute-start(f32[2,128,128]{2,1,0:T(8,128)S(1)} %pad_maximum_fusion.2), channel_id=1, source_target_pairs={{0,6},{1,7},{2,4},{3,5},{4,2},{5,3},{6,0},{7,1},{8,14},{9,15},{10,... | collective-permute-start | bytes 393224 | tf_op jit(solution)/shard_map/ppermute | solution.py:436
  33.9 7.0 %collective-permute-start = (f32[128,128]{1,0:T(8,128)S(1)}, f32[128,128]{1,0:T(8,128)S(1)}, u32[]{:S(2)}, u32[]{:S(2)}) collective-permute-start(f32[128,128]{1,0:T(8,128)S(1)} %get-tuple-element.22), channel_id=1, source_target_pairs={{0,8},{1,9},{2,10},{3,11},{4,12},{5,13},{6,14},{7,15},{16,24},{17,... | collective-permute-start | bytes 196616 | tf_op jit(solution)/shard_map/ppermute | solution.py:397
  43.0 3.8 %collective-permute-start.5 = (f32[128,128]{1,0:T(8,128)S(1)}, f32[128,128]{1,0:T(8,128)S(1)}, u32[]{:S(2)}, u32[]{:S(2)}) collective-permute-start(f32[128,128]{1,0:T(8,128)S(1)} %get-tuple-element.32), channel_id=1, source_target_pairs={{8,0},{9,1},{10,2},{11,3},{12,4},{13,5},{14,6},{15,7},{24,16},{25,... | collective-permute-start | bytes 196616 | tf_op jit(solution)/shard_map/ppermute | solution.py:397
  48.2 30.0 %all-to-all-start.1 = ((bf16[16,192,128]{2,1,0:T(8,128)(2,1)}), bf16[16,192,128]{2,1,0:T(8,128)(2,1)S(1)}, u32[]{:S(2)}, u32[]{:S(2)}) async-start(bf16[16,192,128]{2,1,0:T(8,128)(2,1)} %shard_map.83), calls=%async_computation.1 | async-start | bytes 1572864 | tf_op jit(solution)/shard_map/all_to_all | solution.py:422
  54.9 1.4 %collective-permute-start.6 = (bf16[4,128,128]{2,1,0:T(8,128)(2,1)S(1)}, bf16[4,128,128]{2,1,0:T(8,128)(2,1)S(1)}, u32[]{:S(2)}, u32[]{:S(2)}) collective-permute-start(bf16[4,128,128]{2,1,0:T(8,128)(2,1)S(1)} %slice.65), channel_id=1, source_target_pairs={{0,1},{1,0},{2,3},{3,2},{4,5},{5,4},{6,7},{7,6},{8,9},{9,8},{10,11... | collective-permute-start | bytes 393224 | tf_op jit(solution)/shard_map/ppermute | solution.py:436
  56.4 17.0 %collective-permute-start.9 = (bf16[2,128,128]{2,1,0:T(8,128)(2,1)S(1)}, bf16[2,128,128]{2,1,0:T(8,128)(2,1)S(1)}, u32[]{:S(2)}, u32[]{:S(2)}) collective-permute-start(bf16[2,128,128]{2,1,0:T(8,128)(2,1)S(1)} %pad_maximum_fusion.5), channel_id=1, source_target_pairs={{0,6},{1,7},{2,4},{3,5},{4,2},{5,3},{6,0},{7,1},{8,14},{9,15},{10,... | collective-permute-start | bytes 196616 | tf_op jit(solution)/shard_map/ppermute | solution.py:436
  58.8 4.9 %collective-permute-start.7 = (bf16[2,128,128]{2,1,0:T(8,128)(2,1)S(1)}, bf16[2,128,128]{2,1,0:T(8,128)(2,1)S(1)}, u32[]{:S(2)}, u32[]{:S(2)}) collective-permute-start(bf16[2,128,128]{2,1,0:T(8,128)(2,1)S(1)} %pad_maximum_fusion.3), channel_id=1, source_target_pairs={{0,2},{1,3},{2,0},{3,1},{4,6},{5,7},{6,4},{7,5},{8,10},{9,11},{10,... | collective-permute-start | bytes 196616 | tf_op jit(solution)/shard_map/ppermute | solution.py:436
  59.5 13.9 %collective-permute-start.8 = (bf16[2,128,128]{2,1,0:T(8,128)(2,1)S(1)}, bf16[2,128,128]{2,1,0:T(8,128)(2,1)S(1)}, u32[]{:S(2)}, u32[]{:S(2)}) collective-permute-start(bf16[2,128,128]{2,1,0:T(8,128)(2,1)S(1)} %pad_maximum_fusion.4), channel_id=1, source_target_pairs={{0,4},{1,5},{2,6},{3,7},{4,0},{5,1},{6,2},{7,3},{8,12},{9,13},{10,... | collective-permute-start | bytes 196616 | tf_op jit(solution)/shard_map/ppermute | solution.py:436

commit v3 on v2

--- a/solution.py
+++ b/solution.py
@@ -178,29 +178,53 @@
     )
 
 
-def grad_weight_kernel(mine_ref, normed_ref, up_ref, out_ref):
-    out_ref[...] = dot_tn(normed_ref[0], up_ref[...]).astype(bf16)
-
-
-def grad_weight_of(normed, upstream, mine):
-    heads, rows, _ = normed.shape
-    width = upstream.shape[1]
-    return call(
-        grad_weight_kernel,
-        jax.ShapeDtypeStruct((heads * LANES, width), bf16),
-        (mine.reshape(1), normed, upstream),
-        flops=2 * rows * heads * LANES * width,
-        moved=2 * (upstream.size + normed.size + heads * LANES * width),
-        grid_spec=pltpu.PrefetchScalarGridSpec(
-            num_scalar_prefetch=1,
-            grid=(heads,),
-            in_specs=[
-                pl.BlockSpec((1, rows, LANES), lambda i, mine: (i, 0, 0)),
-                pl.BlockSpec((rows, width), lambda i, mine: (0, 0)),
-            ],
-            out_specs=pl.BlockSpec((LANES, width), lambda i, mine: (jnp.bitwise_xor(mine[0], i), 0)),
-        ),
-    )
+def grad_weight_of(normed, upstream, heads, mine):
+    rows, width = upstream.shape
+    total = jax.ShapeDtypeStruct((heads * LANES, width), bf16)
+    calls = [normed[:2]] + [[pair] for pair in normed[2:]]
+    out = None
+    for at, pieces in enumerate(calls):
+        count = sum(piece.shape[0] for piece in pieces)
+
+        def body(mine_ref, *refs):
+            *piece_refs, up_ref, out_ref = refs[: len(pieces) + 1] + refs[-1:]
+            step = pl.program_id(0)
+            first = 0
+            for piece_ref in piece_refs:
+                for i in range(piece_ref.shape[0]):
+
+                    @pl.when(step == first)
+                    def _(piece_ref=piece_ref, i=i):
+                        out_ref[...] = dot_tn(piece_ref[i], up_ref[...]).astype(bf16)
+
+                    first += 1
+
+        given = [] if out is None else [out]
+        out = pl.pallas_call(
+            body,
+            out_shape=total,
+            grid_spec=pltpu.PrefetchScalarGridSpec(
+                num_scalar_prefetch=1,
+                grid=(count,),
+                in_specs=[
+                    pl.BlockSpec(piece.shape, lambda i, mine: (0, 0, 0)) for piece in pieces
+                ]
+                + [pl.BlockSpec((rows, width), lambda i, mine: (0, 0))]
+                + [ANY for _ in given],
+                out_specs=pl.BlockSpec(
+                    (LANES, width),
+                    lambda i, mine, at=at: (jnp.bitwise_xor(mine[0], 2 * at + i), 0),
+                ),
+            ),
+            input_output_aliases={len(pieces) + 2: 0} if given else {},
+            compiler_params=PARAMS,
+            cost_estimate=pl.CostEstimate(
+                flops=2 * rows * count * LANES * width,
+                bytes_accessed=2 * count * LANES * width,
+                transcendentals=0,
+            ),
+        )(mine.reshape(1), *pieces, upstream, *given)
+    return out
 
 
 def part_rows(ref, part, chunk):
@@ -263,7 +287,7 @@
         keep_ref[chunk, LANES:, :] = jnp.where(line == 0, before, total)
         state = total * state + dot_tn(high, value) + dot_tn(low, value)
         before = total * before
-    last_ref[...] = state
+    last_ref[...] = state.astype(bf16)
     gain_ref[...] = jnp.broadcast_to(before, (8, LANES))
 
 
@@ -285,6 +309,13 @@
         weights_ref[chunk] = weights
         inner_ref[chunk] = dot(weights, value)
         ends_ref[chunk] = jnp.where(lane == 0, enter, leave)
+
+
+def arriving(came_ref, heads, step):
+    segment = lax.div(lax.axis_index("seq"), heads)
+    last = lax.div(lax.axis_size("seq"), heads) - 1
+    end = 0 if step == 1 else last
+    return jnp.where(segment == end, 0.0, came_ref[...].astype(f32))
 
 
 def entering(keep_ref, chunk, came):
@@ -312,7 +343,7 @@
     back = jnp.zeros((LANES, LANES), f32)
     after = jnp.ones((1, LANES), f32)
     line = iota((8, LANES), 0)
-    came = came_ref[...]
+    came = arriving(came_ref, heads, 1)
     normed_rows = []
     for chunk in range(chunks):
         query = part_rows(rows_ref, 0, chunk)
@@ -350,13 +381,13 @@
         high, low = halves(query.astype(f32) * enter)
         back = gain * back + dot_tn(high, grad) + dot_tn(low, grad)
         after = gain * after
-    last_ref[...] = back
+    last_ref[...] = back.astype(bf16)
 
 
 def local_kernel(
-    chunks, rows_ref, mix_ref, weights_ref, ends_ref, keep_ref, came_ref, grad_ref, query_ref, part_ref
+    heads, chunks, rows_ref, mix_ref, weights_ref, ends_ref, keep_ref, came_ref, grad_ref, query_ref, part_ref
 ):
-    came = came_ref[...]
+    came = arriving(came_ref, heads, 1)
     for chunk in range(chunks):
         query, key, value = (part_rows(rows_ref, part, chunk) for part in range(3))
         grad = grad_ref[chunk]
@@ -371,9 +402,9 @@
         part_ref[1, chunk] = dot_tn(weights_ref[chunk], grad)
 
 
-def final_kernel(chunks, rows_ref, ends_ref, query_ref, part_ref, back_ref, came_ref, out_ref):
+def final_kernel(heads, chunks, rows_ref, ends_ref, query_ref, part_ref, back_ref, came_ref, out_ref):
     per = chunks * 16
-    came = came_ref[...]
+    came = arriving(came_ref, heads, -1)
     out_ref[:, 0:per, :] = query_ref[...]
     for chunk in range(chunks):
         key, value = (part_rows(rows_ref, part, chunk) for part in (1, 2))
@@ -387,6 +418,10 @@
 
 
 def carried(last, gain, segments, heads, step):
+    if segments == 2:
+        pairs = [(i, (i + heads) % (2 * heads)) for i in range(2 * heads)]
+        return lax.ppermute(last, "seq", pairs)
+
     def shift(value, by):
         pairs = [
             (s * heads + h, (s + by * step) * heads + h)
@@ -469,7 +504,7 @@
     unit = 2 * chunks * CHUNK * LANES
     last, keep, gain = call(
         functools.partial(state_kernel, heads, chunks),
-        (shape(LANES, LANES), shape(*states), shape(8, LANES)),
+        (shape(LANES, LANES, dtype=bf16), shape(*states), shape(8, LANES)),
         (arrived, meta, place),
         flops=unit * 512,
         moved=2 * arrived.size,
@@ -490,7 +525,7 @@
         functools.partial(output_kernel, heads, chunks, runs),
         (
             shape(*tall, dtype=bf16), shape(heads, rows, LANES, dtype=bf16), shape(*states),
-            shape(LANES, LANES),
+            shape(LANES, LANES, dtype=bf16),
         ),
         (arrived, inner, ends, keep, came, *normal),
         flops=unit * 1024,
@@ -504,7 +539,7 @@
     )
     came_back = carried(last, gain, segments, heads, -1)
     grad_query, part = call(
-        functools.partial(local_kernel, chunks),
+        functools.partial(local_kernel, heads, chunks),
         (shape(*low, dtype=bf16), shape(2, *tall)),
         (arrived, mix, weights, ends, keep, came, grad),
         flops=unit * 1024,
@@ -513,7 +548,7 @@
         out_specs=[VMEM] * 2,
     )
     grads = call(
-        functools.partial(final_kernel, chunks),
+        functools.partial(final_kernel, heads, chunks),
         shape(16, 3 * chunks * 16, LANES, dtype=bf16),
         (arrived, ends, grad_query, part, back, came_back),
         flops=unit * 512,
@@ -523,7 +558,7 @@
     )
     normed, grads = lax.optimization_barrier((normed, grads))
     if per == 16:
-        normed = jnp.concatenate(deal(normed[: heads // 2], normed[heads // 2 :]))
+        normed = deal(normed[: heads // 2], normed[heads // 2 :])
     else:
         normed = normed.reshape(2, heads // 2, rows, LANES).swapaxes(0, 1)
         normed = normed.reshape(heads, rows, LANES)
@@ -531,11 +566,12 @@
         normed = normed.reshape(chunks, peers, CHUNK // rows, rows // peers, LANES)
         normed = among_heads(normed.swapaxes(1, 2).reshape(heads, rows, LANES))
         normed = jnp.stack([normed[step] for step in steps])
+        normed = [normed[0:1], normed[1:2], *(normed[i : i + 2] for i in range(2, heads, 2))]
         grads = grads.reshape(16, 3, chunks, 16, LANES).transpose(1, 2, 0, 3, 4)
         grads = grads.reshape(3, chunks, peers, per, LANES).transpose(2, 0, 1, 3, 4)
         grads = grads.reshape(peers, 3 * per_seg, LANES)
     grad_projected = unpack(exchange(grads), rows, heads, segments)
-    grad_weight = grad_weight_of(normed, turned, mine)
+    grad_weight = grad_weight_of(normed, turned, heads, mine)
     return (grad_projected, grad_weight)
 
 

time: 79.8 us -> 74 us (0.927)
  starting transfers between devices: 24.1 us -> 18.9 us
  waiting for transfers between devices: 29.9 us -> 28.4 us
  Pallas kernels: 18.1 us -> 19.1 us
    pallas_call x0 -> x4, Pallas kernels: none -> 5.84 us  [grad_weight_of(): pl.pallas_call(body, out_shape=total, grid_spec=pltpu.PrefetchScalarGridS...]
    pallas_call x9 -> x8, Pallas kernels: 18.1 us -> 13.2 us  [call(): pl.pallas_call(body, out_shape=outs, compiler_params=PARAMS, cost_estimat...]
    ppermute x8, waiting for transfers between devices: 15.8 us -> 12.7 us  [swap(): return lax.ppermute(value, 'seq', [(i, i ^ step) for i in range(peers)])]
    ppermute x2, starting transfers between devices: 3.23 us -> 0.44 us  [carried(): return lax.ppermute(last, 'seq', pairs)]
    all_to_all x2, starting transfers between devices: 13 us -> 10.6 us  [exchange(): return lax.all_to_all(value, 'seq', split_axis=0, concat_axis=0, tiled=True)]
    ppermute x2, waiting for transfers between devices: 4.09 us -> 5.71 us  [carried(): return lax.ppermute(last, 'seq', pairs)]
    unnamed x16 -> x14, local copies, waits for them, and re-layouts: 6.37 us -> 6.34 us
  transfers between devices with their start and end apart: 12 -> 12, of which waited for: 7 -> 8; matrix products, arithmetic and copies ran while one was open for 0% -> 0% of each run, Pallas kernels for 16% -> 18%
where the time goes in v3:
time: 74 us; the launch traced here: 73.5 us
  waiting for transfers between devices  28.4 us (38%)
  Pallas kernels  19.1 us (26%)
  starting transfers between devices  18.9 us (26%)
  local copies, waits for them, and re-layouts  6.41 us (9%)
  between operations  0.76 us (1%)
    pallas_call x8, Pallas kernels, call(): pl.pallas_call(body, out_shape=outs, compiler_params=PARAMS, cost_estimat...  13.2 us
    ppermute x8, waiting for transfers between devices, swap(): return lax.ppermute(value, 'seq', [(i, i ^ step) for i in range(peers)])  12.7 us
    all_to_all x2, starting transfers between devices, exchange(): return lax.all_to_all(value, 'seq', split_axis=0, concat_axis=0, tiled=True)  10.6 us
    all_to_all x2, waiting for transfers between devices, exchange(): return lax.all_to_all(value, 'seq', split_axis=0, concat_axis=0, tiled=True)  9.98 us
    ppermute x8, starting transfers between devices, swap(): return lax.ppermute(value, 'seq', [(i, i ^ step) for i in range(peers)])  7.79 us
    unnamed x14, local copies, waits for them, and re-layouts  6.34 us
    pallas_call x4, Pallas kernels, grad_weight_of(): pl.pallas_call(body, out_shape=total, grid_spec=pltpu.PrefetchScalarGridS...  5.84 us
    ppermute x2, waiting for transfers between devices, carried(): return lax.ppermute(last, 'seq', pairs)  5.71 us
  transfers between devices with their start and end apart: 12, of which 8 were waited for; matrix products, arithmetic and copies ran while one was open for 0% of the time, Pallas kernels for 18%

profile of v3, /device:TPU:18, one launch (start us, length us, event | category | flops | bytes accessed | tf_op | source)
XLA Modules:
  0.0 73.5 jit_solution(1333515645043675880)
XLA Ops:
  0.6 1.1 %copy-done.1 = bf16[128,3072]{1,0:T(8,128)(2,1)S(1)} copy-done((bf16[128,3072]{1,0:T(8,128)(2,1)S(1)}, bf16[128,3072]{1,0:T(8,128)(2,1)}, u32[]{:S(2)}) %copy-start.1) | copy-done | bytes 786456
  1.8 0.7 copy-done.5
  2.4 0.7 copy-done.6
  3.1 1.0 %shard_map.77 = bf16[16,200,128]{2,1,0:T(8,128)(2,1)} custom-call(bf16[128,3072]{1,0:T(8,128)(2,1)S(1)} %copy-done.1, bf16[8,128]{1,0:T(8,128)(2,1)S(1)} %bitcast.7, s32[1,128]{1,0:T(1,128)S(1)} %bitcast.8), custom_call_target="tpu_custom_call" | custom-call | bytes 1572864 | tf_op jit(solution)/shard_map/pallas_call | solution.py:49
  4.1 6.3 %all-to-all-start = ((bf16[16,200,128]{2,1,0:T(8,128)(2,1)}), bf16[16,200,128]{2,1,0:T(8,128)(2,1)S(1)}, u32[]{:S(2)}, u32[]{:S(2)}) async-start(bf16[16,200,128]{2,1,0:T(8,128)(2,1)} %shard_map.77), calls=%async_computation | async-start | bytes 1638400 | tf_op jit(solution)/shard_map/all_to_all | solution.py:457
  10.5 2.2 %copy-done = bf16[1024,2048]{1,0:T(8,128)(2,1)S(1)} copy-done((bf16[1024,2048]{1,0:T(8,128)(2,1)S(1)}, bf16[1024,2048]{1,0:T(8,128)(2,1)}, u32[]{:S(2)}) %copy-start) | copy-done | bytes 4194328
  12.6 1.0 %copy-done.2 = bf16[128,2048]{1,0:T(8,128)(2,1)S(1)} copy-done((bf16[128,2048]{1,0:T(8,128)(2,1)S(1)}, bf16[128,2048]{1,0:T(8,128)(2,1)}, u32[]{:S(2)}) %copy-start.2) | copy-done | bytes 524312
  13.7 0.7 copy-done.3
  14.3 1.5 %shard_map.80 = (f32[4,128,128]{2,1,0:T(8,128)S(1)}, f32[4,128,128]{2,1,0:T(8,128)S(1)}, bf16[128,2048]{1,0:T(8,128)(2,1)S(1)}) custom-call(bf16[128,2048]{1,0:T(8,128)(2,1)S(1)} %copy-done.2, s32[1,128]{1,0:T(1,128)S(1)} %bitcast.4, bf16[1024,2048]{1,0:T(8,128)(2,1)S(1)} %copy-done), custom_call_target="tpu_custom_call" | custom-call | flops 536870912 | bytes 5242880 | tf_op jit(solution)/shard_map/pallas_call | solution.py:49
  16.1 1.4 %collective-permute-done.1 = f32[4,128,128]{2,1,0:T(8,128)S(1)} collective-permute-done((f32[4,128,128]{2,1,0:T(8,128)S(1)}, f32[4,128,128]{2,1,0:T(8,128)S(1)}, u32[]{:S(2)}, u32[]{:S(2)}) %collective-permute-start.1) | collective-permute-done | bytes 262176 | tf_op jit(solution)/shard_map/ppermute | solution.py:471
  17.5 1.5 %collective-permute-start.2 = (f32[2,128,128]{2,1,0:T(8,128)S(1)}, f32[2,128,128]{2,1,0:T(8,128)S(1)}, u32[]{:S(2)}, u32[]{:S(2)}) collective-permute-start(f32[2,128,128]{2,1,0:T(8,128)S(1)} %pad_maximum_fusion), channel_id=1, source_target_pairs={{0,2},{1,3},{2,0},{3,1},{4,6},{5,7},{6,4},{7,5},{8,10},{9,11},{10,... | collective-permute-start | bytes 393224 | tf_op jit(solution)/shard_map/ppermute | solution.py:471
  19.1 1.5 %collective-permute-start.3 = (f32[2,128,128]{2,1,0:T(8,128)S(1)}, f32[2,128,128]{2,1,0:T(8,128)S(1)}, u32[]{:S(2)}, u32[]{:S(2)}) collective-permute-start(f32[2,128,128]{2,1,0:T(8,128)S(1)} %pad_maximum_fusion.1), channel_id=1, source_target_pairs={{0,4},{1,5},{2,6},{3,7},{4,0},{5,1},{6,2},{7,3},{8,12},{9,13},{10,... | collective-permute-start | bytes 393224 | tf_op jit(solution)/shard_map/ppermute | solution.py:471
  21.2 10.0 %all-to-all-done.rows_ref.meta_ref = bf16[16,200,128]{2,1,0:T(8,128)(2,1)S(1)} async-done(((bf16[16,200,128]{2,1,0:T(8,128)(2,1)}), bf16[16,200,128]{2,1,0:T(8,128)(2,1)S(1)}, u32[]{:S(2)}, u32[]{:S(2)}) %all-to-all-start) | async-done | bytes 819232 | tf_op jit(solution)/shard_map/all_to_all | solution.py:457
  31.2 2.6 %shard_map.79 = (bf16[128,128]{1,0:T(8,128)(2,1)S(1)}, f32[4,136,128]{2,1,0:T(8,128)S(1)}, f32[8,128]{1,0:T(8,128)}) custom-call(bf16[16,200,128]{2,1,0:T(8,128)(2,1)S(1)} %all-to-all-done.rows_ref.meta_ref, bf16[16,200,128]{2,1,0:T(8,128)(2,1)S(1)} %all-to-all-done.rows_ref.meta_ref, s32[1,128]{1,0:T(1,128)S(1)} %bitcast.5), custom_call_target="tpu_custom_call" | custom-call | flops 134217728 | bytes 819200 | tf_op jit(solution)/shard_map/pallas_call | solution.py:49
  33.9 2.2 %shard_map.78 = (f32[4,256,256]{2,1,0:T(8,128)S(1)}, bf16[4,256,256]{2,1,0:T(8,128)(2,1)S(1)}, f32[4,256,128]{2,1,0:T(8,128)S(1)}, f32[4,256,128]{2,1,0:T(8,128)S(1)}) custom-call(bf16[16,200,128]{2,1,0:T(8,128)(2,1)S(1)} %all-to-all-done.rows_ref.meta_ref, bf16[16,200,128]{2,1,0:T(8,128)(2,1)S(1)} %all-to-all-done.rows_ref.meta_ref, s32[1,128]{1,0:T(1,128)S(1)} %bitcast.6), custom_call_target="tpu_custom_call" | custom-call | flops 268435456 | bytes 2916352 | tf_op jit(solution)/shard_map/pallas_call | solution.py:49
  36.1 2.6 %collective-permute-done.came_ref = bf16[128,128]{1,0:T(8,128)(2,1)S(1)} collective-permute-done((bf16[128,128]{1,0:T(8,128)(2,1)S(1)}, bf16[128,128]{1,0:T(8,128)(2,1)S(1)}, u32[]{:S(2)}, u32[]{:S(2)}) %collective-permute-start) | collective-permute-done | bytes 32800 | tf_op jit(solution)/shard_map/ppermute | solution.py:423
  38.7 2.1 %shard_map.81 = (bf16[4,256,128]{2,1,0:T(8,128)(2,1)S(1)}, bf16[8,128,128]{2,1,0:T(8,128)(2,1)S(1)}, f32[4,136,128]{2,1,0:T(8,128)S(1)}, bf16[128,128]{1,0:T(8,128)(2,1)S(1)}) custom-call(bf16[16,200,128]{2,1,0:T(8,128)(2,1)S(1)} %all-to-all-done.rows_ref.meta_ref, f32[4,256,128]{2,1,0:T(8,128)S(1)} %get-tuple-element.19.inner_ref, ...), custom_call_target="tpu_custom_call" | custom-call | flops 268435456 | bytes 1867776 | tf_op jit(solution)/shard_map/pallas_call | solution.py:49
  41.2 1.3 %shard_map.82 = (bf16[16,64,128]{2,1,0:T(8,128)(2,1)S(1)}, f32[2,4,256,128]{3,2,1,0:T(8,128)S(1)}) custom-call(bf16[16,200,128]{2,1,0:T(8,128)(2,1)S(1)} %all-to-all-done.rows_ref.meta_ref, f32[4,256,256]{2,1,0:T(8,128)S(1)} %get-tuple-element.26.mix_ref, bf16[4,256,256]{2,1,0:T(8,128)(2,1)S(1)} %get-tuple-element.27.weights_ref, ...), custom_call_target="tpu_custom_call" | custom-call | flops 268435456 | bytes 2916352 | tf_op jit(solution)/shard_map/pallas_call | solution.py:49
  42.6 3.1 %collective-permute-done.5.came_ref = bf16[128,128]{1,0:T(8,128)(2,1)S(1)} collective-permute-done((bf16[128,128]{1,0:T(8,128)(2,1)S(1)}, bf16[128,128]{1,0:T(8,128)(2,1)S(1)}, u32[]{:S(2)}, u32[]{:S(2)}) %collective-permute-start.5) | collective-permute-done | bytes 32800 | tf_op jit(solution)/shard_map/ppermute | solution.py:423
  45.7 1.3 %shard_map.83 = bf16[16,192,128]{2,1,0:T(8,128)(2,1)} custom-call(bf16[16,200,128]{2,1,0:T(8,128)(2,1)S(1)} %all-to-all-done.rows_ref.meta_ref, f32[4,256,128]{2,1,0:T(8,128)S(1)} %get-tuple-element.20.ends_ref, bf16[16,64,128]{2,1,0:T(8,128)(2,1)S(1)} %get-tuple-element.29.query_ref, f32[2,4,256,128]{3,2,1,0:T(8,128)S(1)} %get-tuple-element.30.part_ref, ...), custom_call_target="tpu_custom_call" | custom-call | flops 134217728 | bytes 1638400 | tf_op jit(solution)/shard_map/pallas_call | solution.py:49
  47.0 4.3 %all-to-all-start.1 = ((bf16[16,192,128]{2,1,0:T(8,128)(2,1)}), bf16[16,192,128]{2,1,0:T(8,128)(2,1)S(1)}, u32[]{:S(2)}, u32[]{:S(2)}) async-start(bf16[16,192,128]{2,1,0:T(8,128)(2,1)} %shard_map.83), calls=%async_computation.1 | async-start | bytes 1572864 | tf_op jit(solution)/shard_map/all_to_all | solution.py:457
  51.5 1.2 %collective-permute-done.6 = bf16[4,128,128]{2,1,0:T(8,128)(2,1)S(1)} collective-permute-done((bf16[4,128,128]{2,1,0:T(8,128)(2,1)S(1)}, bf16[4,128,128]{2,1,0:T(8,128)(2,1)S(1)}, u32[]{:S(2)}, u32[]{:S(2)}) %collective-permute-start.6) | collective-permute-done | bytes 131104 | tf_op jit(solution)/shard_map/ppermute | solution.py:471
  52.8 1.5 %collective-permute-start.8 = (bf16[2,128,128]{2,1,0:T(8,128)(2,1)S(1)}, bf16[2,128,128]{2,1,0:T(8,128)(2,1)S(1)}, u32[]{:S(2)}, u32[]{:S(2)}) collective-permute-start(bf16[2,128,128]{2,1,0:T(8,128)(2,1)S(1)} %pad_maximum_fusion.4), channel_id=1, source_target_pairs={{0,4},{1,5},{2,6},{3,7},{4,0},{5,1},{6,2},{7,3},{8,12},{9,13},{10,... | collective-permute-start | bytes 196616 | tf_op jit(solution)/shard_map/ppermute | solution.py:471
  54.3 1.5 %collective-permute-start.9 = (bf16[2,128,128]{2,1,0:T(8,128)(2,1)S(1)}, bf16[2,128,128]{2,1,0:T(8,128)(2,1)S(1)}, u32[]{:S(2)}, u32[]{:S(2)}) collective-permute-start(bf16[2,128,128]{2,1,0:T(8,128)(2,1)S(1)} %pad_maximum_fusion.5), channel_id=1, source_target_pairs={{0,2},{1,3},{2,0},{3,1},{4,6},{5,7},{6,4},{7,5},{8,10},{9,11},{10,... | collective-permute-start | bytes 196616 | tf_op jit(solution)/shard_map/ppermute | solution.py:471
  56.5 1.5 %shard_map.85.refs_2_ = bf16[1024,2048]{1,0:T(8,128)(2,1)} custom-call(s32[1]{0:T(128)} %bitcast.3.mine_ref, bf16[1,128,128]{2,1,0:T(8,128)(2,1)S(1)} %get-tuple-element.36.refs_0_, bf16[1,128,128]{2,1,0:T(8,128)(2,1)S(1)} %get-tuple-element.48.refs_1_, bf16[128,2048]{1,0:T(8,128)(2,1)S(1)} %get-tuple-element.35.refs_2_.refs_1_), custom_call_target="tpu_custom_call" | custom-call | flops 134217728 | bytes 1048576 | tf_op jit(solution)/shard_map/pallas_call | solution.py:203
  57.9 1.6 %collective-permute-done.9.refs_0_ = bf16[2,128,128]{2,1,0:T(8,128)(2,1)S(1)} collective-permute-done((bf16[2,128,128]{2,1,0:T(8,128)(2,1)S(1)}, bf16[2,128,128]{2,1,0:T(8,128)(2,1)S(1)}, u32[]{:S(2)}, u32[]{:S(2)}) %collective-permute-start.9) | collective-permute-done | bytes 65568 | tf_op jit(solution)/shard_map/ppermute | solution.py:471
  59.5 1.5 %shard_map.86.refs_2_ = bf16[1024,2048]{1,0:T(8,128)(2,1)} custom-call(s32[1]{0:T(128)} %bitcast.3.mine_ref, bf16[2,128,128]{2,1,0:T(8,128)(2,1)S(1)} %collective-permute-done.9.refs_0_, bf16[128,2048]{1,0:T(8,128)(2,1)S(1)} %get-tuple-element.35.refs_2_.refs_1_, bf16[1024,2048]{1,0:T(8,128)(2,1)} %shard_map.85.refs_2_), custom_call_target="tpu_custom_call", output_to_operand_aliasing={{}: (3, {})} | custom-call | flops 134217728 | bytes 1048576 | tf_op jit(solution)/shard_map/pallas_call | solution.py:203
  61.0 7.6 %collective-permute-done.8.refs_0_ = bf16[2,128,128]{2,1,0:T(8,128)(2,1)S(1)} collective-permute-done((bf16[2,128,128]{2,1,0:T(8,128)(2,1)S(1)}, bf16[2,128,128]{2,1,0:T(8,128)(2,1)S(1)}, u32[]{:S(2)}, u32[]{:S(2)}) %collective-permute-start.8) | collective-permute-done | bytes 65568 | tf_op jit(solution)/shard_map/ppermute | solution.py:471
  68.6 1.5 %shard_map.87.refs_2_ = bf16[1024,2048]{1,0:T(8,128)(2,1)} custom-call(s32[1]{0:T(128)} %bitcast.3.mine_ref, bf16[2,128,128]{2,1,0:T(8,128)(2,1)S(1)} %collective-permute-done.8.refs_0_, bf16[128,2048]{1,0:T(8,128)(2,1)S(1)} %get-tuple-element.35.refs_2_.refs_1_, bf16[1024,2048]{1,0:T(8,128)(2,1)} %shard_map.86.refs_2_), custom_call_target="tpu_custom_call", output_to_operand_aliasing={{}: (3, {})} | custom-call | flops 134217728 | bytes 1048576 | tf_op jit(solution)/shard_map/pallas_call | solution.py:203
  70.1 0.9 %collective-permute-done.7.refs_0_ = bf16[2,128,128]{2,1,0:T(8,128)(2,1)S(1)} collective-permute-done((bf16[2,128,128]{2,1,0:T(8,128)(2,1)S(1)}, bf16[2,128,128]{2,1,0:T(8,128)(2,1)S(1)}, u32[]{:S(2)}, u32[]{:S(2)}) %collective-permute-start.7) | collective-permute-done | bytes 65568 | tf_op jit(solution)/shard_map/ppermute | solution.py:471
  71.0 1.5 %shard_map.88 = bf16[1024,2048]{1,0:T(8,128)(2,1)} custom-call(s32[1]{0:T(128)} %bitcast.3.mine_ref, bf16[2,128,128]{2,1,0:T(8,128)(2,1)S(1)} %collective-permute-done.7.refs_0_, bf16[128,2048]{1,0:T(8,128)(2,1)S(1)} %get-tuple-element.35.refs_2_.refs_1_, bf16[1024,2048]{1,0:T(8,128)(2,1)} %shard_map.87.refs_2_), custom_call_target="tpu_custom_call", output_to_operand_aliasing={{}: (3, {})} | custom-call | flops 134217728 | bytes 1048576 | tf_op jit(solution)/shard_map/pallas_call | solution.py:203
  72.5 1.1 %shard_map.84 = bf16[128,3072]{1,0:T(8,128)(2,1)} custom-call(bf16[16,192,128]{2,1,0:T(8,128)(2,1)S(1)} %all-to-all-done.1.in_ref), custom_call_target="tpu_custom_call" | custom-call | bytes 1572864 | tf_op jit(solution)/shard_map/pallas_call | solution.py:49
  (29 shorter events, 2.3 us)
Async XLA Ops:
  0.6 1.1 %copy-start.1 = (bf16[128,3072]{1,0:T(8,128)(2,1)S(1)}, bf16[128,3072]{1,0:T(8,128)(2,1)}, u32[]{:S(2)}) copy-start(bf16[128,3072]{1,0:T(8,128)(2,1)} %rows_ref.1) | copy-start | bytes 2359300
  1.8 0.7 copy-start.5
  2.4 0.7 copy-start.6
  4.1 27.1 %copy-start.4 = (s32[128]{0:T(128)S(1)}, s32[128]{0:T(128)}, u32[]{:S(2)}) copy-start(s32[128]{0:T(128)} %param.9) | copy-start | bytes 1540
  4.1 27.1 %all-to-all-start = ((bf16[16,200,128]{2,1,0:T(8,128)(2,1)}), bf16[16,200,128]{2,1,0:T(8,128)(2,1)S(1)}, u32[]{:S(2)}, u32[]{:S(2)}) async-start(bf16[16,200,128]{2,1,0:T(8,128)(2,1)} %shard_map.77), calls=%async_computation | async-start | bytes 1638400 | tf_op jit(solution)/shard_map/all_to_all | solution.py:457
  10.5 2.2 %copy-start = (bf16[1024,2048]{1,0:T(8,128)(2,1)S(1)}, bf16[1024,2048]{1,0:T(8,128)(2,1)}, u32[]{:S(2)}) copy-start(bf16[1024,2048]{1,0:T(8,128)(2,1)} %weight_ref.1) | copy-start | bytes 12582916
  12.6 1.0 %copy-start.2 = (bf16[128,2048]{1,0:T(8,128)(2,1)S(1)}, bf16[128,2048]{1,0:T(8,128)(2,1)}, u32[]{:S(2)}) copy-start(bf16[128,2048]{1,0:T(8,128)(2,1)} %up_ref.1) | copy-start | bytes 1572868
  13.7 0.7 copy-start.3
  15.9 1.6 %collective-permute-start.1 = (f32[4,128,128]{2,1,0:T(8,128)S(1)}, f32[4,128,128]{2,1,0:T(8,128)S(1)}, u32[]{:S(2)}, u32[]{:S(2)}) collective-permute-start(f32[4,128,128]{2,1,0:T(8,128)S(1)} %get-tuple-element.24), channel_id=1, source_target_pairs={{0,1},{1,0},{2,3},{3,2},{4,5},{5,4},{6,7},{7,6},{8,9},{9,8},{10,11... | collective-permute-start | bytes 786440 | tf_op jit(solution)/shard_map/ppermute | solution.py:471
  17.5 18.5 %collective-permute-start.2 = (f32[2,128,128]{2,1,0:T(8,128)S(1)}, f32[2,128,128]{2,1,0:T(8,128)S(1)}, u32[]{:S(2)}, u32[]{:S(2)}) collective-permute-start(f32[2,128,128]{2,1,0:T(8,128)S(1)} %pad_maximum_fusion), channel_id=1, source_target_pairs={{0,2},{1,3},{2,0},{3,1},{4,6},{5,7},{6,4},{7,5},{8,10},{9,11},{10,... | collective-permute-start | bytes 393224 | tf_op jit(solution)/shard_map/ppermute | solution.py:471
  19.1 17.0 %collective-permute-start.3 = (f32[2,128,128]{2,1,0:T(8,128)S(1)}, f32[2,128,128]{2,1,0:T(8,128)S(1)}, u32[]{:S(2)}, u32[]{:S(2)}) collective-permute-start(f32[2,128,128]{2,1,0:T(8,128)S(1)} %pad_maximum_fusion.1), channel_id=1, source_target_pairs={{0,4},{1,5},{2,6},{3,7},{4,0},{5,1},{6,2},{7,3},{8,12},{9,13},{10,... | collective-permute-start | bytes 393224 | tf_op jit(solution)/shard_map/ppermute | solution.py:471
  20.6 15.5 %collective-permute-start.4 = (f32[2,128,128]{2,1,0:T(8,128)S(1)}, f32[2,128,128]{2,1,0:T(8,128)S(1)}, u32[]{:S(2)}, u32[]{:S(2)}) collective-permute-start(f32[2,128,128]{2,1,0:T(8,128)S(1)} %pad_maximum_fusion.2), channel_id=1, source_target_pairs={{0,6},{1,7},{2,4},{3,5},{4,2},{5,3},{6,0},{7,1},{8,14},{9,15},{10,... | collective-permute-start | bytes 393224 | tf_op jit(solution)/shard_map/ppermute | solution.py:471
  33.9 4.8 %collective-permute-start = (bf16[128,128]{1,0:T(8,128)(2,1)S(1)}, bf16[128,128]{1,0:T(8,128)(2,1)S(1)}, u32[]{:S(2)}, u32[]{:S(2)}) collective-permute-start(bf16[128,128]{1,0:T(8,128)(2,1)S(1)} %get-tuple-element.22), channel_id=1, source_target_pairs={{0,8},{1,9},{2,10},{3,11},{4,12},{5,13},{6,14},{7,15},{8,0},{9,1},... | collective-permute-start | bytes 98312 | tf_op jit(solution)/shard_map/ppermute | solution.py:423
  40.8 4.9 %collective-permute-start.5 = (bf16[128,128]{1,0:T(8,128)(2,1)S(1)}, bf16[128,128]{1,0:T(8,128)(2,1)S(1)}, u32[]{:S(2)}, u32[]{:S(2)}) collective-permute-start(bf16[128,128]{1,0:T(8,128)(2,1)S(1)} %get-tuple-element.32), channel_id=1, source_target_pairs={{0,8},{1,9},{2,10},{3,11},{4,12},{5,13},{6,14},{7,15},{8,0},{9,1},... | collective-permute-start | bytes 98312 | tf_op jit(solution)/shard_map/ppermute | solution.py:423
  47.0 25.5 %all-to-all-start.1 = ((bf16[16,192,128]{2,1,0:T(8,128)(2,1)}), bf16[16,192,128]{2,1,0:T(8,128)(2,1)S(1)}, u32[]{:S(2)}, u32[]{:S(2)}) async-start(bf16[16,192,128]{2,1,0:T(8,128)(2,1)} %shard_map.83), calls=%async_computation.1 | async-start | bytes 1572864 | tf_op jit(solution)/shard_map/all_to_all | solution.py:457
  51.3 1.4 %collective-permute-start.6 = (bf16[4,128,128]{2,1,0:T(8,128)(2,1)S(1)}, bf16[4,128,128]{2,1,0:T(8,128)(2,1)S(1)}, u32[]{:S(2)}, u32[]{:S(2)}) collective-permute-start(bf16[4,128,128]{2,1,0:T(8,128)(2,1)S(1)} %slice.65), channel_id=1, source_target_pairs={{0,1},{1,0},{2,3},{3,2},{4,5},{5,4},{6,7},{7,6},{8,9},{9,8},{10,11... | collective-permute-start | bytes 393224 | tf_op jit(solution)/shard_map/ppermute | solution.py:471
  52.8 15.9 %collective-permute-start.8 = (bf16[2,128,128]{2,1,0:T(8,128)(2,1)S(1)}, bf16[2,128,128]{2,1,0:T(8,128)(2,1)S(1)}, u32[]{:S(2)}, u32[]{:S(2)}) collective-permute-start(bf16[2,128,128]{2,1,0:T(8,128)(2,1)S(1)} %pad_maximum_fusion.4), channel_id=1, source_target_pairs={{0,4},{1,5},{2,6},{3,7},{4,0},{5,1},{6,2},{7,3},{8,12},{9,13},{10,... | collective-permute-start | bytes 196616 | tf_op jit(solution)/shard_map/ppermute | solution.py:471
  54.3 5.2 %collective-permute-start.9 = (bf16[2,128,128]{2,1,0:T(8,128)(2,1)S(1)}, bf16[2,128,128]{2,1,0:T(8,128)(2,1)S(1)}, u32[]{:S(2)}, u32[]{:S(2)}) collective-permute-start(bf16[2,128,128]{2,1,0:T(8,128)(2,1)S(1)} %pad_maximum_fusion.5), channel_id=1, source_target_pairs={{0,2},{1,3},{2,0},{3,1},{4,6},{5,7},{6,4},{7,5},{8,10},{9,11},{10,... | collective-permute-start | bytes 196616 | tf_op jit(solution)/shard_map/ppermute | solution.py:471
  55.8 15.2 %collective-permute-start.7 = (bf16[2,128,128]{2,1,0:T(8,128)(2,1)S(1)}, bf16[2,128,128]{2,1,0:T(8,128)(2,1)S(1)}, u32[]{:S(2)}, u32[]{:S(2)}) collective-permute-start(bf16[2,128,128]{2,1,0:T(8,128)(2,1)S(1)} %pad_maximum_fusion.3), channel_id=1, source_target_pairs={{0,6},{1,7},{2,4},{3,5},{4,2},{5,3},{6,0},{7,1},{8,14},{9,15},{10,... | collective-permute-start | bytes 196616 | tf_op jit(solution)/shard_map/ppermute | solution.py:471

commit v4 on v3

--- a/solution.py
+++ b/solution.py
@@ -17,6 +17,7 @@
 VMEM = pl.BlockSpec(memory_space=pltpu.VMEM)
 SMEM = pl.BlockSpec(memory_space=pltpu.SMEM)
 PARAMS = pltpu.CompilerParams(vmem_limit_bytes=24 * 1024 * 1024)
+WHOLE = pltpu.CompilerParams(vmem_limit_bytes=60 * 1024 * 1024)
 ANY = pl.BlockSpec(memory_space=pl.ANY)
 
 
@@ -55,22 +56,33 @@
     )(*ins)
 
 
-def pack_kernel(heads, segments, rows_ref, decay_ref, starts_ref, out_ref):
+def pack_kernel(heads, segments, rows_ref, decay_ref, starts_ref, out_ref, decay, flags, sems):
     per = rows_ref.shape[0] // segments
     inner = heads * LANES
-    decay_rows = decay_ref[...].astype(f32)
-    flags = starts_ref[...].astype(f32)
+    copies = [
+        pltpu.make_async_copy(decay_ref, decay, sems.at[0]),
+        pltpu.make_async_copy(starts_ref, flags, sems.at[1]),
+    ]
+    for segment in range(segments):
+        for head in range(heads):
+            for part in range(3):
+                source = rows_ref.at[
+                    pl.ds(segment * per, per), pl.ds(part * inner + head * LANES, LANES)
+                ]
+                target = out_ref.at[segment * heads + head, pl.ds(part * per, per), :]
+                copies.append(pltpu.make_async_copy(source, target, sems.at[len(copies)]))
+    for copy in copies:
+        copy.start()
+    for copy in copies[:2]:
+        copy.wait()
     line = iota((META, LANES), 0)
     for head in range(heads):
-        meta = jnp.where(line == 0, decay_rows[head : head + 1, :], jnp.where(line == 1, flags, 0.0))
+        meta = decay[...].astype(f32)[head : head + 1, :]
+        meta = jnp.where(line == 0, meta, jnp.where(line == 1, flags[...].astype(f32), 0.0))
         for segment in range(segments):
-            to = segment * heads + head
-            for part in range(3):
-                at = part * inner + head * LANES
-                out_ref[to, part * per : (part + 1) * per, :] = rows_ref[
-                    segment * per : (segment + 1) * per, at : at + LANES
-                ]
-            out_ref[to, 3 * per :, :] = meta.astype(bf16)
+            out_ref[segment * heads + head, 3 * per :, :] = meta.astype(bf16)
+    for copy in copies[2:]:
+        copy.wait()
 
 
 def pack(projected, decay_log, starts, heads, segments):
@@ -78,14 +90,18 @@
     per = rows // segments
     peers = heads * segments
     if per % 16 == 0:
-        return call(
+        return pl.pallas_call(
             functools.partial(pack_kernel, heads, segments),
-            jax.ShapeDtypeStruct((peers, 3 * per + META, LANES), bf16),
-            (projected, decay_log.T, starts.reshape(1, rows)),
-            moved=4 * projected.size,
-            in_specs=[VMEM] * 3,
+            out_shape=jax.ShapeDtypeStruct((peers, 3 * per + META, LANES), bf16),
+            in_specs=[ANY] * 3,
             out_specs=VMEM,
-        )
+            scratch_shapes=[
+                pltpu.VMEM((heads, rows), bf16),
+                pltpu.VMEM((1, rows), jnp.int32),
+                pltpu.SemaphoreType.DMA((3 * peers + 2,)),
+            ],
+            compiler_params=WHOLE,
+        )(projected, decay_log.T, starts.reshape(1, rows))
     body = projected.reshape(segments, per, 3, heads, LANES).transpose(0, 3, 2, 1, 4)
     body = body.reshape(peers, 3 * per, LANES)
     flags = jnp.broadcast_to(starts.astype(bf16)[None, None, :], (heads, 1, rows))
@@ -235,80 +251,77 @@
     return ref[:, at : at + 16, :].reshape(CHUNK, LANES)
 
 
-class Terms:
-    def __init__(self, heads, chunks, meta_ref, destination_ref):
-        self.meta_ref = meta_ref
-        self.peers = meta_ref.shape[0]
-        self.per = CHUNK // self.peers
-        self.first_row = lax.axis_index("seq") // heads * self.per * chunks
-        self.first_block = lax.axis_index("seq") // heads * heads
-        self.turns = turns_of(destination_ref, self.peers)
-        lines = self.peers * META
-        meta = meta_ref[:, -META:, :].astype(f32).reshape(lines, LANES).astype(bf16)
-        row = iota((CHUNK, lines), 0)
-        pick = jnp.where(iota((CHUNK, lines), 1) == row // self.per * META, 1.0, 0.0)
-        self.decays = dot(pick.astype(bf16), meta)
-
-    def of(self, chunk):
-        group = CHUNK // LANES
-        chosen, column, line = places(
-            self.turns, self.peers, self.first_row + chunk * self.per, self.per, CHUNK
-        )
-        ones = jnp.ones((LANES, LANES), bf16)
-        decay = dot(jnp.where(chosen, self.decays, 0.0).astype(bf16), ones).astype(bf16)
+def plan_kernel(heads, chunks, peers, destination_ref, order_ref, reached_ref, chosen_ref):
+    per = CHUNK // peers
+    turns = turns_of(destination_ref, peers)
+    spot = iota((CHUNK, CHUNK), 1).astype(f32)
+    for chunk in range(chunks):
+        first = (lax.div(lax.axis_index("seq"), heads) * chunks + chunk) * per
+        chosen, column, line = places(turns, peers, first, per, CHUNK)
         column = wide(column)
-        order = line[0:1, :] <= column
-        running = dot(jnp.where(order, 1.0, 0.0).astype(bf16), decay)
+        order_ref[chunk] = jnp.where(line[0:1, :] <= column, 1.0, 0.0).astype(bf16)
+        reached_ref[chunk] = jnp.where(spot <= column, 1.0, 0.0).astype(bf16)
+        chosen_ref[chunk] = jnp.where(chosen, 1.0, 0.0).astype(bf16)
+
+
+def state_kernel(
+    heads, chunks, rows_ref, meta_ref, order_ref, reached_ref, chosen_ref,
+    last_ref, keep_ref, running_ref, count_ref, leave_ref,
+):
+    peers = meta_ref.shape[0]
+    group = CHUNK // LANES
+    first_block = lax.div(lax.axis_index("seq"), heads) * heads
+    lines = peers * META
+    meta = meta_ref[:, -META:, :].astype(f32).reshape(lines, LANES).astype(bf16)
+    row = iota((CHUNK, lines), 0)
+    pick = iota((CHUNK, lines), 1) == lax.div(row, CHUNK // peers) * META
+    decays = dot(jnp.where(pick, 1.0, 0.0).astype(bf16), meta).astype(bf16)
+    ones = jnp.ones((LANES, LANES), bf16)
+    state = jnp.zeros((LANES, LANES), f32)
+    before = jnp.ones((1, LANES), f32)
+    line = iota((8, LANES), 0)
+    for chunk in range(chunks):
+        decay = dot(decays * chosen_ref[chunk], ones).astype(bf16)
+        running = dot(order_ref[chunk], decay)
         flags = [
-            self.meta_ref[self.first_block + chunk * group + i, -META:, :].astype(f32)[1:2, :]
+            meta_ref[first_block + chunk * group + i, -META:, :].astype(f32)[1:2, :]
             for i in range(group)
         ]
         flags = jnp.broadcast_to(jnp.concatenate(flags, axis=1), (LANES, CHUNK)).astype(bf16)
-        reached = iota((CHUNK, CHUNK), 1).astype(f32) <= column
-        count = dot_nt(jnp.where(reached, 1.0, 0.0).astype(bf16), flags)
+        count = dot_nt(reached_ref[chunk], flags)
         last_run = jnp.min(running, axis=0, keepdims=True)
         last_count = jnp.max(count, axis=0, keepdims=True)
         leave = jnp.exp(jnp.minimum(last_run - running, 0.0))
         leave = jnp.where(count == last_count, leave, 0.0)
         total = jnp.where(last_count == 0.0, jnp.exp(last_run), 0.0)
-        return order, running, count, leave, total
-
-
-def state_kernel(heads, chunks, rows_ref, meta_ref, destination_ref, last_ref, keep_ref, gain_ref):
-    terms = Terms(heads, chunks, meta_ref, destination_ref)
-    state = jnp.zeros((LANES, LANES), f32)
-    before = jnp.ones((1, LANES), f32)
-    line = iota((8, LANES), 0)
-    for chunk in range(chunks):
-        _, _, _, leave, total = terms.of(chunk)
         key, value = (part_rows(rows_ref, part, chunk) for part in (1, 2))
         high, low = halves(key.astype(f32) * leave)
         keep_ref[chunk, 0:LANES, :] = state
         keep_ref[chunk, LANES:, :] = jnp.where(line == 0, before, total)
         state = total * state + dot_tn(high, value) + dot_tn(low, value)
         before = total * before
+        running_ref[chunk] = running
+        count_ref[chunk] = count
+        leave_ref[chunk] = leave
     last_ref[...] = state.astype(bf16)
-    gain_ref[...] = jnp.broadcast_to(before, (8, LANES))
 
 
 def inner_kernel(
-    heads, chunks, rows_ref, meta_ref, destination_ref, mix_ref, weights_ref, inner_ref, ends_ref
+    chunks, rows_ref, order_ref, running_ref, count_ref, mix_ref, weights_ref, inner_ref, enter_ref
 ):
-    terms = Terms(heads, chunks, meta_ref, destination_ref)
     lane = iota((CHUNK, LANES), 1)
     for chunk in range(chunks):
-        order, running, count, leave, _ = terms.of(chunk)
+        running, count = running_ref[chunk], count_ref[chunk]
         turned = jnp.where(lane == 0, running, count).T
-        same = order & (wide(count) == turned[1:2, :])
+        same = (order_ref[chunk].astype(f32) > 0.5) & (wide(count) == turned[1:2, :])
         gap = jnp.minimum(wide(running) - turned[0:1, :], 0.0)
         mix = jnp.where(same, jnp.exp(gap), 0.0)
-        enter = jnp.where(count == 0.0, jnp.exp(running), 0.0)
         query, key, value = (part_rows(rows_ref, part, chunk) for part in range(3))
         weights = (dot_nt(query, key) * mix).astype(bf16)
         mix_ref[chunk] = mix
         weights_ref[chunk] = weights
         inner_ref[chunk] = dot(weights, value)
-        ends_ref[chunk] = jnp.where(lane == 0, enter, leave)
+        enter_ref[chunk] = jnp.where(count == 0.0, jnp.exp(running), 0.0)
 
 
 def arriving(came_ref, heads, step):
@@ -324,7 +337,7 @@
 
 
 def output_kernel(
-    heads, chunks, runs, rows_ref, inner_ref, ends_ref, keep_ref, came_ref, *refs
+    heads, chunks, runs, rows_ref, inner_ref, enter_ref, keep_ref, came_ref, *refs
 ):
     given, (grad_ref, block_ref, back_ref, last_ref, normal_ref, sems) = refs[:-6], refs[-6:]
     mine = lax.rem(lax.axis_index("seq"), heads)
@@ -347,7 +360,7 @@
     normed_rows = []
     for chunk in range(chunks):
         query = part_rows(rows_ref, 0, chunk)
-        enter = ends_ref[chunk][:, 0:1]
+        enter = enter_ref[chunk]
         (high, low), _ = entering(keep_ref, chunk, came)
         output = inner_ref[chunk] + enter * (dot(query, high) + dot(query, low))
         scale = lax.rsqrt(jnp.mean(output * output, axis=1, keepdims=True) + norm_eps)
@@ -363,7 +376,7 @@
     for chunk in reversed(range(chunks)):
         normed, scale = normed_rows[chunk]
         query = part_rows(rows_ref, 0, chunk)
-        enter = ends_ref[chunk][:, 0:1]
+        enter = enter_ref[chunk]
         normal = jnp.concatenate(
             [
                 normal_ref[chunk * group + i].reshape(runs, 1, CHUNK // (runs * group), LANES)
@@ -385,7 +398,7 @@
 
 
 def local_kernel(
-    heads, chunks, rows_ref, mix_ref, weights_ref, ends_ref, keep_ref, came_ref, grad_ref, query_ref, part_ref
+    heads, chunks, rows_ref, mix_ref, weights_ref, enter_ref, keep_ref, came_ref, grad_ref, query_ref, part_ref
 ):
     came = arriving(came_ref, heads, 1)
     for chunk in range(chunks):
@@ -394,7 +407,7 @@
         (high, low), _ = entering(keep_ref, chunk, came)
         grad_mix = (dot_nt(grad, value) * mix_ref[chunk]).astype(bf16)
         grad_query = dot_nt(grad, high) + dot_nt(grad, low)
-        grad_query = dot(grad_mix, key) + ends_ref[chunk][:, 0:1] * grad_query
+        grad_query = dot(grad_mix, key) + enter_ref[chunk] * grad_query
         query_ref[:, chunk * 16 : (chunk + 1) * 16, :] = (
             grad_query.astype(bf16).reshape(16, 16, LANES)
         )
@@ -402,13 +415,13 @@
         part_ref[1, chunk] = dot_tn(weights_ref[chunk], grad)
 
 
-def final_kernel(heads, chunks, rows_ref, ends_ref, query_ref, part_ref, back_ref, came_ref, out_ref):
+def final_kernel(heads, chunks, rows_ref, leave_ref, query_ref, part_ref, back_ref, came_ref, out_ref):
     per = chunks * 16
     came = arriving(came_ref, heads, -1)
     out_ref[:, 0:per, :] = query_ref[...]
     for chunk in range(chunks):
         key, value = (part_rows(rows_ref, part, chunk) for part in (1, 2))
-        leave = ends_ref[chunk][:, 1:2]
+        leave = leave_ref[chunk]
         (high, low), _ = entering(back_ref, chunk, came)
         grad_key = part_ref[0, chunk] + leave * (dot_nt(value, high) + dot_nt(value, low))
         grad_value = part_ref[1, chunk] + leave * (dot(key, high) + dot(key, low))
@@ -502,23 +515,37 @@
     states = (chunks, LANES + 8, LANES)
     low = (16, chunks * 16, LANES)
     unit = 2 * chunks * CHUNK * LANES
-    last, keep, gain = call(
+    order, reached, chosen = call(
+        functools.partial(plan_kernel, heads, chunks, peers),
+        (shape(*square, dtype=bf16), shape(*square, dtype=bf16), shape(*tall, dtype=bf16)),
+        (place,),
+        flops=unit * 256,
+        moved=4 * chunks * CHUNK * CHUNK,
+        in_specs=[VMEM],
+        out_specs=[VMEM] * 3,
+    )
+    last, keep, running, count, leave = call(
         functools.partial(state_kernel, heads, chunks),
-        (shape(LANES, LANES, dtype=bf16), shape(*states), shape(8, LANES)),
-        (arrived, meta, place),
+        (
+            shape(LANES, LANES, dtype=bf16), shape(*states), shape(*tall), shape(*tall),
+            shape(*tall),
+        ),
+        (arrived, meta, order, reached, chosen),
         flops=unit * 512,
         moved=2 * arrived.size,
-        in_specs=[VMEM] * 3,
-        out_specs=[VMEM] * 3,
-    )
+        in_specs=[VMEM] * 5,
+        out_specs=[VMEM] * 5,
+    )
+    gain = keep[-1, LANES : LANES + 1] * keep[-1, LANES + 1 : LANES + 2]
+    gain = jnp.broadcast_to(gain, (8, LANES))
     came = carried(last, gain, segments, heads, 1)
-    mix, weights, inner, ends = call(
-        functools.partial(inner_kernel, heads, chunks),
+    mix, weights, inner, enter = call(
+        functools.partial(inner_kernel, chunks),
         (shape(*square), shape(*square, dtype=bf16), shape(*tall), shape(*tall)),
-        (arrived, meta, place),
+        (arrived, order, running, count),
         flops=unit * 1024,
         moved=2 * arrived.size + 8 * chunks * CHUNK * CHUNK,
-        in_specs=[VMEM] * 3,
+        in_specs=[VMEM] * 4,
         out_specs=[VMEM] * 4,
     )
     grad, normed, back, last = call(
@@ -527,7 +554,7 @@
             shape(*tall, dtype=bf16), shape(heads, rows, LANES, dtype=bf16), shape(*states),
             shape(LANES, LANES, dtype=bf16),
         ),
-        (arrived, inner, ends, keep, came, *normal),
+        (arrived, inner, enter, keep, came, *normal),
         flops=unit * 1024,
         moved=2 * arrived.size + 8 * chunks * CHUNK * LANES,
         in_specs=[VMEM] * 5 + [ANY] * len(normal),
@@ -541,7 +568,7 @@
     grad_query, part = call(
         functools.partial(local_kernel, heads, chunks),
         (shape(*low, dtype=bf16), shape(2, *tall)),
-        (arrived, mix, weights, ends, keep, came, grad),
+        (arrived, mix, weights, enter, keep, came, grad),
         flops=unit * 1024,
         moved=2 * arrived.size + 8 * chunks * CHUNK * CHUNK,
         in_specs=[VMEM] * 7,
@@ -550,7 +577,7 @@
     grads = call(
         functools.partial(final_kernel, heads, chunks),
         shape(16, 3 * chunks * 16, LANES, dtype=bf16),
-        (arrived, ends, grad_query, part, back, came_back),
+        (arrived, leave, grad_query, part, back, came_back),
         flops=unit * 512,
         moved=4 * arrived.size,
         in_specs=[VMEM] * 6,

time: 74 us -> 71.9 us (0.972)
  local copies, waits for them, and re-layouts: 6.41 us -> 3.94 us
    pallas_call x8, Pallas kernels: 13.2 us -> 10.4 us  [call(): pl.pallas_call(body, out_shape=outs, compiler_params=PARAMS, cost_estimat...]
    unnamed x14 -> x6, local copies, waits for them, and re-layouts: 6.34 us -> 3.88 us
    pallas_call x0 -> x1, Pallas kernels: none -> 2.44 us  [pack(): pl.pallas_call(functools.partial(pack_kernel, heads, segments), out_shape...]
    ppermute x2, waiting for transfers between devices: 5.71 us -> 7.4 us  [carried(): return lax.ppermute(last, 'seq', pairs)]
    all_to_all x2, waiting for transfers between devices: 9.98 us -> 8.88 us  [exchange(): return lax.all_to_all(value, 'seq', split_axis=0, concat_axis=0, tiled=True)]
  transfers between devices with their start and end apart: 12 -> 12, of which waited for: 8 -> 8; matrix products, arithmetic and copies ran while one was open for 0% -> 1% of each run, Pallas kernels for 18% -> 17%
where the time goes in v4:
time: 71.9 us; the launch traced here: 71.5 us
  waiting for transfers between devices  29 us (40%)
  Pallas kernels  18.7 us (26%)
  starting transfers between devices  18.4 us (26%)
  local copies, waits for them, and re-layouts  3.94 us (5%)
  between operations  0.78 us (1%)
    ppermute x8, waiting for transfers between devices, swap(): return lax.ppermute(value, 'seq', [(i, i ^ step) for i in range(peers)])  12.7 us
    all_to_all x2, starting transfers between devices, exchange(): return lax.all_to_all(value, 'seq', split_axis=0, concat_axis=0, tiled=True)  10.5 us
    pallas_call x8, Pallas kernels, call(): pl.pallas_call(body, out_shape=outs, compiler_params=PARAMS, cost_estimat...  10.4 us
    all_to_all x2, waiting for transfers between devices, exchange(): return lax.all_to_all(value, 'seq', split_axis=0, concat_axis=0, tiled=True)  8.88 us
    ppermute x8, starting transfers between devices, swap(): return lax.ppermute(value, 'seq', [(i, i ^ step) for i in range(peers)])  7.72 us
    ppermute x2, waiting for transfers between devices, carried(): return lax.ppermute(last, 'seq', pairs)  7.4 us
    pallas_call x4, Pallas kernels, grad_weight_of(): pl.pallas_call(body, out_shape=total, grid_spec=pltpu.PrefetchScalarGridS...  5.84 us
    unnamed x6, local copies, waits for them, and re-layouts  3.88 us
  transfers between devices with their start and end apart: 12, of which 8 were waited for; matrix products, arithmetic and copies ran while one was open for 1% of the time, Pallas kernels for 17%

profile of v4, /device:TPU:18, one launch (start us, length us, event | category | flops | bytes accessed | tf_op | source)
XLA Modules:
  0.0 71.5 jit_solution(13494532460000926324)
XLA Ops:
  0.6 2.4 %shard_map.77 = bf16[16,200,128]{2,1,0:T(8,128)(2,1)} custom-call(bf16[128,3072]{1,0:T(8,128)(2,1)} %rows_ref.1, bf16[8,128]{1,0:T(8,128)(2,1)} %bitcast.6, s32[1,128]{1,0:T(1,128)} %bitcast.7), custom_call_target="tpu_custom_call" | custom-call | tf_op jit(solution)/shard_map/pallas_call | solution.py:93
  3.1 6.2 %all-to-all-start = ((bf16[16,200,128]{2,1,0:T(8,128)(2,1)}), bf16[16,200,128]{2,1,0:T(8,128)(2,1)S(1)}, u32[]{:S(2)}, u32[]{:S(2)}) async-start(bf16[16,200,128]{2,1,0:T(8,128)(2,1)} %shard_map.77), calls=%async_computation | async-start | bytes 1638400 | tf_op jit(solution)/shard_map/all_to_all | solution.py:470
  9.3 2.2 %copy-done = bf16[1024,2048]{1,0:T(8,128)(2,1)S(1)} copy-done((bf16[1024,2048]{1,0:T(8,128)(2,1)S(1)}, bf16[1024,2048]{1,0:T(8,128)(2,1)}, u32[]{:S(2)}) %copy-start) | copy-done | bytes 4194328
  11.5 1.0 %copy-done.1 = bf16[128,2048]{1,0:T(8,128)(2,1)S(1)} copy-done((bf16[128,2048]{1,0:T(8,128)(2,1)S(1)}, bf16[128,2048]{1,0:T(8,128)(2,1)}, u32[]{:S(2)}) %copy-start.1) | copy-done | bytes 524312
  12.5 0.7 copy-done.2
  13.2 1.5 %shard_map.81 = (f32[4,128,128]{2,1,0:T(8,128)S(1)}, f32[4,128,128]{2,1,0:T(8,128)S(1)}, bf16[128,2048]{1,0:T(8,128)(2,1)S(1)}) custom-call(bf16[128,2048]{1,0:T(8,128)(2,1)S(1)} %copy-done.1, s32[1,128]{1,0:T(1,128)S(1)} %bitcast.4, bf16[1024,2048]{1,0:T(8,128)(2,1)S(1)} %copy-done), custom_call_target="tpu_custom_call" | custom-call | flops 536870912 | bytes 5242880 | tf_op jit(solution)/shard_map/pallas_call | solution.py:50
  14.9 1.4 %collective-permute-done.1 = f32[4,128,128]{2,1,0:T(8,128)S(1)} collective-permute-done((f32[4,128,128]{2,1,0:T(8,128)S(1)}, f32[4,128,128]{2,1,0:T(8,128)S(1)}, u32[]{:S(2)}, u32[]{:S(2)}) %collective-permute-start.1) | collective-permute-done | bytes 262176 | tf_op jit(solution)/shard_map/ppermute | solution.py:484
  16.3 1.5 %collective-permute-start.2 = (f32[2,128,128]{2,1,0:T(8,128)S(1)}, f32[2,128,128]{2,1,0:T(8,128)S(1)}, u32[]{:S(2)}, u32[]{:S(2)}) collective-permute-start(f32[2,128,128]{2,1,0:T(8,128)S(1)} %pad_maximum_fusion), channel_id=1, source_target_pairs={{0,2},{1,3},{2,0},{3,1},{4,6},{5,7},{6,4},{7,5},{8,10},{9,11},{10,... | collective-permute-start | bytes 393224 | tf_op jit(solution)/shard_map/ppermute | solution.py:484
  17.9 1.5 %collective-permute-start.3 = (f32[2,128,128]{2,1,0:T(8,128)S(1)}, f32[2,128,128]{2,1,0:T(8,128)S(1)}, u32[]{:S(2)}, u32[]{:S(2)}) collective-permute-start(f32[2,128,128]{2,1,0:T(8,128)S(1)} %pad_maximum_fusion.1), channel_id=1, source_target_pairs={{0,4},{1,5},{2,6},{3,7},{4,0},{5,1},{6,2},{7,3},{8,12},{9,13},{10,... | collective-permute-start | bytes 393224 | tf_op jit(solution)/shard_map/ppermute | solution.py:484
  19.4 0.7 pad_maximum_fusion.2
  20.1 0.6 collective-permute-start.4
  21.2 8.9 %all-to-all-done.rows_ref.meta_ref = bf16[16,200,128]{2,1,0:T(8,128)(2,1)S(1)} async-done(((bf16[16,200,128]{2,1,0:T(8,128)(2,1)}), bf16[16,200,128]{2,1,0:T(8,128)(2,1)S(1)}, u32[]{:S(2)}, u32[]{:S(2)}) %all-to-all-start) | async-done | bytes 819232 | tf_op jit(solution)/shard_map/all_to_all | solution.py:470
  30.0 2.1 %shard_map.79 = (bf16[128,128]{1,0:T(8,128)(2,1)S(1)}, f32[4,136,128]{2,1,0:T(8,128)S(1)}, f32[4,256,128]{2,1,0:T(8,128)S(1)}, f32[4,256,128]{2,1,0:T(8,128)S(1)}, f32[4,256,128]{2,1,0:T(8,128)S(1)}) custom-call(bf16[16,200,128]{2,1,0:T(8,128)(2,1)S(1)} %all-to-all-done.rows_ref.meta_ref, bf16[16,200,128]{2,1,0:T(8,128)(2,1)S(1)} %all-to-all-done.rows_ref.meta_ref, ...), custom_call_target="tpu_custom_call" | custom-call | flops 134217728 | bytes 819200 | tf_op jit(solution)/shard_map/pallas_call | solution.py:50
  32.3 0.8 %shard_map.80 = (f32[4,256,256]{2,1,0:T(8,128)S(1)}, bf16[4,256,256]{2,1,0:T(8,128)(2,1)S(1)}, f32[4,256,128]{2,1,0:T(8,128)S(1)}, f32[4,256,128]{2,1,0:T(8,128)S(1)}) custom-call(bf16[16,200,128]{2,1,0:T(8,128)(2,1)S(1)} %all-to-all-done.rows_ref.meta_ref, bf16[4,256,256]{2,1,0:T(8,128)(2,1)S(1)} %get-tuple-element.25.order_ref, ...), custom_call_target="tpu_custom_call" | custom-call | flops 268435456 | bytes 2916352 | tf_op jit(solution)/shard_map/pallas_call | solution.py:50
  33.1 4.0 %collective-permute-done.came_ref = bf16[128,128]{1,0:T(8,128)(2,1)S(1)} collective-permute-done((bf16[128,128]{1,0:T(8,128)(2,1)S(1)}, bf16[128,128]{1,0:T(8,128)(2,1)S(1)}, u32[]{:S(2)}, u32[]{:S(2)}) %collective-permute-start) | collective-permute-done | bytes 32800 | tf_op jit(solution)/shard_map/ppermute | solution.py:436
  37.1 1.7 %shard_map.82 = (bf16[4,256,128]{2,1,0:T(8,128)(2,1)S(1)}, bf16[8,128,128]{2,1,0:T(8,128)(2,1)S(1)}, f32[4,136,128]{2,1,0:T(8,128)S(1)}, bf16[128,128]{1,0:T(8,128)(2,1)S(1)}) custom-call(bf16[16,200,128]{2,1,0:T(8,128)(2,1)S(1)} %all-to-all-done.rows_ref.meta_ref, f32[4,256,128]{2,1,0:T(8,128)S(1)} %get-tuple-element.30.inner_ref, ...), custom_call_target="tpu_custom_call" | custom-call | flops 268435456 | bytes 1867776 | tf_op jit(solution)/shard_map/pallas_call | solution.py:50
  38.8 1.4 %shard_map.83 = (bf16[16,64,128]{2,1,0:T(8,128)(2,1)S(1)}, f32[2,4,256,128]{3,2,1,0:T(8,128)S(1)}) custom-call(bf16[16,200,128]{2,1,0:T(8,128)(2,1)S(1)} %all-to-all-done.rows_ref.meta_ref, f32[4,256,256]{2,1,0:T(8,128)S(1)} %get-tuple-element.38.mix_ref, bf16[4,256,256]{2,1,0:T(8,128)(2,1)S(1)} %get-tuple-element.39.weights_ref, ...), custom_call_target="tpu_custom_call" | custom-call | flops 268435456 | bytes 2916352 | tf_op jit(solution)/shard_map/pallas_call | solution.py:50
  40.2 3.4 %collective-permute-done.5.came_ref = bf16[128,128]{1,0:T(8,128)(2,1)S(1)} collective-permute-done((bf16[128,128]{1,0:T(8,128)(2,1)S(1)}, bf16[128,128]{1,0:T(8,128)(2,1)S(1)}, u32[]{:S(2)}, u32[]{:S(2)}) %collective-permute-start.5) | collective-permute-done | bytes 32800 | tf_op jit(solution)/shard_map/ppermute | solution.py:436
  43.6 1.3 %shard_map.84 = bf16[16,192,128]{2,1,0:T(8,128)(2,1)} custom-call(bf16[16,200,128]{2,1,0:T(8,128)(2,1)S(1)} %all-to-all-done.rows_ref.meta_ref, f32[4,256,128]{2,1,0:T(8,128)S(1)} %get-tuple-element.37.leave_ref, bf16[16,64,128]{2,1,0:T(8,128)(2,1)S(1)} %get-tuple-element.41.query_ref, f32[2,4,256,128]{3,2,1,0:T(8,128)S(1)} %get-tuple-element.42.part_ref, ...), custom_call_target="tpu_custom_call" | custom-call | flops 134217728 | bytes 1638400 | tf_op jit(solution)/shard_map/pallas_call | solution.py:50
  44.9 4.3 %all-to-all-start.1 = ((bf16[16,192,128]{2,1,0:T(8,128)(2,1)}), bf16[16,192,128]{2,1,0:T(8,128)(2,1)S(1)}, u32[]{:S(2)}, u32[]{:S(2)}) async-start(bf16[16,192,128]{2,1,0:T(8,128)(2,1)} %shard_map.84), calls=%async_computation.1 | async-start | bytes 1572864 | tf_op jit(solution)/shard_map/all_to_all | solution.py:470
  49.5 1.2 %collective-permute-done.6 = bf16[4,128,128]{2,1,0:T(8,128)(2,1)S(1)} collective-permute-done((bf16[4,128,128]{2,1,0:T(8,128)(2,1)S(1)}, bf16[4,128,128]{2,1,0:T(8,128)(2,1)S(1)}, u32[]{:S(2)}, u32[]{:S(2)}) %collective-permute-start.6) | collective-permute-done | bytes 131104 | tf_op jit(solution)/shard_map/ppermute | solution.py:484
  50.7 1.5 %collective-permute-start.8 = (bf16[2,128,128]{2,1,0:T(8,128)(2,1)S(1)}, bf16[2,128,128]{2,1,0:T(8,128)(2,1)S(1)}, u32[]{:S(2)}, u32[]{:S(2)}) collective-permute-start(bf16[2,128,128]{2,1,0:T(8,128)(2,1)S(1)} %pad_maximum_fusion.4), channel_id=1, source_target_pairs={{0,4},{1,5},{2,6},{3,7},{4,0},{5,1},{6,2},{7,3},{8,12},{9,13},{10,... | collective-permute-start | bytes 196616 | tf_op jit(solution)/shard_map/ppermute | solution.py:484
  52.2 1.5 %collective-permute-start.9 = (bf16[2,128,128]{2,1,0:T(8,128)(2,1)S(1)}, bf16[2,128,128]{2,1,0:T(8,128)(2,1)S(1)}, u32[]{:S(2)}, u32[]{:S(2)}) collective-permute-start(bf16[2,128,128]{2,1,0:T(8,128)(2,1)S(1)} %pad_maximum_fusion.5), channel_id=1, source_target_pairs={{0,2},{1,3},{2,0},{3,1},{4,6},{5,7},{6,4},{7,5},{8,10},{9,11},{10,... | collective-permute-start | bytes 196616 | tf_op jit(solution)/shard_map/ppermute | solution.py:484
  53.7 0.6 collective-permute-start.7
  54.4 1.5 %shard_map.86.refs_2_ = bf16[1024,2048]{1,0:T(8,128)(2,1)} custom-call(s32[1]{0:T(128)} %bitcast.3.mine_ref, bf16[1,128,128]{2,1,0:T(8,128)(2,1)S(1)} %get-tuple-element.48.refs_0_, bf16[1,128,128]{2,1,0:T(8,128)(2,1)S(1)} %get-tuple-element.60.refs_1_, bf16[128,2048]{1,0:T(8,128)(2,1)S(1)} %get-tuple-element.47.refs_2_.refs_1_), custom_call_target="tpu_custom_call" | custom-call | flops 134217728 | bytes 1048576 | tf_op jit(solution)/shard_map/pallas_call | solution.py:219
  55.8 1.6 %collective-permute-done.9.refs_0_ = bf16[2,128,128]{2,1,0:T(8,128)(2,1)S(1)} collective-permute-done((bf16[2,128,128]{2,1,0:T(8,128)(2,1)S(1)}, bf16[2,128,128]{2,1,0:T(8,128)(2,1)S(1)}, u32[]{:S(2)}, u32[]{:S(2)}) %collective-permute-start.9) | collective-permute-done | bytes 65568 | tf_op jit(solution)/shard_map/ppermute | solution.py:484
  57.4 1.5 %shard_map.87.refs_2_ = bf16[1024,2048]{1,0:T(8,128)(2,1)} custom-call(s32[1]{0:T(128)} %bitcast.3.mine_ref, bf16[2,128,128]{2,1,0:T(8,128)(2,1)S(1)} %collective-permute-done.9.refs_0_, bf16[128,2048]{1,0:T(8,128)(2,1)S(1)} %get-tuple-element.47.refs_2_.refs_1_, bf16[1024,2048]{1,0:T(8,128)(2,1)} %shard_map.86.refs_2_), custom_call_target="tpu_custom_call", output_to_operand_aliasing={{}: (3, {})} | custom-call | flops 134217728 | bytes 1048576 | tf_op jit(solution)/shard_map/pallas_call | solution.py:219
  58.9 7.7 %collective-permute-done.8.refs_0_ = bf16[2,128,128]{2,1,0:T(8,128)(2,1)S(1)} collective-permute-done((bf16[2,128,128]{2,1,0:T(8,128)(2,1)S(1)}, bf16[2,128,128]{2,1,0:T(8,128)(2,1)S(1)}, u32[]{:S(2)}, u32[]{:S(2)}) %collective-permute-start.8) | collective-permute-done | bytes 65568 | tf_op jit(solution)/shard_map/ppermute | solution.py:484
  66.5 1.5 %shard_map.88.refs_2_ = bf16[1024,2048]{1,0:T(8,128)(2,1)} custom-call(s32[1]{0:T(128)} %bitcast.3.mine_ref, bf16[2,128,128]{2,1,0:T(8,128)(2,1)S(1)} %collective-permute-done.8.refs_0_, bf16[128,2048]{1,0:T(8,128)(2,1)S(1)} %get-tuple-element.47.refs_2_.refs_1_, bf16[1024,2048]{1,0:T(8,128)(2,1)} %shard_map.87.refs_2_), custom_call_target="tpu_custom_call", output_to_operand_aliasing={{}: (3, {})} | custom-call | flops 134217728 | bytes 1048576 | tf_op jit(solution)/shard_map/pallas_call | solution.py:219
  68.0 0.9 %collective-permute-done.7.refs_0_ = bf16[2,128,128]{2,1,0:T(8,128)(2,1)S(1)} collective-permute-done((bf16[2,128,128]{2,1,0:T(8,128)(2,1)S(1)}, bf16[2,128,128]{2,1,0:T(8,128)(2,1)S(1)}, u32[]{:S(2)}, u32[]{:S(2)}) %collective-permute-start.7) | collective-permute-done | bytes 65568 | tf_op jit(solution)/shard_map/ppermute | solution.py:484
  68.9 1.5 %shard_map.89 = bf16[1024,2048]{1,0:T(8,128)(2,1)} custom-call(s32[1]{0:T(128)} %bitcast.3.mine_ref, bf16[2,128,128]{2,1,0:T(8,128)(2,1)S(1)} %collective-permute-done.7.refs_0_, bf16[128,2048]{1,0:T(8,128)(2,1)S(1)} %get-tuple-element.47.refs_2_.refs_1_, bf16[1024,2048]{1,0:T(8,128)(2,1)} %shard_map.88.refs_2_), custom_call_target="tpu_custom_call", output_to_operand_aliasing={{}: (3, {})} | custom-call | flops 134217728 | bytes 1048576 | tf_op jit(solution)/shard_map/pallas_call | solution.py:219
  70.4 1.1 %shard_map.85 = bf16[128,3072]{1,0:T(8,128)(2,1)} custom-call(bf16[16,192,128]{2,1,0:T(8,128)(2,1)S(1)} %all-to-all-done.1.in_ref), custom_call_target="tpu_custom_call" | custom-call | bytes 1572864 | tf_op jit(solution)/shard_map/pallas_call | solution.py:50
  (22 shorter events, 1.2 us)
Async XLA Ops:
  3.1 26.9 %all-to-all-start = ((bf16[16,200,128]{2,1,0:T(8,128)(2,1)}), bf16[16,200,128]{2,1,0:T(8,128)(2,1)S(1)}, u32[]{:S(2)}, u32[]{:S(2)}) async-start(bf16[16,200,128]{2,1,0:T(8,128)(2,1)} %shard_map.77), calls=%async_computation | async-start | bytes 1638400 | tf_op jit(solution)/shard_map/all_to_all | solution.py:470
  9.3 2.2 %copy-start = (bf16[1024,2048]{1,0:T(8,128)(2,1)S(1)}, bf16[1024,2048]{1,0:T(8,128)(2,1)}, u32[]{:S(2)}) copy-start(bf16[1024,2048]{1,0:T(8,128)(2,1)} %weight_ref.1) | copy-start | bytes 12582916
  11.5 1.0 %copy-start.1 = (bf16[128,2048]{1,0:T(8,128)(2,1)S(1)}, bf16[128,2048]{1,0:T(8,128)(2,1)}, u32[]{:S(2)}) copy-start(bf16[128,2048]{1,0:T(8,128)(2,1)} %up_ref.1) | copy-start | bytes 1572868
  12.5 0.7 copy-start.2
  14.7 1.6 %collective-permute-start.1 = (f32[4,128,128]{2,1,0:T(8,128)S(1)}, f32[4,128,128]{2,1,0:T(8,128)S(1)}, u32[]{:S(2)}, u32[]{:S(2)}) collective-permute-start(f32[4,128,128]{2,1,0:T(8,128)S(1)} %get-tuple-element.35), channel_id=1, source_target_pairs={{0,1},{1,0},{2,3},{3,2},{4,5},{5,4},{6,7},{7,6},{8,9},{9,8},{10,11... | collective-permute-start | bytes 786440 | tf_op jit(solution)/shard_map/ppermute | solution.py:484
  16.3 16.7 %collective-permute-start.2 = (f32[2,128,128]{2,1,0:T(8,128)S(1)}, f32[2,128,128]{2,1,0:T(8,128)S(1)}, u32[]{:S(2)}, u32[]{:S(2)}) collective-permute-start(f32[2,128,128]{2,1,0:T(8,128)S(1)} %pad_maximum_fusion), channel_id=1, source_target_pairs={{0,2},{1,3},{2,0},{3,1},{4,6},{5,7},{6,4},{7,5},{8,10},{9,11},{10,... | collective-permute-start | bytes 393224 | tf_op jit(solution)/shard_map/ppermute | solution.py:484
  17.9 15.2 %collective-permute-start.3 = (f32[2,128,128]{2,1,0:T(8,128)S(1)}, f32[2,128,128]{2,1,0:T(8,128)S(1)}, u32[]{:S(2)}, u32[]{:S(2)}) collective-permute-start(f32[2,128,128]{2,1,0:T(8,128)S(1)} %pad_maximum_fusion.1), channel_id=1, source_target_pairs={{0,4},{1,5},{2,6},{3,7},{4,0},{5,1},{6,2},{7,3},{8,12},{9,13},{10,... | collective-permute-start | bytes 393224 | tf_op jit(solution)/shard_map/ppermute | solution.py:484
  20.1 13.0 %collective-permute-start.4 = (f32[2,128,128]{2,1,0:T(8,128)}, f32[2,128,128]{2,1,0:T(8,128)S(1)}, u32[]{:S(2)}, u32[]{:S(2)}) collective-permute-start(f32[2,128,128]{2,1,0:T(8,128)} %pad_maximum_fusion.2), channel_id=1, source_target_pairs={{0,6},{1,7},{2,4},{3,5},{4,2},{5,3},{6,0},{7,1},{8,14},{9,15},{10,... | collective-permute-start | bytes 393224 | tf_op jit(solution)/shard_map/ppermute | solution.py:484
  32.2 4.9 %collective-permute-start = (bf16[128,128]{1,0:T(8,128)(2,1)S(1)}, bf16[128,128]{1,0:T(8,128)(2,1)S(1)}, u32[]{:S(2)}, u32[]{:S(2)}) collective-permute-start(bf16[128,128]{1,0:T(8,128)(2,1)S(1)} %get-tuple-element.33), channel_id=1, source_target_pairs={{0,8},{1,9},{2,10},{3,11},{4,12},{5,13},{6,14},{7,15},{8,0},{9,1},... | collective-permute-start | bytes 98312 | tf_op jit(solution)/shard_map/ppermute | solution.py:436
  38.7 4.9 %collective-permute-start.5 = (bf16[128,128]{1,0:T(8,128)(2,1)S(1)}, bf16[128,128]{1,0:T(8,128)(2,1)S(1)}, u32[]{:S(2)}, u32[]{:S(2)}) collective-permute-start(bf16[128,128]{1,0:T(8,128)(2,1)S(1)} %get-tuple-element.44), channel_id=1, source_target_pairs={{0,8},{1,9},{2,10},{3,11},{4,12},{5,13},{6,14},{7,15},{8,0},{9,1},... | collective-permute-start | bytes 98312 | tf_op jit(solution)/shard_map/ppermute | solution.py:436
  44.9 25.5 %all-to-all-start.1 = ((bf16[16,192,128]{2,1,0:T(8,128)(2,1)}), bf16[16,192,128]{2,1,0:T(8,128)(2,1)S(1)}, u32[]{:S(2)}, u32[]{:S(2)}) async-start(bf16[16,192,128]{2,1,0:T(8,128)(2,1)} %shard_map.84), calls=%async_computation.1 | async-start | bytes 1572864 | tf_op jit(solution)/shard_map/all_to_all | solution.py:470
  49.2 1.4 %collective-permute-start.6 = (bf16[4,128,128]{2,1,0:T(8,128)(2,1)S(1)}, bf16[4,128,128]{2,1,0:T(8,128)(2,1)S(1)}, u32[]{:S(2)}, u32[]{:S(2)}) collective-permute-start(bf16[4,128,128]{2,1,0:T(8,128)(2,1)S(1)} %slice.65), channel_id=1, source_target_pairs={{0,1},{1,0},{2,3},{3,2},{4,5},{5,4},{6,7},{7,6},{8,9},{9,8},{10,11... | collective-permute-start | bytes 393224 | tf_op jit(solution)/shard_map/ppermute | solution.py:484
  50.7 15.9 %collective-permute-start.8 = (bf16[2,128,128]{2,1,0:T(8,128)(2,1)S(1)}, bf16[2,128,128]{2,1,0:T(8,128)(2,1)S(1)}, u32[]{:S(2)}, u32[]{:S(2)}) collective-permute-start(bf16[2,128,128]{2,1,0:T(8,128)(2,1)S(1)} %pad_maximum_fusion.4), channel_id=1, source_target_pairs={{0,4},{1,5},{2,6},{3,7},{4,0},{5,1},{6,2},{7,3},{8,12},{9,13},{10,... | collective-permute-start | bytes 196616 | tf_op jit(solution)/shard_map/ppermute | solution.py:484
  52.2 5.2 %collective-permute-start.9 = (bf16[2,128,128]{2,1,0:T(8,128)(2,1)S(1)}, bf16[2,128,128]{2,1,0:T(8,128)(2,1)S(1)}, u32[]{:S(2)}, u32[]{:S(2)}) collective-permute-start(bf16[2,128,128]{2,1,0:T(8,128)(2,1)S(1)} %pad_maximum_fusion.5), channel_id=1, source_target_pairs={{0,2},{1,3},{2,0},{3,1},{4,6},{5,7},{6,4},{7,5},{8,10},{9,11},{10,... | collective-permute-start | bytes 196616 | tf_op jit(solution)/shard_map/ppermute | solution.py:484
  53.7 15.2 %collective-permute-start.7 = (bf16[2,128,128]{2,1,0:T(8,128)(2,1)S(1)}, bf16[2,128,128]{2,1,0:T(8,128)(2,1)S(1)}, u32[]{:S(2)}, u32[]{:S(2)}) collective-permute-start(bf16[2,128,128]{2,1,0:T(8,128)(2,1)S(1)} %pad_maximum_fusion.3), channel_id=1, source_target_pairs={{0,6},{1,7},{2,4},{3,5},{4,2},{5,3},{6,0},{7,1},{8,14},{9,15},{10,... | collective-permute-start | bytes 196616 | tf_op jit(solution)/shard_map/ppermute | solution.py:484

commit v5 on v4

--- a/solution.py
+++ b/solution.py
@@ -36,6 +36,10 @@
 def halves(value):
     high = value.astype(bf16)
     return high, (value - high.astype(f32)).astype(bf16)
+
+
+def folded(value):
+    return value[:, :LANES] + value[:, LANES:]
 
 
 def wide(value):
@@ -56,32 +60,41 @@
     )(*ins)
 
 
-def pack_kernel(heads, segments, rows_ref, decay_ref, starts_ref, out_ref, decay, flags, sems):
+def pack_kernel(
+    heads, segments, rows_ref, decay_ref, starts_ref, out_ref, held, stage, decay, flags, sems, out_sems
+):
     per = rows_ref.shape[0] // segments
     inner = heads * LANES
-    copies = [
+    quarter = per // 2
+    arriving = [
         pltpu.make_async_copy(decay_ref, decay, sems.at[0]),
         pltpu.make_async_copy(starts_ref, flags, sems.at[1]),
     ]
-    for segment in range(segments):
-        for head in range(heads):
-            for part in range(3):
-                source = rows_ref.at[
-                    pl.ds(segment * per, per), pl.ds(part * inner + head * LANES, LANES)
-                ]
-                target = out_ref.at[segment * heads + head, pl.ds(part * per, per), :]
-                copies.append(pltpu.make_async_copy(source, target, sems.at[len(copies)]))
-    for copy in copies:
+    for i in range(2 * segments):
+        here = pl.ds(i * quarter, quarter)
+        arriving.append(pltpu.make_async_copy(rows_ref.at[here, :], held.at[here, :], sems.at[2 + i]))
+    for copy in arriving:
         copy.start()
-    for copy in copies[:2]:
+    for copy in arriving[:2]:
         copy.wait()
     line = iota((META, LANES), 0)
-    for head in range(heads):
-        meta = decay[...].astype(f32)[head : head + 1, :]
-        meta = jnp.where(line == 0, meta, jnp.where(line == 1, flags[...].astype(f32), 0.0))
-        for segment in range(segments):
-            out_ref[segment * heads + head, 3 * per :, :] = meta.astype(bf16)
-    for copy in copies[2:]:
+    leaving = []
+    for segment in range(segments):
+        for copy in arriving[2 + 2 * segment : 4 + 2 * segment]:
+            copy.wait()
+        for head in range(heads):
+            to = segment * heads + head
+            for part in range(3):
+                at = part * inner + head * LANES
+                stage[to, part * per : (part + 1) * per, :] = held[
+                    segment * per : (segment + 1) * per, at : at + LANES
+                ]
+            meta = decay[...].astype(f32)[head : head + 1, :]
+            meta = jnp.where(line == 0, meta, jnp.where(line == 1, flags[...].astype(f32), 0.0))
+            stage[to, 3 * per :, :] = meta.astype(bf16)
+            leaving.append(pltpu.make_async_copy(stage.at[to], out_ref.at[to], out_sems.at[to]))
+            leaving[-1].start()
+    for copy in leaving:
         copy.wait()
 
 
@@ -89,16 +102,19 @@
     rows = projected.shape[0]
     per = rows // segments
     peers = heads * segments
-    if per % 16 == 0:
+    if per % 32 == 0:
         return pl.pallas_call(
             functools.partial(pack_kernel, heads, segments),
             out_shape=jax.ShapeDtypeStruct((peers, 3 * per + META, LANES), bf16),
             in_specs=[ANY] * 3,
-            out_specs=VMEM,
+            out_specs=ANY,
             scratch_shapes=[
+                pltpu.VMEM(projected.shape, bf16),
+                pltpu.VMEM((peers, 3 * per + META, LANES), bf16),
                 pltpu.VMEM((heads, rows), bf16),
                 pltpu.VMEM((1, rows), jnp.int32),
-                pltpu.SemaphoreType.DMA((3 * peers + 2,)),
+                pltpu.SemaphoreType.DMA((2 + 2 * segments,)),
+                pltpu.SemaphoreType.DMA((peers,)),
             ],
             compiler_params=WHOLE,
         )(projected, decay_log.T, starts.reshape(1, rows))
@@ -112,28 +128,41 @@
     return jnp.concatenate([body, meta], axis=1)
 
 
-def unpack_kernel(heads, segments, in_ref, out_ref):
+def unpack_kernel(heads, segments, in_ref, out_ref, stage, sems):
     per = out_ref.shape[0] // segments
     inner = heads * LANES
-    for segment in range(segments):
+    quarter = per // 2
+    copies = []
+    for i in range(2 * segments):
+        here = slice(i * quarter, (i + 1) * quarter)
         for head in range(heads):
             for part in range(3):
                 at = part * inner + head * LANES
-                out_ref[segment * per : (segment + 1) * per, at : at + LANES] = in_ref[
-                    segment * heads + head, part * per : (part + 1) * per, :
+                first = part * per + i % 2 * quarter
+                stage[here, at : at + LANES] = in_ref[
+                    i // 2 * heads + head, first : first + quarter, :
                 ]
+        here = pl.ds(i * quarter, quarter)
+        copies.append(pltpu.make_async_copy(stage.at[here, :], out_ref.at[here, :], sems.at[i]))
+        copies[-1].start()
+    for copy in copies:
+        copy.wait()
 
 
 def unpack(arrived, rows, heads, segments):
     per = rows // segments
-    if per % 16 == 0:
+    if per % 32 == 0:
         return call(
             functools.partial(unpack_kernel, heads, segments),
             jax.ShapeDtypeStruct((rows, 3 * heads * LANES), bf16),
             (arrived,),
             moved=4 * arrived.size,
             in_specs=[VMEM],
-            out_specs=VMEM,
+            out_specs=ANY,
+            scratch_shapes=[
+                pltpu.VMEM((rows, 3 * heads * LANES), bf16),
+                pltpu.SemaphoreType.DMA((2 * segments,)),
+            ],
         )
     body = arrived.reshape(segments, heads, 3, per, LANES).transpose(0, 3, 2, 1, 4)
     return body.reshape(rows, 3 * heads * LANES)
@@ -194,53 +223,48 @@
     )
 
 
-def grad_weight_of(normed, upstream, heads, mine):
+def grad_weight_kernel(heads, at, count, *refs):
+    given, up_ref, (out_ref, stage, sems) = refs[:count], refs[count], refs[-3:]
+    mine = lax.rem(lax.axis_index("seq"), heads)
+    one, other = [ref[i] for ref in given for i in range(ref.shape[0])]
+    odd = jnp.bitwise_and(mine, 1) == 1
+    left = jnp.concatenate([jnp.where(odd, other, one), jnp.where(odd, one, other)], axis=1)
+    first = pl.multiple_of(jnp.bitwise_xor(lax.div(mine, 2), at) * 2 * LANES, 2 * LANES)
+    tile = up_ref.shape[1] // sems.shape[0]
+    copies = []
+    for i in range(sems.shape[0]):
+        here = pl.ds(i * tile, tile)
+        stage[:, here] = dot_tn(left, up_ref[:, here]).astype(bf16)
+        there = out_ref.at[pl.ds(first, 2 * LANES), here]
+        copies.append(pltpu.make_async_copy(stage.at[:, here], there, sems.at[i]))
+        copies[-1].start()
+    for copy in copies:
+        copy.wait()
+
+
+def grad_weight_of(normed, upstream):
     rows, width = upstream.shape
-    total = jax.ShapeDtypeStruct((heads * LANES, width), bf16)
-    calls = [normed[:2]] + [[pair] for pair in normed[2:]]
-    out = None
-    for at, pieces in enumerate(calls):
-        count = sum(piece.shape[0] for piece in pieces)
-
-        def body(mine_ref, *refs):
-            *piece_refs, up_ref, out_ref = refs[: len(pieces) + 1] + refs[-1:]
-            step = pl.program_id(0)
-            first = 0
-            for piece_ref in piece_refs:
-                for i in range(piece_ref.shape[0]):
-
-                    @pl.when(step == first)
-                    def _(piece_ref=piece_ref, i=i):
-                        out_ref[...] = dot_tn(piece_ref[i], up_ref[...]).astype(bf16)
-
-                    first += 1
-
-        given = [] if out is None else [out]
-        out = pl.pallas_call(
-            body,
-            out_shape=total,
-            grid_spec=pltpu.PrefetchScalarGridSpec(
-                num_scalar_prefetch=1,
-                grid=(count,),
-                in_specs=[
-                    pl.BlockSpec(piece.shape, lambda i, mine: (0, 0, 0)) for piece in pieces
-                ]
-                + [pl.BlockSpec((rows, width), lambda i, mine: (0, 0))]
-                + [ANY for _ in given],
-                out_specs=pl.BlockSpec(
-                    (LANES, width),
-                    lambda i, mine, at=at: (jnp.bitwise_xor(mine[0], 2 * at + i), 0),
-                ),
-            ),
-            input_output_aliases={len(pieces) + 2: 0} if given else {},
-            compiler_params=PARAMS,
-            cost_estimate=pl.CostEstimate(
-                flops=2 * rows * count * LANES * width,
-                bytes_accessed=2 * count * LANES * width,
-                transcendentals=0,
-            ),
-        )(mine.reshape(1), *pieces, upstream, *given)
-    return out
+    heads = sum(piece.shape[0] for piece in normed)
+    out = []
+    for at, pieces in enumerate([normed[:2]] + [[pair] for pair in normed[2:]]):
+        count = len(pieces)
+        out = [
+            call(
+                functools.partial(grad_weight_kernel, heads, at, count),
+                jax.ShapeDtypeStruct((heads * LANES, width), bf16),
+                (*pieces, upstream, *out),
+                flops=4 * rows * LANES * width,
+                moved=4 * LANES * width,
+                in_specs=[VMEM] * (count + 1) + [ANY] * len(out),
+                out_specs=ANY,
+                input_output_aliases={count + 1: 0} if out else {},
+                scratch_shapes=[
+                    pltpu.VMEM((2 * LANES, width), bf16),
+                    pltpu.SemaphoreType.DMA((4,)),
+                ],
+            )
+        ]
+    return out[0]
 
 
 def part_rows(ref, part, chunk):
@@ -298,7 +322,8 @@
         high, low = halves(key.astype(f32) * leave)
         keep_ref[chunk, 0:LANES, :] = state
         keep_ref[chunk, LANES:, :] = jnp.where(line == 0, before, total)
-        state = total * state + dot_tn(high, value) + dot_tn(low, value)
+        local = folded(dot_tn(value, jnp.concatenate([high, low], axis=1)))
+        state = total * state + local
         before = total * before
         running_ref[chunk] = running
         count_ref[chunk] = count
@@ -307,8 +332,20 @@
 
 
 def inner_kernel(
-    chunks, rows_ref, order_ref, running_ref, count_ref, mix_ref, weights_ref, inner_ref, enter_ref
+    heads, chunks, runs, rows_ref, order_ref, running_ref, count_ref, keep_ref, *refs
 ):
+    given, (mix_ref, weights_ref, inner_ref, enter_ref, normal_ref, blocks, sems) = refs[:-7], refs[-7:]
+    mine = lax.rem(lax.axis_index("seq"), heads)
+    sources = [given[0].at[0], given[1].at[0]]
+    for pair in given[2:]:
+        sources += [pair.at[0], pair.at[1]]
+    copies = [
+        pltpu.make_async_copy(source, blocks.at[jnp.bitwise_xor(mine, step)], sems.at[step])
+        for step, source in enumerate(sources)
+    ]
+    for copy in copies:
+        copy.start()
+    group = CHUNK // LANES
     lane = iota((CHUNK, LANES), 1)
     for chunk in range(chunks):
         running, count = running_ref[chunk], count_ref[chunk]
@@ -320,70 +357,49 @@
         weights = (dot_nt(query, key) * mix).astype(bf16)
         mix_ref[chunk] = mix
         weights_ref[chunk] = weights
-        inner_ref[chunk] = dot(weights, value)
-        enter_ref[chunk] = jnp.where(count == 0.0, jnp.exp(running), 0.0)
+        inner = dot(weights, value)
+        enter = jnp.where(count == 0.0, jnp.exp(running), 0.0)
+        if chunk:
+            state = jnp.concatenate(halves(keep_ref[chunk, 0:LANES, :]), axis=0)
+            inner = inner + enter * folded(dot_nt(query, state))
+        inner_ref[chunk] = inner
+        enter_ref[chunk] = enter
+    for copy in copies:
+        copy.wait()
+    for chunk in range(chunks):
+        normal_ref[chunk] = jnp.concatenate(
+            [
+                blocks[chunk * group + i].reshape(runs, 1, CHUNK // (runs * group), LANES)
+                for i in range(group)
+            ],
+            axis=1,
+        ).reshape(CHUNK, LANES)
 
 
 def arriving(came_ref, heads, step):
     segment = lax.div(lax.axis_index("seq"), heads)
     last = lax.div(lax.axis_size("seq"), heads) - 1
     end = 0 if step == 1 else last
-    return jnp.where(segment == end, 0.0, came_ref[...].astype(f32))
-
-
-def entering(keep_ref, chunk, came):
-    keep = keep_ref[chunk]
-    return halves(keep[0:LANES, :] + keep[LANES : LANES + 1, :] * came), keep[LANES + 1 : LANES + 2, :]
+    return jnp.where(segment == end, 0.0, came_ref[...].astype(f32)).astype(bf16)
 
 
 def output_kernel(
-    heads, chunks, runs, rows_ref, inner_ref, enter_ref, keep_ref, came_ref, *refs
+    heads, chunks, rows_ref, inner_ref, enter_ref, keep_ref, normal_ref, came_ref,
+    grad_ref, normed_ref, back_ref, last_ref,
 ):
-    given, (grad_ref, block_ref, back_ref, last_ref, normal_ref, sems) = refs[:-6], refs[-6:]
-    mine = lax.rem(lax.axis_index("seq"), heads)
-    sources = [given[0].at[0], given[1].at[0]]
-    for pair in given[2:]:
-        sources += [pair.at[0], pair.at[1]]
-    copies = [
-        pltpu.make_async_copy(
-            source, normal_ref.at[jnp.bitwise_xor(mine, step)], sems.at[step]
-        )
-        for step, source in enumerate(sources)
-    ]
-    for copy in copies:
-        copy.start()
-    group = CHUNK // LANES
     back = jnp.zeros((LANES, LANES), f32)
     after = jnp.ones((1, LANES), f32)
     line = iota((8, LANES), 0)
     came = arriving(came_ref, heads, 1)
-    normed_rows = []
-    for chunk in range(chunks):
+    for chunk in reversed(range(chunks)):
         query = part_rows(rows_ref, 0, chunk)
         enter = enter_ref[chunk]
-        (high, low), _ = entering(keep_ref, chunk, came)
-        output = inner_ref[chunk] + enter * (dot(query, high) + dot(query, low))
+        before = keep_ref[chunk, LANES : LANES + 1, :]
+        output = inner_ref[chunk] + before * enter * dot_nt(query, came)
         scale = lax.rsqrt(jnp.mean(output * output, axis=1, keepdims=True) + norm_eps)
         normed = output * scale
-        split = normed.reshape(runs, group, CHUNK // (runs * group), LANES)
-        for i in range(group):
-            step = jnp.bitwise_xor(mine, chunk * group + i)
-            at = jnp.bitwise_and(step, 1) * (heads // 2) + lax.div(step, 2)
-            block_ref[at] = split[:, i].reshape(LANES, LANES).astype(bf16)
-        normed_rows.append((normed, scale))
-    for copy in copies:
-        copy.wait()
-    for chunk in reversed(range(chunks)):
-        normed, scale = normed_rows[chunk]
-        query = part_rows(rows_ref, 0, chunk)
-        enter = enter_ref[chunk]
-        normal = jnp.concatenate(
-            [
-                normal_ref[chunk * group + i].reshape(runs, 1, CHUNK // (runs * group), LANES)
-                for i in range(group)
-            ],
-            axis=1,
-        ).reshape(CHUNK, LANES)
+        normed_ref[chunk] = normed.astype(bf16)
+        normal = normal_ref[chunk]
         grad = (
             (normal - normed * jnp.mean(normal * normed, axis=1, keepdims=True)) * scale
         ).astype(bf16)
@@ -392,42 +408,74 @@
         back_ref[chunk, 0:LANES, :] = back
         back_ref[chunk, LANES:, :] = jnp.where(line == 0, after, gain)
         high, low = halves(query.astype(f32) * enter)
-        back = gain * back + dot_tn(high, grad) + dot_tn(low, grad)
+        back = gain * back + folded(dot_tn(grad, jnp.concatenate([high, low], axis=1)))
         after = gain * after
     last_ref[...] = back.astype(bf16)
 
 
 def local_kernel(
-    heads, chunks, rows_ref, mix_ref, weights_ref, enter_ref, keep_ref, came_ref, grad_ref, query_ref, part_ref
+    heads, chunks, runs, rows_ref, mix_ref, weights_ref, enter_ref, leave_ref, keep_ref, back_ref,
+    came_ref, grad_ref, normed_ref, out_ref, part_ref, block_ref, query_ref, sems,
 ):
-    came = arriving(came_ref, heads, 1)
+    mine = lax.rem(lax.axis_index("seq"), heads)
+    group = CHUNK // LANES
+    copies = []
+    came = arriving(came_ref, heads, 1).astype(f32)
     for chunk in range(chunks):
         query, key, value = (part_rows(rows_ref, part, chunk) for part in range(3))
         grad = grad_ref[chunk]
-        (high, low), _ = entering(keep_ref, chunk, came)
+        state = keep_ref[chunk, 0:LANES, :] + keep_ref[chunk, LANES : LANES + 1, :] * came
+        state = jnp.concatenate(halves(state), axis=1)
         grad_mix = (dot_nt(grad, value) * mix_ref[chunk]).astype(bf16)
-        grad_query = dot_nt(grad, high) + dot_nt(grad, low)
-        grad_query = dot(grad_mix, key) + enter_ref[chunk] * grad_query
+        grad_query = dot(grad_mix, key) + enter_ref[chunk] * folded(dot(grad, state))
         query_ref[:, chunk * 16 : (chunk + 1) * 16, :] = (
             grad_query.astype(bf16).reshape(16, 16, LANES)
         )
-        part_ref[0, chunk] = dot_tn(grad_mix, query)
-        part_ref[1, chunk] = dot_tn(weights_ref[chunk], grad)
-
-
-def final_kernel(heads, chunks, rows_ref, leave_ref, query_ref, part_ref, back_ref, came_ref, out_ref):
+        here = pl.ds(chunk * 16, 16)
+        copies.append(
+            pltpu.make_async_copy(query_ref.at[:, here, :], out_ref.at[:, here, :], sems.at[chunk])
+        )
+        copies[-1].start()
+        split = normed_ref[chunk].astype(f32).reshape(runs, group, CHUNK // (runs * group), LANES)
+        for i in range(group):
+            step = jnp.bitwise_xor(mine, chunk * group + i)
+            at = jnp.bitwise_and(step, 1) * (heads // 2) + lax.div(step, 2)
+            block_ref[at] = split[:, i].reshape(LANES, LANES).astype(bf16)
+        grad_key = dot_tn(grad_mix, query)
+        grad_value = dot_tn(weights_ref[chunk], grad)
+        if chunk < chunks - 1:
+            high, low = halves(back_ref[chunk, 0:LANES, :])
+            leave = leave_ref[chunk]
+            across, down = jnp.concatenate([high, low], axis=1), jnp.concatenate([high, low], axis=0)
+            grad_key = grad_key + leave * folded(dot(value, across))
+            grad_value = grad_value + leave * folded(dot_nt(key, down))
+        part_ref[0, chunk] = grad_key
+        part_ref[1, chunk] = grad_value
+    for copy in copies:
+        copy.wait()
+
+
+def final_kernel(
+    heads, chunks, rows_ref, leave_ref, part_ref, back_ref, came_ref, given_ref, out_ref, stage, sems
+):
     per = chunks * 16
     came = arriving(came_ref, heads, -1)
-    out_ref[:, 0:per, :] = query_ref[...]
+    copies = []
     for chunk in range(chunks):
         key, value = (part_rows(rows_ref, part, chunk) for part in (1, 2))
-        leave = leave_ref[chunk]
-        (high, low), _ = entering(back_ref, chunk, came)
-        grad_key = part_ref[0, chunk] + leave * (dot_nt(value, high) + dot_nt(value, low))
-        grad_value = part_ref[1, chunk] + leave * (dot(key, high) + dot(key, low))
-        for part, grad in ((1, grad_key), (2, grad_value)):
-            at = part * per + chunk * 16
-            out_ref[:, at : at + 16, :] = grad.astype(bf16).reshape(16, 16, LANES)
+        leave = leave_ref[chunk] * back_ref[chunk, LANES : LANES + 1, :]
+        grad_key = part_ref[0, chunk] + leave * dot(value, came)
+        grad_value = part_ref[1, chunk] + leave * dot_nt(key, came)
+        for part, grad in ((0, grad_key), (1, grad_value)):
+            stage[part, chunk] = grad.astype(bf16).reshape(16, 16, LANES)
+            there = pl.ds((part + 1) * per + chunk * 16, 16)
+            copy = pltpu.make_async_copy(
+                stage.at[part, chunk], out_ref.at[:, there, :], sems.at[len(copies)]
+            )
+            copy.start()
+            copies.append(copy)
+    for copy in copies:
+        copy.wait()
 
 
 def carried(last, gain, segments, heads, step):
@@ -513,7 +561,6 @@
     tall = (chunks, CHUNK, LANES)
     square = (chunks, CHUNK, CHUNK)
     states = (chunks, LANES + 8, LANES)
-    low = (16, chunks * 16, LANES)
     unit = 2 * chunks * CHUNK * LANES
     order, reached, chosen = call(
         functools.partial(plan_kernel, heads, chunks, peers),
@@ -539,49 +586,59 @@
     gain = keep[-1, LANES : LANES + 1] * keep[-1, LANES + 1 : LANES + 2]
     gain = jnp.broadcast_to(gain, (8, LANES))
     came = carried(last, gain, segments, heads, 1)
-    mix, weights, inner, enter = call(
-        functools.partial(inner_kernel, chunks),
-        (shape(*square), shape(*square, dtype=bf16), shape(*tall), shape(*tall)),
-        (arrived, order, running, count),
+    mix, weights, inner, enter, normal = call(
+        functools.partial(inner_kernel, heads, chunks, runs),
+        (shape(*square), shape(*square, dtype=bf16), shape(*tall), shape(*tall), shape(*tall)),
+        (arrived, order, running, count, keep, *normal),
         flops=unit * 1024,
         moved=2 * arrived.size + 8 * chunks * CHUNK * CHUNK,
-        in_specs=[VMEM] * 4,
-        out_specs=[VMEM] * 4,
-    )
-    grad, normed, back, last = call(
-        functools.partial(output_kernel, heads, chunks, runs),
-        (
-            shape(*tall, dtype=bf16), shape(heads, rows, LANES, dtype=bf16), shape(*states),
-            shape(LANES, LANES, dtype=bf16),
-        ),
-        (arrived, inner, enter, keep, came, *normal),
-        flops=unit * 1024,
-        moved=2 * arrived.size + 8 * chunks * CHUNK * LANES,
         in_specs=[VMEM] * 5 + [ANY] * len(normal),
-        out_specs=[VMEM] * 4,
+        out_specs=[VMEM] * 5,
         scratch_shapes=[
             pltpu.VMEM((heads, rows, LANES), f32),
             pltpu.SemaphoreType.DMA((heads,)),
         ],
     )
+    grad, normed, back, last = call(
+        functools.partial(output_kernel, heads, chunks),
+        (
+            shape(*tall, dtype=bf16), shape(*tall, dtype=bf16), shape(*states),
+            shape(LANES, LANES, dtype=bf16),
+        ),
+        (arrived, inner, enter, keep, normal, came),
+        flops=unit * 1024,
+        moved=2 * arrived.size + 8 * chunks * CHUNK * LANES,
+        in_specs=[VMEM] * 6,
+        out_specs=[VMEM] * 4,
+    )
     came_back = carried(last, gain, segments, heads, -1)
-    grad_query, part = call(
-        functools.partial(local_kernel, heads, chunks),
-        (shape(*low, dtype=bf16), shape(2, *tall)),
-        (arrived, mix, weights, enter, keep, came, grad),
+    full = shape(16, 3 * chunks * 16, LANES, dtype=bf16)
+    grads, part, normed = call(
+        functools.partial(local_kernel, heads, chunks, runs),
+        (full, shape(2, *tall), shape(heads, rows, LANES, dtype=bf16)),
+        (arrived, mix, weights, enter, leave, keep, back, came, grad, normed),
         flops=unit * 1024,
         moved=2 * arrived.size + 8 * chunks * CHUNK * CHUNK,
-        in_specs=[VMEM] * 7,
-        out_specs=[VMEM] * 2,
+        in_specs=[VMEM] * 10,
+        out_specs=[ANY] + [VMEM] * 2,
+        scratch_shapes=[
+            pltpu.VMEM((16, chunks * 16, LANES), bf16),
+            pltpu.SemaphoreType.DMA((chunks,)),
+        ],
     )
     grads = call(
         functools.partial(final_kernel, heads, chunks),
-        shape(16, 3 * chunks * 16, LANES, dtype=bf16),
-        (arrived, leave, grad_query, part, back, came_back),
+        full,
+        (arrived, leave, part, back, came_back, grads),
         flops=unit * 512,
         moved=4 * arrived.size,
-        in_specs=[VMEM] * 6,
-        out_specs=VMEM,
+        in_specs=[VMEM] * 5 + [ANY],
+        out_specs=ANY,
+        input_output_aliases={5: 0},
+        scratch_shapes=[
+            pltpu.VMEM((2, chunks, 16, 16, LANES), bf16),
+            pltpu.SemaphoreType.DMA((2 * chunks,)),
+        ],
     )
     normed, grads = lax.optimization_barrier((normed, grads))
     if per == 16:
@@ -598,7 +655,7 @@
         grads = grads.reshape(3, chunks, peers, per, LANES).transpose(2, 0, 1, 3, 4)
         grads = grads.reshape(peers, 3 * per_seg, LANES)
     grad_projected = unpack(exchange(grads), rows, heads, segments)
-    grad_weight = grad_weight_of(normed, turned, heads, mine)
+    grad_weight = grad_weight_of(normed, turned)
     return (grad_projected, grad_weight)
 
 

time: 71.9 us -> 69.6 us (0.968)
  Pallas kernels: 18.7 us -> 17 us
    pallas_call x4 -> x0, Pallas kernels: 5.84 us -> none  [grad_weight_of(): pl.pallas_call(body, out_shape=total, grid_spec=pltpu.PrefetchScalarGridS...]
    pallas_call x8 -> x12, Pallas kernels: 10.4 us -> 14.8 us  [call(): pl.pallas_call(body, out_shape=outs, compiler_params=PARAMS, cost_estimat...]
    ppermute x2, waiting for transfers between devices: 7.4 us -> 5.57 us  [carried(): return lax.ppermute(last, 'seq', pairs)]
    ppermute x8, waiting for transfers between devices: 12.7 us -> 13.8 us  [swap(): return lax.ppermute(value, 'seq', [(i, i ^ step) for i in range(peers)])]
  transfers between devices with their start and end apart: 12 -> 12, of which waited for: 8 -> 9; matrix products, arithmetic and copies ran while one was open for 1% -> 1% of each run, Pallas kernels for 17% -> 17%
where the time goes in v5:
time: 69.6 us; the launch traced here: 69.1 us
  waiting for transfers between devices  28.3 us (41%)
  starting transfers between devices  18.4 us (26%)
  Pallas kernels  17 us (24%)
  local copies, waits for them, and re-layouts  3.94 us (6%)
  between operations  0.81 us (1%)
  other arithmetic  0.71 us (1%)
    pallas_call x12, Pallas kernels, call(): pl.pallas_call(body, out_shape=outs, compiler_params=PARAMS, cost_estimat...  14.8 us
    ppermute x8, waiting for transfers between devices, swap(): return lax.ppermute(value, 'seq', [(i, i ^ step) for i in range(peers)])  13.8 us
    all_to_all x2, starting transfers between devices, exchange(): return lax.all_to_all(value, 'seq', split_axis=0, concat_axis=0, tiled=True)  10.5 us
    all_to_all x2, waiting for transfers between devices, exchange(): return lax.all_to_all(value, 'seq', split_axis=0, concat_axis=0, tiled=True)  8.88 us
    ppermute x8, starting transfers between devices, swap(): return lax.ppermute(value, 'seq', [(i, i ^ step) for i in range(peers)])  7.72 us
    ppermute x2, waiting for transfers between devices, carried(): return lax.ppermute(last, 'seq', pairs)  5.57 us
    unnamed x6, local copies, waits for them, and re-layouts  3.88 us
    pallas_call x1, Pallas kernels, pack(): pl.pallas_call(functools.partial(pack_kernel, heads, segments), out_shape...  2.19 us
  transfers between devices with their start and end apart: 12, of which 9 were waited for; matrix products, arithmetic and copies ran while one was open for 1% of the time, Pallas kernels for 17%

profile of v5, /device:TPU:18, one launch (start us, length us, event | category | flops | bytes accessed | tf_op | source)
XLA Modules:
  0.0 69.1 jit_solution(16880036640482243613)
XLA Ops:
  0.6 2.2 %shard_map.77 = bf16[16,200,128]{2,1,0:T(8,128)(2,1)} custom-call(bf16[128,3072]{1,0:T(8,128)(2,1)} %rows_ref.1, bf16[8,128]{1,0:T(8,128)(2,1)} %bitcast.5, s32[1,128]{1,0:T(1,128)} %bitcast.6), custom_call_target="tpu_custom_call" | custom-call | tf_op jit(solution)/shard_map/pallas_call | solution.py:106
  2.8 6.2 %all-to-all-start = ((bf16[16,200,128]{2,1,0:T(8,128)(2,1)}), bf16[16,200,128]{2,1,0:T(8,128)(2,1)S(1)}, u32[]{:S(2)}, u32[]{:S(2)}) async-start(bf16[16,200,128]{2,1,0:T(8,128)(2,1)} %shard_map.77), calls=%async_computation | async-start | bytes 1638400 | tf_op jit(solution)/shard_map/all_to_all | solution.py:518
  9.0 2.2 %copy-done = bf16[1024,2048]{1,0:T(8,128)(2,1)S(1)} copy-done((bf16[1024,2048]{1,0:T(8,128)(2,1)S(1)}, bf16[1024,2048]{1,0:T(8,128)(2,1)}, u32[]{:S(2)}) %copy-start) | copy-done | bytes 4194328
  11.2 1.0 %copy-done.1 = bf16[128,2048]{1,0:T(8,128)(2,1)S(1)} copy-done((bf16[128,2048]{1,0:T(8,128)(2,1)S(1)}, bf16[128,2048]{1,0:T(8,128)(2,1)}, u32[]{:S(2)}) %copy-start.1) | copy-done | bytes 524312
  12.3 0.7 copy-done.2
  12.9 1.5 %shard_map.80 = (f32[4,128,128]{2,1,0:T(8,128)S(1)}, f32[4,128,128]{2,1,0:T(8,128)S(1)}, bf16[128,2048]{1,0:T(8,128)(2,1)S(1)}) custom-call(bf16[128,2048]{1,0:T(8,128)(2,1)S(1)} %copy-done.1, s32[1,128]{1,0:T(1,128)S(1)} %bitcast.3, bf16[1024,2048]{1,0:T(8,128)(2,1)S(1)} %copy-done), custom_call_target="tpu_custom_call" | custom-call | flops 536870912 | bytes 5242880 | tf_op jit(solution)/shard_map/pallas_call | solution.py:54
  14.7 1.4 %collective-permute-done = f32[4,128,128]{2,1,0:T(8,128)S(1)} collective-permute-done((f32[4,128,128]{2,1,0:T(8,128)S(1)}, f32[4,128,128]{2,1,0:T(8,128)S(1)}, u32[]{:S(2)}, u32[]{:S(2)}) %collective-permute-start) | collective-permute-done | bytes 262176 | tf_op jit(solution)/shard_map/ppermute | solution.py:532
  16.1 1.5 %collective-permute-start.1 = (f32[2,128,128]{2,1,0:T(8,128)S(1)}, f32[2,128,128]{2,1,0:T(8,128)S(1)}, u32[]{:S(2)}, u32[]{:S(2)}) collective-permute-start(f32[2,128,128]{2,1,0:T(8,128)S(1)} %pad_maximum_fusion), channel_id=1, source_target_pairs={{0,2},{1,3},{2,0},{3,1},{4,6},{5,7},{6,4},{7,5},{8,10},{9,11},{10,... | collective-permute-start | bytes 393224 | tf_op jit(solution)/shard_map/ppermute | solution.py:532
  17.6 1.5 %collective-permute-start.2 = (f32[2,128,128]{2,1,0:T(8,128)S(1)}, f32[2,128,128]{2,1,0:T(8,128)S(1)}, u32[]{:S(2)}, u32[]{:S(2)}) collective-permute-start(f32[2,128,128]{2,1,0:T(8,128)S(1)} %pad_maximum_fusion.1), channel_id=1, source_target_pairs={{0,4},{1,5},{2,6},{3,7},{4,0},{5,1},{6,2},{7,3},{8,12},{9,13},{10,... | collective-permute-start | bytes 393224 | tf_op jit(solution)/shard_map/ppermute | solution.py:532
  19.2 0.7 pad_maximum_fusion.2
  19.8 0.6 collective-permute-start.3
  20.9 8.9 %all-to-all-done.rows_ref.meta_ref = bf16[16,200,128]{2,1,0:T(8,128)(2,1)S(1)} async-done(((bf16[16,200,128]{2,1,0:T(8,128)(2,1)}), bf16[16,200,128]{2,1,0:T(8,128)(2,1)S(1)}, u32[]{:S(2)}, u32[]{:S(2)}) %all-to-all-start) | async-done | bytes 819232 | tf_op jit(solution)/shard_map/all_to_all | solution.py:518
  29.8 1.5 %shard_map.79 = (bf16[128,128]{1,0:T(8,128)(2,1)S(1)}, f32[4,136,128]{2,1,0:T(8,128)S(1)}, f32[4,256,128]{2,1,0:T(8,128)S(1)}, f32[4,256,128]{2,1,0:T(8,128)S(1)}, f32[4,256,128]{2,1,0:T(8,128)S(1)}) custom-call(bf16[16,200,128]{2,1,0:T(8,128)(2,1)S(1)} %all-to-all-done.rows_ref.meta_ref, bf16[16,200,128]{2,1,0:T(8,128)(2,1)S(1)} %all-to-all-done.rows_ref.meta_ref, ...), custom_call_target="tpu_custom_call" | custom-call | flops 134217728 | bytes 819200 | tf_op jit(solution)/shard_map/pallas_call | solution.py:54
  31.9 1.6 %shard_map.81 = (f32[4,256,256]{2,1,0:T(8,128)S(1)}, bf16[4,256,256]{2,1,0:T(8,128)(2,1)S(1)}, f32[4,256,128]{2,1,0:T(8,128)S(1)}, f32[4,256,128]{2,1,0:T(8,128)S(1)}, f32[4,256,128]{2,1,0:T(8,128)S(1)}) custom-call(bf16[16,200,128]{2,1,0:T(8,128)(2,1)S(1)} %all-to-all-done.rows_ref.meta_ref, bf16[4,256,256]{2,1,0:T(8,128)(2,1)S(1)} %get-tuple-element.27.order_ref, ...), custom_call_target="tpu_custom_call" | custom-call | flops 268435456 | bytes 2916352 | tf_op jit(solution)/shard_map/pallas_call | solution.py:54
  33.6 2.6 %collective-permute-done.4.came_ref = bf16[128,128]{1,0:T(8,128)(2,1)S(1)} collective-permute-done((bf16[128,128]{1,0:T(8,128)(2,1)S(1)}, bf16[128,128]{1,0:T(8,128)(2,1)S(1)}, u32[]{:S(2)}, u32[]{:S(2)}) %collective-permute-start.4) | collective-permute-done | bytes 32800 | tf_op jit(solution)/shard_map/ppermute | solution.py:484
  36.2 0.8 %shard_map.82 = (bf16[4,256,128]{2,1,0:T(8,128)(2,1)S(1)}, bf16[4,256,128]{2,1,0:T(8,128)(2,1)S(1)}, f32[4,136,128]{2,1,0:T(8,128)S(1)}, bf16[128,128]{1,0:T(8,128)(2,1)S(1)}) custom-call(bf16[16,200,128]{2,1,0:T(8,128)(2,1)S(1)} %all-to-all-done.rows_ref.meta_ref, f32[4,256,128]{2,1,0:T(8,128)S(1)} %get-tuple-element.39.inner_ref, ...), custom_call_target="tpu_custom_call" | custom-call | flops 268435456 | bytes 1867776 | tf_op jit(solution)/shard_map/pallas_call | solution.py:54
  37.1 1.8 %shard_map.83 = (bf16[16,192,128]{2,1,0:T(8,128)(2,1)}, f32[2,4,256,128]{3,2,1,0:T(8,128)S(1)}, bf16[8,128,128]{2,1,0:T(8,128)(2,1)S(1)}) custom-call(bf16[16,200,128]{2,1,0:T(8,128)(2,1)S(1)} %all-to-all-done.rows_ref.meta_ref, f32[4,256,256]{2,1,0:T(8,128)S(1)} %get-tuple-element.35.mix_ref, bf16[4,256,256]{2,1,0:T(8,128)(2,1)S(1)} %get-tuple-element.36.weights_ref, ...), custom_call_target="tpu_custom_call" | custom-call | flops 268435456 | bytes 2916352 | tf_op jit(solution)/shard_map/pallas_call | solution.py:54
  38.9 3.0 %collective-permute-done.5.came_ref = bf16[128,128]{1,0:T(8,128)(2,1)S(1)} collective-permute-done((bf16[128,128]{1,0:T(8,128)(2,1)S(1)}, bf16[128,128]{1,0:T(8,128)(2,1)S(1)}, u32[]{:S(2)}, u32[]{:S(2)}) %collective-permute-start.5) | collective-permute-done | bytes 32800 | tf_op jit(solution)/shard_map/ppermute | solution.py:484
  41.9 1.0 %shard_map.84 = bf16[16,192,128]{2,1,0:T(8,128)(2,1)} custom-call(bf16[16,200,128]{2,1,0:T(8,128)(2,1)S(1)} %all-to-all-done.rows_ref.meta_ref, f32[4,256,128]{2,1,0:T(8,128)S(1)} %get-tuple-element.38.leave_ref, f32[2,4,256,128]{3,2,1,0:T(8,128)S(1)} %get-tuple-element.46.part_ref, ...), custom_call_target="tpu_custom_call", output_to_operand_aliasing={{}: (5, {})} | custom-call | flops 134217728 | bytes 1638400 | tf_op jit(solution)/shard_map/pallas_call | solution.py:54
  42.9 4.3 %all-to-all-start.1 = ((bf16[16,192,128]{2,1,0:T(8,128)(2,1)}), bf16[16,192,128]{2,1,0:T(8,128)(2,1)S(1)}, u32[]{:S(2)}, u32[]{:S(2)}) async-start(bf16[16,192,128]{2,1,0:T(8,128)(2,1)} %shard_map.84), calls=%async_computation.1 | async-start | bytes 1572864 | tf_op jit(solution)/shard_map/all_to_all | solution.py:518
  47.5 1.2 %collective-permute-done.6 = bf16[4,128,128]{2,1,0:T(8,128)(2,1)S(1)} collective-permute-done((bf16[4,128,128]{2,1,0:T(8,128)(2,1)S(1)}, bf16[4,128,128]{2,1,0:T(8,128)(2,1)S(1)}, u32[]{:S(2)}, u32[]{:S(2)}) %collective-permute-start.6) | collective-permute-done | bytes 131104 | tf_op jit(solution)/shard_map/ppermute | solution.py:532
  48.7 1.5 %collective-permute-start.8 = (bf16[2,128,128]{2,1,0:T(8,128)(2,1)S(1)}, bf16[2,128,128]{2,1,0:T(8,128)(2,1)S(1)}, u32[]{:S(2)}, u32[]{:S(2)}) collective-permute-start(bf16[2,128,128]{2,1,0:T(8,128)(2,1)S(1)} %pad_maximum_fusion.4), channel_id=1, source_target_pairs={{0,4},{1,5},{2,6},{3,7},{4,0},{5,1},{6,2},{7,3},{8,12},{9,13},{10,... | collective-permute-start | bytes 196616 | tf_op jit(solution)/shard_map/ppermute | solution.py:532
  50.2 1.5 %collective-permute-start.9 = (bf16[2,128,128]{2,1,0:T(8,128)(2,1)S(1)}, bf16[2,128,128]{2,1,0:T(8,128)(2,1)S(1)}, u32[]{:S(2)}, u32[]{:S(2)}) collective-permute-start(bf16[2,128,128]{2,1,0:T(8,128)(2,1)S(1)} %pad_maximum_fusion.5), channel_id=1, source_target_pairs={{0,2},{1,3},{2,0},{3,1},{4,6},{5,7},{6,4},{7,5},{8,10},{9,11},{10,... | collective-permute-start | bytes 196616 | tf_op jit(solution)/shard_map/ppermute | solution.py:532
  51.8 0.6 collective-permute-start.7
  52.4 1.3 %shard_map.86.refs_2_ = bf16[1024,2048]{1,0:T(8,128)(2,1)} custom-call(bf16[1,128,128]{2,1,0:T(8,128)(2,1)S(1)} %get-tuple-element.52.refs_0_, bf16[1,128,128]{2,1,0:T(8,128)(2,1)S(1)} %get-tuple-element.64.refs_1_, bf16[128,2048]{1,0:T(8,128)(2,1)S(1)} %get-tuple-element.51.refs_2_.refs_1_), custom_call_target="tpu_custom_call" | custom-call | flops 134217728 | bytes 1048576 | tf_op jit(solution)/shard_map/pallas_call | solution.py:54
  53.6 1.8 %collective-permute-done.9.refs_0_ = bf16[2,128,128]{2,1,0:T(8,128)(2,1)S(1)} collective-permute-done((bf16[2,128,128]{2,1,0:T(8,128)(2,1)S(1)}, bf16[2,128,128]{2,1,0:T(8,128)(2,1)S(1)}, u32[]{:S(2)}, u32[]{:S(2)}) %collective-permute-start.9) | collective-permute-done | bytes 65568 | tf_op jit(solution)/shard_map/ppermute | solution.py:532
  55.4 1.3 %shard_map.87.refs_2_ = bf16[1024,2048]{1,0:T(8,128)(2,1)} custom-call(bf16[2,128,128]{2,1,0:T(8,128)(2,1)S(1)} %collective-permute-done.9.refs_0_, bf16[128,2048]{1,0:T(8,128)(2,1)S(1)} %get-tuple-element.51.refs_2_.refs_1_, bf16[1024,2048]{1,0:T(8,128)(2,1)} %shard_map.86.refs_2_), custom_call_target="tpu_custom_call", output_to_operand_aliasing={{}: (2, {})} | custom-call | flops 134217728 | bytes 1048576 | tf_op jit(solution)/shard_map/pallas_call | solution.py:54
  56.7 7.8 %collective-permute-done.8.refs_0_ = bf16[2,128,128]{2,1,0:T(8,128)(2,1)S(1)} collective-permute-done((bf16[2,128,128]{2,1,0:T(8,128)(2,1)S(1)}, bf16[2,128,128]{2,1,0:T(8,128)(2,1)S(1)}, u32[]{:S(2)}, u32[]{:S(2)}) %collective-permute-start.8) | collective-permute-done | bytes 65568 | tf_op jit(solution)/shard_map/ppermute | solution.py:532
  64.5 1.3 %shard_map.88.refs_2_ = bf16[1024,2048]{1,0:T(8,128)(2,1)} custom-call(bf16[2,128,128]{2,1,0:T(8,128)(2,1)S(1)} %collective-permute-done.8.refs_0_, bf16[128,2048]{1,0:T(8,128)(2,1)S(1)} %get-tuple-element.51.refs_2_.refs_1_, bf16[1024,2048]{1,0:T(8,128)(2,1)} %shard_map.87.refs_2_), custom_call_target="tpu_custom_call", output_to_operand_aliasing={{}: (2, {})} | custom-call | flops 134217728 | bytes 1048576 | tf_op jit(solution)/shard_map/pallas_call | solution.py:54
  65.8 1.1 %collective-permute-done.7.refs_0_ = bf16[2,128,128]{2,1,0:T(8,128)(2,1)S(1)} collective-permute-done((bf16[2,128,128]{2,1,0:T(8,128)(2,1)S(1)}, bf16[2,128,128]{2,1,0:T(8,128)(2,1)S(1)}, u32[]{:S(2)}, u32[]{:S(2)}) %collective-permute-start.7) | collective-permute-done | bytes 65568 | tf_op jit(solution)/shard_map/ppermute | solution.py:532
  66.9 1.3 %shard_map.89 = bf16[1024,2048]{1,0:T(8,128)(2,1)} custom-call(bf16[2,128,128]{2,1,0:T(8,128)(2,1)S(1)} %collective-permute-done.7.refs_0_, bf16[128,2048]{1,0:T(8,128)(2,1)S(1)} %get-tuple-element.51.refs_2_.refs_1_, bf16[1024,2048]{1,0:T(8,128)(2,1)} %shard_map.88.refs_2_), custom_call_target="tpu_custom_call", output_to_operand_aliasing={{}: (2, {})} | custom-call | flops 134217728 | bytes 1048576 | tf_op jit(solution)/shard_map/pallas_call | solution.py:54
  68.2 1.0 %shard_map.85 = bf16[128,3072]{1,0:T(8,128)(2,1)} custom-call(bf16[16,192,128]{2,1,0:T(8,128)(2,1)S(1)} %all-to-all-done.1.in_ref), custom_call_target="tpu_custom_call" | custom-call | bytes 1572864 | tf_op jit(solution)/shard_map/pallas_call | solution.py:54
  (22 shorter events, 1.7 us)
Async XLA Ops:
  2.8 26.9 %all-to-all-start = ((bf16[16,200,128]{2,1,0:T(8,128)(2,1)}), bf16[16,200,128]{2,1,0:T(8,128)(2,1)S(1)}, u32[]{:S(2)}, u32[]{:S(2)}) async-start(bf16[16,200,128]{2,1,0:T(8,128)(2,1)} %shard_map.77), calls=%async_computation | async-start | bytes 1638400 | tf_op jit(solution)/shard_map/all_to_all | solution.py:518
  9.0 2.2 %copy-start = (bf16[1024,2048]{1,0:T(8,128)(2,1)S(1)}, bf16[1024,2048]{1,0:T(8,128)(2,1)}, u32[]{:S(2)}) copy-start(bf16[1024,2048]{1,0:T(8,128)(2,1)} %weight_ref.1) | copy-start | bytes 12582916
  11.2 1.0 %copy-start.1 = (bf16[128,2048]{1,0:T(8,128)(2,1)S(1)}, bf16[128,2048]{1,0:T(8,128)(2,1)}, u32[]{:S(2)}) copy-start(bf16[128,2048]{1,0:T(8,128)(2,1)} %up_ref.1) | copy-start | bytes 1572868
  12.3 0.7 copy-start.2
  14.4 1.6 %collective-permute-start = (f32[4,128,128]{2,1,0:T(8,128)S(1)}, f32[4,128,128]{2,1,0:T(8,128)S(1)}, u32[]{:S(2)}, u32[]{:S(2)}) collective-permute-start(f32[4,128,128]{2,1,0:T(8,128)S(1)} %get-tuple-element.34), channel_id=1, source_target_pairs={{0,1},{1,0},{2,3},{3,2},{4,5},{5,4},{6,7},{7,6},{8,9},{9,8},{10,11... | collective-permute-start | bytes 786440 | tf_op jit(solution)/shard_map/ppermute | solution.py:532
  16.1 15.3 %collective-permute-start.1 = (f32[2,128,128]{2,1,0:T(8,128)S(1)}, f32[2,128,128]{2,1,0:T(8,128)S(1)}, u32[]{:S(2)}, u32[]{:S(2)}) collective-permute-start(f32[2,128,128]{2,1,0:T(8,128)S(1)} %pad_maximum_fusion), channel_id=1, source_target_pairs={{0,2},{1,3},{2,0},{3,1},{4,6},{5,7},{6,4},{7,5},{8,10},{9,11},{10,... | collective-permute-start | bytes 393224 | tf_op jit(solution)/shard_map/ppermute | solution.py:532
  17.6 13.8 %collective-permute-start.2 = (f32[2,128,128]{2,1,0:T(8,128)S(1)}, f32[2,128,128]{2,1,0:T(8,128)S(1)}, u32[]{:S(2)}, u32[]{:S(2)}) collective-permute-start(f32[2,128,128]{2,1,0:T(8,128)S(1)} %pad_maximum_fusion.1), channel_id=1, source_target_pairs={{0,4},{1,5},{2,6},{3,7},{4,0},{5,1},{6,2},{7,3},{8,12},{9,13},{10,... | collective-permute-start | bytes 393224 | tf_op jit(solution)/shard_map/ppermute | solution.py:532
  19.8 12.1 %collective-permute-start.3 = (f32[2,128,128]{2,1,0:T(8,128)}, f32[2,128,128]{2,1,0:T(8,128)S(1)}, u32[]{:S(2)}, u32[]{:S(2)}) collective-permute-start(f32[2,128,128]{2,1,0:T(8,128)} %pad_maximum_fusion.2), channel_id=1, source_target_pairs={{0,6},{1,7},{2,4},{3,5},{4,2},{5,3},{6,0},{7,1},{8,14},{9,15},{10,... | collective-permute-start | bytes 393224 | tf_op jit(solution)/shard_map/ppermute | solution.py:532
  31.3 4.9 %collective-permute-start.4 = (bf16[128,128]{1,0:T(8,128)(2,1)S(1)}, bf16[128,128]{1,0:T(8,128)(2,1)S(1)}, u32[]{:S(2)}, u32[]{:S(2)}) collective-permute-start(bf16[128,128]{1,0:T(8,128)(2,1)S(1)} %get-tuple-element.41), channel_id=1, source_target_pairs={{0,8},{1,9},{2,10},{3,11},{4,12},{5,13},{6,14},{7,15},{8,0},{9,1},... | collective-permute-start | bytes 98312 | tf_op jit(solution)/shard_map/ppermute | solution.py:484
  37.0 4.9 %collective-permute-start.5 = (bf16[128,128]{1,0:T(8,128)(2,1)S(1)}, bf16[128,128]{1,0:T(8,128)(2,1)S(1)}, u32[]{:S(2)}, u32[]{:S(2)}) collective-permute-start(bf16[128,128]{1,0:T(8,128)(2,1)S(1)} %get-tuple-element.47), channel_id=1, source_target_pairs={{0,8},{1,9},{2,10},{3,11},{4,12},{5,13},{6,14},{7,15},{8,0},{9,1},... | collective-permute-start | bytes 98312 | tf_op jit(solution)/shard_map/ppermute | solution.py:484
  42.9 25.3 %all-to-all-start.1 = ((bf16[16,192,128]{2,1,0:T(8,128)(2,1)}), bf16[16,192,128]{2,1,0:T(8,128)(2,1)S(1)}, u32[]{:S(2)}, u32[]{:S(2)}) async-start(bf16[16,192,128]{2,1,0:T(8,128)(2,1)} %shard_map.84), calls=%async_computation.1 | async-start | bytes 1572864 | tf_op jit(solution)/shard_map/all_to_all | solution.py:518
  47.2 1.4 %collective-permute-start.6 = (bf16[4,128,128]{2,1,0:T(8,128)(2,1)S(1)}, bf16[4,128,128]{2,1,0:T(8,128)(2,1)S(1)}, u32[]{:S(2)}, u32[]{:S(2)}) collective-permute-start(bf16[4,128,128]{2,1,0:T(8,128)(2,1)S(1)} %slice.65), channel_id=1, source_target_pairs={{0,1},{1,0},{2,3},{3,2},{4,5},{5,4},{6,7},{7,6},{8,9},{9,8},{10,11... | collective-permute-start | bytes 393224 | tf_op jit(solution)/shard_map/ppermute | solution.py:532
  48.7 15.9 %collective-permute-start.8 = (bf16[2,128,128]{2,1,0:T(8,128)(2,1)S(1)}, bf16[2,128,128]{2,1,0:T(8,128)(2,1)S(1)}, u32[]{:S(2)}, u32[]{:S(2)}) collective-permute-start(bf16[2,128,128]{2,1,0:T(8,128)(2,1)S(1)} %pad_maximum_fusion.4), channel_id=1, source_target_pairs={{0,4},{1,5},{2,6},{3,7},{4,0},{5,1},{6,2},{7,3},{8,12},{9,13},{10,... | collective-permute-start | bytes 196616 | tf_op jit(solution)/shard_map/ppermute | solution.py:532
  50.2 5.2 %collective-permute-start.9 = (bf16[2,128,128]{2,1,0:T(8,128)(2,1)S(1)}, bf16[2,128,128]{2,1,0:T(8,128)(2,1)S(1)}, u32[]{:S(2)}, u32[]{:S(2)}) collective-permute-start(bf16[2,128,128]{2,1,0:T(8,128)(2,1)S(1)} %pad_maximum_fusion.5), channel_id=1, source_target_pairs={{0,2},{1,3},{2,0},{3,1},{4,6},{5,7},{6,4},{7,5},{8,10},{9,11},{10,... | collective-permute-start | bytes 196616 | tf_op jit(solution)/shard_map/ppermute | solution.py:532
  51.8 15.2 %collective-permute-start.7 = (bf16[2,128,128]{2,1,0:T(8,128)(2,1)S(1)}, bf16[2,128,128]{2,1,0:T(8,128)(2,1)S(1)}, u32[]{:S(2)}, u32[]{:S(2)}) collective-permute-start(bf16[2,128,128]{2,1,0:T(8,128)(2,1)S(1)} %pad_maximum_fusion.3), channel_id=1, source_target_pairs={{0,6},{1,7},{2,4},{3,5},{4,2},{5,3},{6,0},{7,1},{8,14},{9,15},{10,... | collective-permute-start | bytes 196616 | tf_op jit(solution)/shard_map/ppermute | solution.py:532

commit v6 on v5

--- a/solution.py
+++ b/solution.py
@@ -65,6 +65,7 @@
 ):
     per = rows_ref.shape[0] // segments
     inner = heads * LANES
+    peers = heads * segments
     quarter = per // 2
     arriving = [
         pltpu.make_async_copy(decay_ref, decay, sems.at[0]),
@@ -77,7 +78,15 @@
         copy.start()
     for copy in arriving[:2]:
         copy.wait()
+    chunks = heads * rows_ref.shape[0] // CHUNK
+    spots = CHUNK // peers
+    first = lax.rem(lax.axis_index("seq") * spots, LANES)
     line = iota((META, LANES), 0)
+    row, spot = iota((LANES, LANES), 0), iota((LANES, LANES), 1) - first
+    placed = []
+    for i in range(segments * chunks):
+        pick = (spot >= 0) & (spot < spots) & (row == i * spots + spot)
+        placed.append(dot(decay[...], jnp.where(pick, 1.0, 0.0).astype(bf16)))
     leaving = []
     for segment in range(segments):
         for copy in arriving[2 + 2 * segment : 4 + 2 * segment]:
@@ -89,8 +98,10 @@
                 stage[to, part * per : (part + 1) * per, :] = held[
                     segment * per : (segment + 1) * per, at : at + LANES
                 ]
-            meta = decay[...].astype(f32)[head : head + 1, :]
-            meta = jnp.where(line == 0, meta, jnp.where(line == 1, flags[...].astype(f32), 0.0))
+            meta = jnp.where(line == chunks, flags[...].astype(f32), 0.0)
+            for i in range(chunks):
+                here = placed[segment * chunks + i][head : head + 1, :]
+                meta = jnp.where(line == i, here, meta)
             stage[to, 3 * per :, :] = meta.astype(bf16)
             leaving.append(pltpu.make_async_copy(stage.at[to], out_ref.at[to], out_sems.at[to]))
             leaving[-1].start()
@@ -120,11 +131,16 @@
         )(projected, decay_log.T, starts.reshape(1, rows))
     body = projected.reshape(segments, per, 3, heads, LANES).transpose(0, 3, 2, 1, 4)
     body = body.reshape(peers, 3 * per, LANES)
-    flags = jnp.broadcast_to(starts.astype(bf16)[None, None, :], (heads, 1, rows))
-    meta = jnp.concatenate(
-        [decay_log.T[:, None, :], flags, jnp.zeros((heads, META - 2, rows), bf16)], axis=1
-    )
-    meta = jnp.broadcast_to(meta[None], (segments, heads, META, LANES)).reshape(peers, META, LANES)
+    chunks = heads * rows // CHUNK
+    spots = CHUNK // peers
+    first = lax.axis_index("seq") * spots % LANES
+    decays = decay_log.T.reshape(heads, segments, chunks, spots).swapaxes(0, 1)
+    placed = lax.dynamic_update_slice(
+        jnp.zeros((segments, heads, chunks, LANES), bf16), decays, (0, 0, 0, first)
+    ).reshape(peers, chunks, LANES)
+    flags = jnp.broadcast_to(starts.astype(bf16)[None, None, :], (peers, 1, rows))
+    blank = jnp.zeros((peers, META - 1 - chunks, LANES), bf16)
+    meta = jnp.concatenate([placed, flags, blank], axis=1)
     return jnp.concatenate([body, meta], axis=1)
 
 
@@ -187,7 +203,7 @@
     along = iota((8, rows), 1)
     turn = dot_nt(turns[0:8, :], pick) + (along // count).astype(f32) - me
     line = (along % count * peers).astype(f32) + wrapped(turn, peers)
-    return chosen, column, line
+    return column, line
 
 
 def grad_normed_kernel(heads, peers, up_ref, destination_ref, weight_ref, even_ref, odd_ref, turned_ref):
@@ -195,7 +211,7 @@
     me = lax.axis_index("seq")
     capacity = rows // peers
     turns = turns_of(destination_ref, peers)
-    _, column, _ = places(turns, peers, me * capacity, capacity, rows)
+    column, _ = places(turns, peers, me * capacity, capacity, rows)
     pick = iota((rows, rows), 1).astype(f32) == column
     turned = dot(jnp.where(pick, 1.0, 0.0).astype(bf16), up_ref[...]).astype(bf16)
     turned_ref[...] = turned
@@ -246,7 +262,9 @@
     rows, width = upstream.shape
     heads = sum(piece.shape[0] for piece in normed)
     out = []
-    for at, pieces in enumerate([normed[:2]] + [[pair] for pair in normed[2:]]):
+    pairs = len(normed) - 1
+    for at in (0, 1, *range(pairs - 1, 1, -1)):
+        pieces = [normed[at + 1]] if at else normed[:2]
         count = len(pieces)
         out = [
             call(
@@ -275,40 +293,39 @@
     return ref[:, at : at + 16, :].reshape(CHUNK, LANES)
 
 
-def plan_kernel(heads, chunks, peers, destination_ref, order_ref, reached_ref, chosen_ref):
+def plan_kernel(heads, chunks, peers, destination_ref, order_ref, reached_ref):
     per = CHUNK // peers
     turns = turns_of(destination_ref, peers)
     spot = iota((CHUNK, CHUNK), 1).astype(f32)
     for chunk in range(chunks):
         first = (lax.div(lax.axis_index("seq"), heads) * chunks + chunk) * per
-        chosen, column, line = places(turns, peers, first, per, CHUNK)
+        column, line = places(turns, peers, first, per, CHUNK)
         column = wide(column)
         order_ref[chunk] = jnp.where(line[0:1, :] <= column, 1.0, 0.0).astype(bf16)
         reached_ref[chunk] = jnp.where(spot <= column, 1.0, 0.0).astype(bf16)
-        chosen_ref[chunk] = jnp.where(chosen, 1.0, 0.0).astype(bf16)
 
 
 def state_kernel(
-    heads, chunks, rows_ref, meta_ref, order_ref, reached_ref, chosen_ref,
+    heads, chunks, rows_ref, meta_ref, order_ref, reached_ref,
     last_ref, keep_ref, running_ref, count_ref, leave_ref,
 ):
     peers = meta_ref.shape[0]
     group = CHUNK // LANES
     first_block = lax.div(lax.axis_index("seq"), heads) * heads
-    lines = peers * META
-    meta = meta_ref[:, -META:, :].astype(f32).reshape(lines, LANES).astype(bf16)
-    row = iota((CHUNK, lines), 0)
-    pick = iota((CHUNK, lines), 1) == lax.div(row, CHUNK // peers) * META
-    decays = dot(jnp.where(pick, 1.0, 0.0).astype(bf16), meta).astype(bf16)
-    ones = jnp.ones((LANES, LANES), bf16)
+    owners = peers // group
+    lines = [
+        jnp.sum(meta_ref[i * owners : (i + 1) * owners, -META:, :].astype(f32), axis=0)
+        for i in range(group)
+    ]
     state = jnp.zeros((LANES, LANES), f32)
     before = jnp.ones((1, LANES), f32)
     line = iota((8, LANES), 0)
     for chunk in range(chunks):
-        decay = dot(decays * chosen_ref[chunk], ones).astype(bf16)
-        running = dot(order_ref[chunk], decay)
+        decay = jnp.concatenate([part[chunk : chunk + 1, :] for part in lines], axis=1)
+        decay = jnp.broadcast_to(decay, (LANES, CHUNK)).astype(bf16)
+        running = dot_nt(order_ref[chunk], decay)
         flags = [
-            meta_ref[first_block + chunk * group + i, -META:, :].astype(f32)[1:2, :]
+            meta_ref[first_block + chunk * group + i, -META:, :].astype(f32)[chunks : chunks + 1, :]
             for i in range(group)
         ]
         flags = jnp.broadcast_to(jnp.concatenate(flags, axis=1), (LANES, CHUNK)).astype(bf16)
@@ -334,18 +351,20 @@
 def inner_kernel(
     heads, chunks, runs, rows_ref, order_ref, running_ref, count_ref, keep_ref, *refs
 ):
-    given, (mix_ref, weights_ref, inner_ref, enter_ref, normal_ref, blocks, sems) = refs[:-7], refs[-7:]
+    given, (mix_ref, weights_ref, inner_ref, enter_ref, normal_ref, sems) = refs[:-6], refs[-6:]
     mine = lax.rem(lax.axis_index("seq"), heads)
     sources = [given[0].at[0], given[1].at[0]]
     for pair in given[2:]:
         sources += [pair.at[0], pair.at[1]]
-    copies = [
-        pltpu.make_async_copy(source, blocks.at[jnp.bitwise_xor(mine, step)], sems.at[step])
-        for step, source in enumerate(sources)
-    ]
-    for copy in copies:
-        copy.start()
     group = CHUNK // LANES
+    lines = LANES // runs
+    copies = []
+    for step, source in enumerate(sources):
+        block = jnp.bitwise_xor(mine, step)
+        here = pl.ds(pl.multiple_of(lax.rem(block, group) * lines, lines), lines)
+        target = normal_ref.at[lax.div(block, group), :, here, :]
+        copies.append(pltpu.make_async_copy(source, target, sems.at[step]))
+        copies[-1].start()
     lane = iota((CHUNK, LANES), 1)
     for chunk in range(chunks):
         running, count = running_ref[chunk], count_ref[chunk]
@@ -366,14 +385,6 @@
         enter_ref[chunk] = enter
     for copy in copies:
         copy.wait()
-    for chunk in range(chunks):
-        normal_ref[chunk] = jnp.concatenate(
-            [
-                blocks[chunk * group + i].reshape(runs, 1, CHUNK // (runs * group), LANES)
-                for i in range(group)
-            ],
-            axis=1,
-        ).reshape(CHUNK, LANES)
 
 
 def arriving(came_ref, heads, step):
@@ -399,7 +410,7 @@
         scale = lax.rsqrt(jnp.mean(output * output, axis=1, keepdims=True) + norm_eps)
         normed = output * scale
         normed_ref[chunk] = normed.astype(bf16)
-        normal = normal_ref[chunk]
+        normal = normal_ref[chunk].reshape(CHUNK, LANES)
         grad = (
             (normal - normed * jnp.mean(normal * normed, axis=1, keepdims=True)) * scale
         ).astype(bf16)
@@ -414,11 +425,9 @@
 
 
 def local_kernel(
-    heads, chunks, runs, rows_ref, mix_ref, weights_ref, enter_ref, leave_ref, keep_ref, back_ref,
-    came_ref, grad_ref, normed_ref, out_ref, part_ref, block_ref, query_ref, sems,
+    heads, chunks, rows_ref, mix_ref, weights_ref, enter_ref, leave_ref, keep_ref, back_ref,
+    came_ref, grad_ref, out_ref, part_ref, query_ref, sems,
 ):
-    mine = lax.rem(lax.axis_index("seq"), heads)
-    group = CHUNK // LANES
     copies = []
     came = arriving(came_ref, heads, 1).astype(f32)
     for chunk in range(chunks):
@@ -436,11 +445,6 @@
             pltpu.make_async_copy(query_ref.at[:, here, :], out_ref.at[:, here, :], sems.at[chunk])
         )
         copies[-1].start()
-        split = normed_ref[chunk].astype(f32).reshape(runs, group, CHUNK // (runs * group), LANES)
-        for i in range(group):
-            step = jnp.bitwise_xor(mine, chunk * group + i)
-            at = jnp.bitwise_and(step, 1) * (heads // 2) + lax.div(step, 2)
-            block_ref[at] = split[:, i].reshape(LANES, LANES).astype(bf16)
         grad_key = dot_tn(grad_mix, query)
         grad_value = dot_tn(weights_ref[chunk], grad)
         if chunk < chunks - 1:
@@ -453,6 +457,17 @@
         part_ref[1, chunk] = grad_value
     for copy in copies:
         copy.wait()
+
+
+def blocks_kernel(heads, runs, normed_ref, block_ref):
+    mine = lax.rem(lax.axis_index("seq"), heads)
+    group = CHUNK // LANES
+    for chunk in range(normed_ref.shape[0]):
+        split = normed_ref[chunk].astype(f32).reshape(runs, group, CHUNK // (runs * group), LANES)
+        for i in range(group):
+            step = jnp.bitwise_xor(mine, chunk * group + i)
+            at = jnp.bitwise_and(step, 1) * (heads // 2) + lax.div(step, 2)
+            block_ref[at] = split[:, i].reshape(LANES, LANES).astype(bf16)
 
 
 def final_kernel(
@@ -562,14 +577,14 @@
     square = (chunks, CHUNK, CHUNK)
     states = (chunks, LANES + 8, LANES)
     unit = 2 * chunks * CHUNK * LANES
-    order, reached, chosen = call(
+    order, reached = call(
         functools.partial(plan_kernel, heads, chunks, peers),
-        (shape(*square, dtype=bf16), shape(*square, dtype=bf16), shape(*tall, dtype=bf16)),
+        (shape(*square, dtype=bf16), shape(*square, dtype=bf16)),
         (place,),
         flops=unit * 256,
         moved=4 * chunks * CHUNK * CHUNK,
         in_specs=[VMEM],
-        out_specs=[VMEM] * 3,
+        out_specs=[VMEM] * 2,
     )
     last, keep, running, count, leave = call(
         functools.partial(state_kernel, heads, chunks),
@@ -577,10 +592,10 @@
             shape(LANES, LANES, dtype=bf16), shape(*states), shape(*tall), shape(*tall),
             shape(*tall),
         ),
-        (arrived, meta, order, reached, chosen),
+        (arrived, meta, order, reached),
         flops=unit * 512,
         moved=2 * arrived.size,
-        in_specs=[VMEM] * 5,
+        in_specs=[VMEM] * 4,
         out_specs=[VMEM] * 5,
     )
     gain = keep[-1, LANES : LANES + 1] * keep[-1, LANES + 1 : LANES + 2]
@@ -588,16 +603,16 @@
     came = carried(last, gain, segments, heads, 1)
     mix, weights, inner, enter, normal = call(
         functools.partial(inner_kernel, heads, chunks, runs),
-        (shape(*square), shape(*square, dtype=bf16), shape(*tall), shape(*tall), shape(*tall)),
-        (arrived, order, running, count, keep, *normal),
+        (
+            shape(*square), shape(*square, dtype=bf16), shape(*tall), shape(*tall),
+            shape(chunks, runs, CHUNK // runs, LANES),
+        ),
+        (arrived, order, running, count, keep, *(piece.reshape(-1, runs, rows // runs, LANES) for piece in normal)),
         flops=unit * 1024,
         moved=2 * arrived.size + 8 * chunks * CHUNK * CHUNK,
         in_specs=[VMEM] * 5 + [ANY] * len(normal),
         out_specs=[VMEM] * 5,
-        scratch_shapes=[
-            pltpu.VMEM((heads, rows, LANES), f32),
-            pltpu.SemaphoreType.DMA((heads,)),
-        ],
+        scratch_shapes=[pltpu.SemaphoreType.DMA((heads,))],
     )
     grad, normed, back, last = call(
         functools.partial(output_kernel, heads, chunks),
@@ -613,14 +628,14 @@
     )
     came_back = carried(last, gain, segments, heads, -1)
     full = shape(16, 3 * chunks * 16, LANES, dtype=bf16)
-    grads, part, normed = call(
-        functools.partial(local_kernel, heads, chunks, runs),
-        (full, shape(2, *tall), shape(heads, rows, LANES, dtype=bf16)),
-        (arrived, mix, weights, enter, leave, keep, back, came, grad, normed),
+    grads, part = call(
+        functools.partial(local_kernel, heads, chunks),
+        (full, shape(2, *tall)),
+        (arrived, mix, weights, enter, leave, keep, back, came, grad),
         flops=unit * 1024,
         moved=2 * arrived.size + 8 * chunks * CHUNK * CHUNK,
-        in_specs=[VMEM] * 10,
-        out_specs=[ANY] + [VMEM] * 2,
+        in_specs=[VMEM] * 9,
+        out_specs=[ANY, VMEM],
         scratch_shapes=[
             pltpu.VMEM((16, chunks * 16, LANES), bf16),
             pltpu.SemaphoreType.DMA((chunks,)),
@@ -641,6 +656,14 @@
         ],
     )
     normed, grads = lax.optimization_barrier((normed, grads))
+    normed = call(
+        functools.partial(blocks_kernel, heads, runs),
+        shape(heads, rows, LANES, dtype=bf16),
+        (normed,),
+        moved=4 * normed.size,
+        in_specs=[VMEM],
+        out_specs=VMEM,
+    )
     if per == 16:
         normed = deal(normed[: heads // 2], normed[heads // 2 :])
     else:

time: 69.6 us -> 69.2 us (level)
  waiting for transfers between devices: 28.3 us -> 29.2 us
  Pallas kernels: 17 us -> 16.3 us
    pallas_call x12 -> x13, Pallas kernels: 14.8 us -> 14.1 us  [call(): pl.pallas_call(body, out_shape=outs, compiler_params=PARAMS, cost_estimat...]
  transfers between devices with their start and end apart: 12 -> 12, of which waited for: 9 -> 8; matrix products, arithmetic and copies ran while one was open for 1% -> 0% of each run, Pallas kernels for 17% -> 16%
where the time goes in v6:
time: 69.2 us; the launch traced here: 68.7 us
  waiting for transfers between devices  29.2 us (42%)
  starting transfers between devices  18.4 us (27%)
  Pallas kernels  16.3 us (24%)
  local copies, waits for them, and re-layouts  3.94 us (6%)
  between operations  0.84 us (1%)
    pallas_call x13, Pallas kernels, call(): pl.pallas_call(body, out_shape=outs, compiler_params=PARAMS, cost_estimat...  14.1 us
    ppermute x8, waiting for transfers between devices, swap(): return lax.ppermute(value, 'seq', [(i, i ^ step) for i in range(peers)])  13.8 us
    all_to_all x2, starting transfers between devices, exchange(): return lax.all_to_all(value, 'seq', split_axis=0, concat_axis=0, tiled=True)  10.5 us
    all_to_all x2, waiting for transfers between devices, exchange(): return lax.all_to_all(value, 'seq', split_axis=0, concat_axis=0, tiled=True)  9.47 us
    ppermute x8, starting transfers between devices, swap(): return lax.ppermute(value, 'seq', [(i, i ^ step) for i in range(peers)])  7.78 us
    ppermute x2, waiting for transfers between devices, carried(): return lax.ppermute(last, 'seq', pairs)  5.95 us
    unnamed x6, local copies, waits for them, and re-layouts  3.88 us
    pallas_call x1, Pallas kernels, pack(): pl.pallas_call(functools.partial(pack_kernel, heads, segments), out_shape...  2.19 us
  transfers between devices with their start and end apart: 12, of which 8 were waited for; matrix products, arithmetic and copies ran while one was open for 0% of the time, Pallas kernels for 16%

profile of v6, /device:TPU:18, one launch (start us, length us, event | category | flops | bytes accessed | tf_op | source)
XLA Modules:
  0.0 68.7 jit_solution(3599791583343805396)
XLA Ops:
  0.6 2.2 %shard_map.77 = bf16[16,200,128]{2,1,0:T(8,128)(2,1)} custom-call(bf16[128,3072]{1,0:T(8,128)(2,1)} %rows_ref.1, bf16[8,128]{1,0:T(8,128)(2,1)} %bitcast.15, s32[1,128]{1,0:T(1,128)} %bitcast.16), custom_call_target="tpu_custom_call" | custom-call | tf_op jit(solution)/shard_map/pallas_call | solution.py:117
  2.8 6.2 %all-to-all-start = ((bf16[16,200,128]{2,1,0:T(8,128)(2,1)}), bf16[16,200,128]{2,1,0:T(8,128)(2,1)S(1)}, u32[]{:S(2)}, u32[]{:S(2)}) async-start(bf16[16,200,128]{2,1,0:T(8,128)(2,1)} %shard_map.77), calls=%async_computation | async-start | bytes 1638400 | tf_op jit(solution)/shard_map/all_to_all | solution.py:533
  9.0 2.2 %copy-done = bf16[1024,2048]{1,0:T(8,128)(2,1)S(1)} copy-done((bf16[1024,2048]{1,0:T(8,128)(2,1)S(1)}, bf16[1024,2048]{1,0:T(8,128)(2,1)}, u32[]{:S(2)}) %copy-start) | copy-done | bytes 4194328
  11.2 1.0 %copy-done.1 = bf16[128,2048]{1,0:T(8,128)(2,1)S(1)} copy-done((bf16[128,2048]{1,0:T(8,128)(2,1)S(1)}, bf16[128,2048]{1,0:T(8,128)(2,1)}, u32[]{:S(2)}) %copy-start.1) | copy-done | bytes 524312
  12.3 0.7 copy-done.2
  12.9 1.5 %shard_map.80 = (f32[4,128,128]{2,1,0:T(8,128)S(1)}, f32[4,128,128]{2,1,0:T(8,128)S(1)}, bf16[128,2048]{1,0:T(8,128)(2,1)S(1)}) custom-call(bf16[128,2048]{1,0:T(8,128)(2,1)S(1)} %copy-done.1, s32[1,128]{1,0:T(1,128)S(1)} %bitcast.13, bf16[1024,2048]{1,0:T(8,128)(2,1)S(1)} %copy-done), custom_call_target="tpu_custom_call" | custom-call | flops 536870912 | bytes 5242880 | tf_op jit(solution)/shard_map/pallas_call | solution.py:54
  14.7 1.4 %collective-permute-done = f32[4,128,128]{2,1,0:T(8,128)S(1)} collective-permute-done((f32[4,128,128]{2,1,0:T(8,128)S(1)}, f32[4,128,128]{2,1,0:T(8,128)S(1)}, u32[]{:S(2)}, u32[]{:S(2)}) %collective-permute-start) | collective-permute-done | bytes 262176 | tf_op jit(solution)/shard_map/ppermute | solution.py:547
  16.1 1.5 %collective-permute-start.1 = (f32[2,128,128]{2,1,0:T(8,128)S(1)}, f32[2,128,128]{2,1,0:T(8,128)S(1)}, u32[]{:S(2)}, u32[]{:S(2)}) collective-permute-start(f32[2,128,128]{2,1,0:T(8,128)S(1)} %pad_maximum_fusion), channel_id=1, source_target_pairs={{0,2},{1,3},{2,0},{3,1},{4,6},{5,7},{6,4},{7,5},{8,10},{9,11},{10,... | collective-permute-start | bytes 393224 | tf_op jit(solution)/shard_map/ppermute | solution.py:547
  17.6 1.5 %collective-permute-start.2 = (f32[2,128,128]{2,1,0:T(8,128)S(1)}, f32[2,128,128]{2,1,0:T(8,128)S(1)}, u32[]{:S(2)}, u32[]{:S(2)}) collective-permute-start(f32[2,128,128]{2,1,0:T(8,128)S(1)} %pad_maximum_fusion.1), channel_id=1, source_target_pairs={{0,4},{1,5},{2,6},{3,7},{4,0},{5,1},{6,2},{7,3},{8,12},{9,13},{10,... | collective-permute-start | bytes 393224 | tf_op jit(solution)/shard_map/ppermute | solution.py:547
  19.2 0.6 collective-permute-start.3
  19.8 0.5 shard_map.78
  20.3 9.5 %all-to-all-done.rows_ref.meta_ref = bf16[16,200,128]{2,1,0:T(8,128)(2,1)S(1)} async-done(((bf16[16,200,128]{2,1,0:T(8,128)(2,1)}), bf16[16,200,128]{2,1,0:T(8,128)(2,1)S(1)}, u32[]{:S(2)}, u32[]{:S(2)}) %all-to-all-start) | async-done | bytes 819232 | tf_op jit(solution)/shard_map/all_to_all | solution.py:533
  29.8 1.3 %shard_map.79 = (bf16[128,128]{1,0:T(8,128)(2,1)S(1)}, f32[4,136,128]{2,1,0:T(8,128)S(1)}, f32[4,256,128]{2,1,0:T(8,128)S(1)}, f32[4,256,128]{2,1,0:T(8,128)S(1)}, f32[4,256,128]{2,1,0:T(8,128)S(1)}) custom-call(bf16[16,200,128]{2,1,0:T(8,128)(2,1)S(1)} %all-to-all-done.rows_ref.meta_ref, bf16[16,200,128]{2,1,0:T(8,128)(2,1)S(1)} %all-to-all-done.rows_ref.meta_ref, ...), custom_call_target="tpu_custom_call" | custom-call | flops 134217728 | bytes 819200 | tf_op jit(solution)/shard_map/pallas_call | solution.py:54
  31.2 0.7 %collective-permute-done.3 = f32[2,128,128]{2,1,0:T(8,128)S(1)} collective-permute-done((f32[2,128,128]{2,1,0:T(8,128)S(1)}, f32[2,128,128]{2,1,0:T(8,128)S(1)}, u32[]{:S(2)}, u32[]{:S(2)}) %collective-permute-start.3) | collective-permute-done | bytes 131104 | tf_op jit(solution)/shard_map/ppermute | solution.py:547
  31.9 1.0 %shard_map.81 = (f32[4,256,256]{2,1,0:T(8,128)S(1)}, bf16[4,256,256]{2,1,0:T(8,128)(2,1)S(1)}, f32[4,256,128]{2,1,0:T(8,128)S(1)}, f32[4,256,128]{2,1,0:T(8,128)S(1)}, f32[4,16,16,128]{3,2,1,0:T(8,128)S(1)}) custom-call(bf16[16,200,128]{2,1,0:T(8,128)(2,1)S(1)} %all-to-all-done.rows_ref.meta_ref, bf16[4,256,256]{2,1,0:T(8,128)(2,1)S(1)} %get-tuple-element.25.order_ref, ...), custom_call_target="tpu_custom_call" | custom-call | flops 268435456 | bytes 2916352 | tf_op jit(solution)/shard_map/pallas_call | solution.py:54
  33.0 3.0 %collective-permute-done.4.came_ref = bf16[128,128]{1,0:T(8,128)(2,1)S(1)} collective-permute-done((bf16[128,128]{1,0:T(8,128)(2,1)S(1)}, bf16[128,128]{1,0:T(8,128)(2,1)S(1)}, u32[]{:S(2)}, u32[]{:S(2)}) %collective-permute-start.4) | collective-permute-done | bytes 32800 | tf_op jit(solution)/shard_map/ppermute | solution.py:499
  36.0 0.8 %shard_map.82 = (bf16[4,256,128]{2,1,0:T(8,128)(2,1)S(1)}, bf16[4,256,128]{2,1,0:T(8,128)(2,1)S(1)}, f32[4,136,128]{2,1,0:T(8,128)S(1)}, bf16[128,128]{1,0:T(8,128)(2,1)S(1)}) custom-call(bf16[16,200,128]{2,1,0:T(8,128)(2,1)S(1)} %all-to-all-done.rows_ref.meta_ref, f32[4,256,128]{2,1,0:T(8,128)S(1)} %get-tuple-element.32.inner_ref, ...), custom_call_target="tpu_custom_call" | custom-call | flops 268435456 | bytes 1867776 | tf_op jit(solution)/shard_map/pallas_call | solution.py:54
  36.8 1.9 %shard_map.83 = (bf16[16,192,128]{2,1,0:T(8,128)(2,1)}, f32[2,4,256,128]{3,2,1,0:T(8,128)S(1)}) custom-call(bf16[16,200,128]{2,1,0:T(8,128)(2,1)S(1)} %all-to-all-done.rows_ref.meta_ref, f32[4,256,256]{2,1,0:T(8,128)S(1)} %get-tuple-element.38.mix_ref, bf16[4,256,256]{2,1,0:T(8,128)(2,1)S(1)} %get-tuple-element.39.weights_ref, ...), custom_call_target="tpu_custom_call" | custom-call | flops 268435456 | bytes 2916352 | tf_op jit(solution)/shard_map/pallas_call | solution.py:54
  38.7 2.9 %collective-permute-done.5.came_ref = bf16[128,128]{1,0:T(8,128)(2,1)S(1)} collective-permute-done((bf16[128,128]{1,0:T(8,128)(2,1)S(1)}, bf16[128,128]{1,0:T(8,128)(2,1)S(1)}, u32[]{:S(2)}, u32[]{:S(2)}) %collective-permute-start.5) | collective-permute-done | bytes 32800 | tf_op jit(solution)/shard_map/ppermute | solution.py:499
  41.6 1.0 %shard_map.84 = bf16[16,192,128]{2,1,0:T(8,128)(2,1)} custom-call(bf16[16,200,128]{2,1,0:T(8,128)(2,1)S(1)} %all-to-all-done.rows_ref.meta_ref, f32[4,256,128]{2,1,0:T(8,128)S(1)} %get-tuple-element.37.leave_ref, f32[2,4,256,128]{3,2,1,0:T(8,128)S(1)} %get-tuple-element.42.part_ref, ...), custom_call_target="tpu_custom_call", output_to_operand_aliasing={{}: (5, {})} | custom-call | flops 134217728 | bytes 1638400 | tf_op jit(solution)/shard_map/pallas_call | solution.py:54
  42.7 4.3 %all-to-all-start.1 = ((bf16[16,192,128]{2,1,0:T(8,128)(2,1)}), bf16[16,192,128]{2,1,0:T(8,128)(2,1)S(1)}, u32[]{:S(2)}, u32[]{:S(2)}) async-start(bf16[16,192,128]{2,1,0:T(8,128)(2,1)} %shard_map.84), calls=%async_computation.1 | async-start | bytes 1572864 | tf_op jit(solution)/shard_map/all_to_all | solution.py:533
  47.3 1.2 %collective-permute-done.6 = bf16[4,128,128]{2,1,0:T(8,128)(2,1)S(1)} collective-permute-done((bf16[4,128,128]{2,1,0:T(8,128)(2,1)S(1)}, bf16[4,128,128]{2,1,0:T(8,128)(2,1)S(1)}, u32[]{:S(2)}, u32[]{:S(2)}) %collective-permute-start.6) | collective-permute-done | bytes 131104 | tf_op jit(solution)/shard_map/ppermute | solution.py:547
  48.5 2.4 %collective-permute-start.8 = (bf16[2,128,128]{2,1,0:T(8,128)(2,1)S(1)}, bf16[2,128,128]{2,1,0:T(8,128)(2,1)S(1)}, u32[]{:S(2)}, u32[]{:S(2)}) collective-permute-start(bf16[2,128,128]{2,1,0:T(8,128)(2,1)S(1)} %pad_maximum_fusion.4), channel_id=1, source_target_pairs={{0,6},{1,7},{2,4},{3,5},{4,2},{5,3},{6,0},{7,1},{8,14},{9,15},{10,... | collective-permute-start | bytes 196616 | tf_op jit(solution)/shard_map/ppermute | solution.py:547
  51.0 0.6 collective-permute-start.9
  51.6 0.6 collective-permute-start.7
  52.2 1.3 %shard_map.87.refs_2_ = bf16[1024,2048]{1,0:T(8,128)(2,1)} custom-call(bf16[1,128,128]{2,1,0:T(8,128)(2,1)S(1)} %get-tuple-element.48.refs_0_, bf16[1,128,128]{2,1,0:T(8,128)(2,1)S(1)} %get-tuple-element.60.refs_1_, bf16[128,2048]{1,0:T(8,128)(2,1)S(1)} %get-tuple-element.47.refs_2_.refs_1_), custom_call_target="tpu_custom_call" | custom-call | flops 134217728 | bytes 1048576 | tf_op jit(solution)/shard_map/pallas_call | solution.py:54
  53.5 2.4 %collective-permute-done.9.refs_0_ = bf16[2,128,128]{2,1,0:T(8,128)(2,1)S(1)} collective-permute-done((bf16[2,128,128]{2,1,0:T(8,128)(2,1)S(1)}, bf16[2,128,128]{2,1,0:T(8,128)(2,1)S(1)}, u32[]{:S(2)}, u32[]{:S(2)}) %collective-permute-start.9) | collective-permute-done | bytes 65568 | tf_op jit(solution)/shard_map/ppermute | solution.py:547
  55.9 1.3 %shard_map.88.refs_2_ = bf16[1024,2048]{1,0:T(8,128)(2,1)} custom-call(bf16[2,128,128]{2,1,0:T(8,128)(2,1)S(1)} %collective-permute-done.9.refs_0_, bf16[128,2048]{1,0:T(8,128)(2,1)S(1)} %get-tuple-element.47.refs_2_.refs_1_, bf16[1024,2048]{1,0:T(8,128)(2,1)} %shard_map.87.refs_2_), custom_call_target="tpu_custom_call", output_to_operand_aliasing={{}: (2, {})} | custom-call | flops 134217728 | bytes 1048576 | tf_op jit(solution)/shard_map/pallas_call | solution.py:54
  57.2 8.1 %collective-permute-done.8.refs_0_ = bf16[2,128,128]{2,1,0:T(8,128)(2,1)S(1)} collective-permute-done((bf16[2,128,128]{2,1,0:T(8,128)(2,1)S(1)}, bf16[2,128,128]{2,1,0:T(8,128)(2,1)S(1)}, u32[]{:S(2)}, u32[]{:S(2)}) %collective-permute-start.8) | collective-permute-done | bytes 65568 | tf_op jit(solution)/shard_map/ppermute | solution.py:547
  65.2 1.3 %shard_map.89.refs_2_ = bf16[1024,2048]{1,0:T(8,128)(2,1)} custom-call(bf16[2,128,128]{2,1,0:T(8,128)(2,1)S(1)} %collective-permute-done.8.refs_0_, bf16[128,2048]{1,0:T(8,128)(2,1)S(1)} %get-tuple-element.47.refs_2_.refs_1_, bf16[1024,2048]{1,0:T(8,128)(2,1)} %shard_map.88.refs_2_), custom_call_target="tpu_custom_call", output_to_operand_aliasing={{}: (2, {})} | custom-call | flops 134217728 | bytes 1048576 | tf_op jit(solution)/shard_map/pallas_call | solution.py:54
  66.5 1.3 %shard_map.90 = bf16[1024,2048]{1,0:T(8,128)(2,1)} custom-call(bf16[2,128,128]{2,1,0:T(8,128)(2,1)S(1)} %collective-permute-done.7.refs_0_, bf16[128,2048]{1,0:T(8,128)(2,1)S(1)} %get-tuple-element.47.refs_2_.refs_1_, bf16[1024,2048]{1,0:T(8,128)(2,1)} %shard_map.89.refs_2_), custom_call_target="tpu_custom_call", output_to_operand_aliasing={{}: (2, {})} | custom-call | flops 134217728 | bytes 1048576 | tf_op jit(solution)/shard_map/pallas_call | solution.py:54
  67.8 1.0 %shard_map.85 = bf16[128,3072]{1,0:T(8,128)(2,1)} custom-call(bf16[16,192,128]{2,1,0:T(8,128)(2,1)S(1)} %all-to-all-done.1.in_ref), custom_call_target="tpu_custom_call" | custom-call | bytes 1572864 | tf_op jit(solution)/shard_map/pallas_call | solution.py:54
  (23 shorter events, 0.8 us)
Async XLA Ops:
  2.8 26.9 %all-to-all-start = ((bf16[16,200,128]{2,1,0:T(8,128)(2,1)}), bf16[16,200,128]{2,1,0:T(8,128)(2,1)S(1)}, u32[]{:S(2)}, u32[]{:S(2)}) async-start(bf16[16,200,128]{2,1,0:T(8,128)(2,1)} %shard_map.77), calls=%async_computation | async-start | bytes 1638400 | tf_op jit(solution)/shard_map/all_to_all | solution.py:533
  9.0 2.2 %copy-start = (bf16[1024,2048]{1,0:T(8,128)(2,1)S(1)}, bf16[1024,2048]{1,0:T(8,128)(2,1)}, u32[]{:S(2)}) copy-start(bf16[1024,2048]{1,0:T(8,128)(2,1)} %weight_ref.1) | copy-start | bytes 12582916
  11.2 1.0 %copy-start.1 = (bf16[128,2048]{1,0:T(8,128)(2,1)S(1)}, bf16[128,2048]{1,0:T(8,128)(2,1)}, u32[]{:S(2)}) copy-start(bf16[128,2048]{1,0:T(8,128)(2,1)} %up_ref.1) | copy-start | bytes 1572868
  12.3 0.7 copy-start.2
  14.4 1.6 %collective-permute-start = (f32[4,128,128]{2,1,0:T(8,128)S(1)}, f32[4,128,128]{2,1,0:T(8,128)S(1)}, u32[]{:S(2)}, u32[]{:S(2)}) collective-permute-start(f32[4,128,128]{2,1,0:T(8,128)S(1)} %get-tuple-element.31), channel_id=1, source_target_pairs={{0,1},{1,0},{2,3},{3,2},{4,5},{5,4},{6,7},{7,6},{8,9},{9,8},{10,11... | collective-permute-start | bytes 786440 | tf_op jit(solution)/shard_map/ppermute | solution.py:547
  16.1 15.1 %collective-permute-start.1 = (f32[2,128,128]{2,1,0:T(8,128)S(1)}, f32[2,128,128]{2,1,0:T(8,128)S(1)}, u32[]{:S(2)}, u32[]{:S(2)}) collective-permute-start(f32[2,128,128]{2,1,0:T(8,128)S(1)} %pad_maximum_fusion), channel_id=1, source_target_pairs={{0,2},{1,3},{2,0},{3,1},{4,6},{5,7},{6,4},{7,5},{8,10},{9,11},{10,... | collective-permute-start | bytes 393224 | tf_op jit(solution)/shard_map/ppermute | solution.py:547
  17.6 13.6 %collective-permute-start.2 = (f32[2,128,128]{2,1,0:T(8,128)S(1)}, f32[2,128,128]{2,1,0:T(8,128)S(1)}, u32[]{:S(2)}, u32[]{:S(2)}) collective-permute-start(f32[2,128,128]{2,1,0:T(8,128)S(1)} %pad_maximum_fusion.1), channel_id=1, source_target_pairs={{0,4},{1,5},{2,6},{3,7},{4,0},{5,1},{6,2},{7,3},{8,12},{9,13},{10,... | collective-permute-start | bytes 393224 | tf_op jit(solution)/shard_map/ppermute | solution.py:547
  19.2 12.7 %collective-permute-start.3 = (f32[2,128,128]{2,1,0:T(8,128)S(1)}, f32[2,128,128]{2,1,0:T(8,128)S(1)}, u32[]{:S(2)}, u32[]{:S(2)}) collective-permute-start(f32[2,128,128]{2,1,0:T(8,128)S(1)} %pad_maximum_fusion.2), channel_id=1, source_target_pairs={{0,6},{1,7},{2,4},{3,5},{4,2},{5,3},{6,0},{7,1},{8,14},{9,15},{10,... | collective-permute-start | bytes 393224 | tf_op jit(solution)/shard_map/ppermute | solution.py:547
  31.1 4.9 %collective-permute-start.4 = (bf16[128,128]{1,0:T(8,128)(2,1)S(1)}, bf16[128,128]{1,0:T(8,128)(2,1)S(1)}, u32[]{:S(2)}, u32[]{:S(2)}) collective-permute-start(bf16[128,128]{1,0:T(8,128)(2,1)S(1)} %get-tuple-element.35), channel_id=1, source_target_pairs={{0,8},{1,9},{2,10},{3,11},{4,12},{5,13},{6,14},{7,15},{8,0},{9,1},... | collective-permute-start | bytes 98312 | tf_op jit(solution)/shard_map/ppermute | solution.py:499
  36.8 4.9 %collective-permute-start.5 = (bf16[128,128]{1,0:T(8,128)(2,1)S(1)}, bf16[128,128]{1,0:T(8,128)(2,1)S(1)}, u32[]{:S(2)}, u32[]{:S(2)}) collective-permute-start(bf16[128,128]{1,0:T(8,128)(2,1)S(1)} %get-tuple-element.43), channel_id=1, source_target_pairs={{0,8},{1,9},{2,10},{3,11},{4,12},{5,13},{6,14},{7,15},{8,0},{9,1},... | collective-permute-start | bytes 98312 | tf_op jit(solution)/shard_map/ppermute | solution.py:499
  42.7 25.1 %all-to-all-start.1 = ((bf16[16,192,128]{2,1,0:T(8,128)(2,1)}), bf16[16,192,128]{2,1,0:T(8,128)(2,1)S(1)}, u32[]{:S(2)}, u32[]{:S(2)}) async-start(bf16[16,192,128]{2,1,0:T(8,128)(2,1)} %shard_map.84), calls=%async_computation.1 | async-start | bytes 1572864 | tf_op jit(solution)/shard_map/all_to_all | solution.py:533
  47.1 1.4 %collective-permute-start.6 = (bf16[4,128,128]{2,1,0:T(8,128)(2,1)S(1)}, bf16[4,128,128]{2,1,0:T(8,128)(2,1)S(1)}, u32[]{:S(2)}, u32[]{:S(2)}) collective-permute-start(bf16[4,128,128]{2,1,0:T(8,128)(2,1)S(1)} %slice.78), channel_id=1, source_target_pairs={{0,1},{1,0},{2,3},{3,2},{4,5},{5,4},{6,7},{7,6},{8,9},{9,8},{10,11... | collective-permute-start | bytes 393224 | tf_op jit(solution)/shard_map/ppermute | solution.py:547
  48.5 16.7 %collective-permute-start.8 = (bf16[2,128,128]{2,1,0:T(8,128)(2,1)S(1)}, bf16[2,128,128]{2,1,0:T(8,128)(2,1)S(1)}, u32[]{:S(2)}, u32[]{:S(2)}) collective-permute-start(bf16[2,128,128]{2,1,0:T(8,128)(2,1)S(1)} %pad_maximum_fusion.4), channel_id=1, source_target_pairs={{0,6},{1,7},{2,4},{3,5},{4,2},{5,3},{6,0},{7,1},{8,14},{9,15},{10,... | collective-permute-start | bytes 196616 | tf_op jit(solution)/shard_map/ppermute | solution.py:547
  51.0 4.9 %collective-permute-start.9 = (bf16[2,128,128]{2,1,0:T(8,128)(2,1)S(1)}, bf16[2,128,128]{2,1,0:T(8,128)(2,1)S(1)}, u32[]{:S(2)}, u32[]{:S(2)}) collective-permute-start(bf16[2,128,128]{2,1,0:T(8,128)(2,1)S(1)} %pad_maximum_fusion.5), channel_id=1, source_target_pairs={{0,2},{1,3},{2,0},{3,1},{4,6},{5,7},{6,4},{7,5},{8,10},{9,11},{10,... | collective-permute-start | bytes 196616 | tf_op jit(solution)/shard_map/ppermute | solution.py:547
  51.6 14.9 %collective-permute-start.7 = (bf16[2,128,128]{2,1,0:T(8,128)(2,1)S(1)}, bf16[2,128,128]{2,1,0:T(8,128)(2,1)S(1)}, u32[]{:S(2)}, u32[]{:S(2)}) collective-permute-start(bf16[2,128,128]{2,1,0:T(8,128)(2,1)S(1)} %pad_maximum_fusion.3), channel_id=1, source_target_pairs={{0,4},{1,5},{2,6},{3,7},{4,0},{5,1},{6,2},{7,3},{8,12},{9,13},{10,... | collective-permute-start | bytes 196616 | tf_op jit(solution)/shard_map/ppermute | solution.py:547

commit v7 on v6

--- a/solution.py
+++ b/solution.py
@@ -82,11 +82,12 @@
     spots = CHUNK // peers
     first = lax.rem(lax.axis_index("seq") * spots, LANES)
     line = iota((META, LANES), 0)
-    row, spot = iota((LANES, LANES), 0), iota((LANES, LANES), 1) - first
+    spot = iota((heads, LANES), 1) - first
+    mine = (spot >= 0) & (spot < spots)
     placed = []
     for i in range(segments * chunks):
-        pick = (spot >= 0) & (spot < spots) & (row == i * spots + spot)
-        placed.append(dot(decay[...], jnp.where(pick, 1.0, 0.0).astype(bf16)))
+        turn = lax.rem(first + LANES - i * spots, LANES)
+        placed.append(jnp.where(mine, pltpu.roll(decay[...].astype(f32), turn, 1), 0.0))
     leaving = []
     for segment in range(segments):
         for copy in arriving[2 + 2 * segment : 4 + 2 * segment]:
@@ -655,7 +656,6 @@
             pltpu.SemaphoreType.DMA((2 * chunks,)),
         ],
     )
-    normed, grads = lax.optimization_barrier((normed, grads))
     normed = call(
         functools.partial(blocks_kernel, heads, runs),
         shape(heads, rows, LANES, dtype=bf16),

time: 69.2 us -> 69.2 us (level)
  no operation moved by 1% of the time
where the time goes in v7:
time: 69.2 us; the launch traced here: 68.7 us
  waiting for transfers between devices  29.2 us (42%)
  starting transfers between devices  18.4 us (27%)
  Pallas kernels  16.3 us (24%)
  local copies, waits for them, and re-layouts  3.94 us (6%)
  between operations  0.84 us (1%)
    pallas_call x13, Pallas kernels, call(): pl.pallas_call(body, out_shape=outs, compiler_params=PARAMS, cost_estimat...  14.1 us
    ppermute x8, waiting for transfers between devices, swap(): return lax.ppermute(value, 'seq', [(i, i ^ step) for i in range(peers)])  13.8 us
    all_to_all x2, starting transfers between devices, exchange(): return lax.all_to_all(value, 'seq', split_axis=0, concat_axis=0, tiled=True)  10.5 us
    all_to_all x2, waiting for transfers between devices, exchange(): return lax.all_to_all(value, 'seq', split_axis=0, concat_axis=0, tiled=True)  9.47 us
    ppermute x8, starting transfers between devices, swap(): return lax.ppermute(value, 'seq', [(i, i ^ step) for i in range(peers)])  7.78 us
    ppermute x2, waiting for transfers between devices, carried(): return lax.ppermute(last, 'seq', pairs)  5.95 us
    unnamed x6, local copies, waits for them, and re-layouts  3.88 us
    pallas_call x1, Pallas kernels, pack(): pl.pallas_call(functools.partial(pack_kernel, heads, segments), out_shape...  2.19 us
  transfers between devices with their start and end apart: 12, of which 8 were waited for; matrix products, arithmetic and copies ran while one was open for 0% of the time, Pallas kernels for 16%

profile of v7, /device:TPU:18, one launch (start us, length us, event | category | flops | bytes accessed | tf_op | source)
XLA Modules:
  0.0 68.7 jit_solution(5478975597595786230)
XLA Ops:
  0.6 2.2 %shard_map.77 = bf16[16,200,128]{2,1,0:T(8,128)(2,1)} custom-call(bf16[128,3072]{1,0:T(8,128)(2,1)} %rows_ref.1, bf16[8,128]{1,0:T(8,128)(2,1)} %bitcast.15, s32[1,128]{1,0:T(1,128)} %bitcast.16), custom_call_target="tpu_custom_call" | custom-call | tf_op jit(solution)/shard_map/pallas_call | solution.py:118
  2.8 6.2 %all-to-all-start = ((bf16[16,200,128]{2,1,0:T(8,128)(2,1)}), bf16[16,200,128]{2,1,0:T(8,128)(2,1)S(1)}, u32[]{:S(2)}, u32[]{:S(2)}) async-start(bf16[16,200,128]{2,1,0:T(8,128)(2,1)} %shard_map.77), calls=%async_computation | async-start | bytes 1638400 | tf_op jit(solution)/shard_map/all_to_all | solution.py:534
  9.0 2.2 %copy-done = bf16[1024,2048]{1,0:T(8,128)(2,1)S(1)} copy-done((bf16[1024,2048]{1,0:T(8,128)(2,1)S(1)}, bf16[1024,2048]{1,0:T(8,128)(2,1)}, u32[]{:S(2)}) %copy-start) | copy-done | bytes 4194328
  11.2 1.0 %copy-done.1 = bf16[128,2048]{1,0:T(8,128)(2,1)S(1)} copy-done((bf16[128,2048]{1,0:T(8,128)(2,1)S(1)}, bf16[128,2048]{1,0:T(8,128)(2,1)}, u32[]{:S(2)}) %copy-start.1) | copy-done | bytes 524312
  12.3 0.7 copy-done.2
  12.9 1.5 %shard_map.80 = (f32[4,128,128]{2,1,0:T(8,128)S(1)}, f32[4,128,128]{2,1,0:T(8,128)S(1)}, bf16[128,2048]{1,0:T(8,128)(2,1)S(1)}) custom-call(bf16[128,2048]{1,0:T(8,128)(2,1)S(1)} %copy-done.1, s32[1,128]{1,0:T(1,128)S(1)} %bitcast.13, bf16[1024,2048]{1,0:T(8,128)(2,1)S(1)} %copy-done), custom_call_target="tpu_custom_call" | custom-call | flops 536870912 | bytes 5242880 | tf_op jit(solution)/shard_map/pallas_call | solution.py:54
  14.7 1.4 %collective-permute-done = f32[4,128,128]{2,1,0:T(8,128)S(1)} collective-permute-done((f32[4,128,128]{2,1,0:T(8,128)S(1)}, f32[4,128,128]{2,1,0:T(8,128)S(1)}, u32[]{:S(2)}, u32[]{:S(2)}) %collective-permute-start) | collective-permute-done | bytes 262176 | tf_op jit(solution)/shard_map/ppermute | solution.py:548
  16.1 1.5 %collective-permute-start.1 = (f32[2,128,128]{2,1,0:T(8,128)S(1)}, f32[2,128,128]{2,1,0:T(8,128)S(1)}, u32[]{:S(2)}, u32[]{:S(2)}) collective-permute-start(f32[2,128,128]{2,1,0:T(8,128)S(1)} %pad_maximum_fusion), channel_id=1, source_target_pairs={{0,2},{1,3},{2,0},{3,1},{4,6},{5,7},{6,4},{7,5},{8,10},{9,11},{10,... | collective-permute-start | bytes 393224 | tf_op jit(solution)/shard_map/ppermute | solution.py:548
  17.6 1.5 %collective-permute-start.2 = (f32[2,128,128]{2,1,0:T(8,128)S(1)}, f32[2,128,128]{2,1,0:T(8,128)S(1)}, u32[]{:S(2)}, u32[]{:S(2)}) collective-permute-start(f32[2,128,128]{2,1,0:T(8,128)S(1)} %pad_maximum_fusion.1), channel_id=1, source_target_pairs={{0,4},{1,5},{2,6},{3,7},{4,0},{5,1},{6,2},{7,3},{8,12},{9,13},{10,... | collective-permute-start | bytes 393224 | tf_op jit(solution)/shard_map/ppermute | solution.py:548
  19.2 0.6 collective-permute-start.3
  19.8 0.5 shard_map.78
  20.3 9.5 %all-to-all-done.rows_ref.meta_ref = bf16[16,200,128]{2,1,0:T(8,128)(2,1)S(1)} async-done(((bf16[16,200,128]{2,1,0:T(8,128)(2,1)}), bf16[16,200,128]{2,1,0:T(8,128)(2,1)S(1)}, u32[]{:S(2)}, u32[]{:S(2)}) %all-to-all-start) | async-done | bytes 819232 | tf_op jit(solution)/shard_map/all_to_all | solution.py:534
  29.8 1.3 %shard_map.79 = (bf16[128,128]{1,0:T(8,128)(2,1)S(1)}, f32[4,136,128]{2,1,0:T(8,128)S(1)}, f32[4,256,128]{2,1,0:T(8,128)S(1)}, f32[4,256,128]{2,1,0:T(8,128)S(1)}, f32[4,256,128]{2,1,0:T(8,128)S(1)}) custom-call(bf16[16,200,128]{2,1,0:T(8,128)(2,1)S(1)} %all-to-all-done.rows_ref.meta_ref, bf16[16,200,128]{2,1,0:T(8,128)(2,1)S(1)} %all-to-all-done.rows_ref.meta_ref, ...), custom_call_target="tpu_custom_call" | custom-call | flops 134217728 | bytes 819200 | tf_op jit(solution)/shard_map/pallas_call | solution.py:54
  31.2 0.7 %collective-permute-done.3 = f32[2,128,128]{2,1,0:T(8,128)S(1)} collective-permute-done((f32[2,128,128]{2,1,0:T(8,128)S(1)}, f32[2,128,128]{2,1,0:T(8,128)S(1)}, u32[]{:S(2)}, u32[]{:S(2)}) %collective-permute-start.3) | collective-permute-done | bytes 131104 | tf_op jit(solution)/shard_map/ppermute | solution.py:548
  31.9 1.0 %shard_map.81 = (f32[4,256,256]{2,1,0:T(8,128)S(1)}, bf16[4,256,256]{2,1,0:T(8,128)(2,1)S(1)}, f32[4,256,128]{2,1,0:T(8,128)S(1)}, f32[4,256,128]{2,1,0:T(8,128)S(1)}, f32[4,16,16,128]{3,2,1,0:T(8,128)S(1)}) custom-call(bf16[16,200,128]{2,1,0:T(8,128)(2,1)S(1)} %all-to-all-done.rows_ref.meta_ref, bf16[4,256,256]{2,1,0:T(8,128)(2,1)S(1)} %get-tuple-element.23.order_ref, ...), custom_call_target="tpu_custom_call" | custom-call | flops 268435456 | bytes 2916352 | tf_op jit(solution)/shard_map/pallas_call | solution.py:54
  33.0 3.0 %collective-permute-done.4.came_ref = bf16[128,128]{1,0:T(8,128)(2,1)S(1)} collective-permute-done((bf16[128,128]{1,0:T(8,128)(2,1)S(1)}, bf16[128,128]{1,0:T(8,128)(2,1)S(1)}, u32[]{:S(2)}, u32[]{:S(2)}) %collective-permute-start.4) | collective-permute-done | bytes 32800 | tf_op jit(solution)/shard_map/ppermute | solution.py:500
  36.0 0.8 %shard_map.82 = (bf16[4,256,128]{2,1,0:T(8,128)(2,1)S(1)}, bf16[4,256,128]{2,1,0:T(8,128)(2,1)S(1)}, f32[4,136,128]{2,1,0:T(8,128)S(1)}, bf16[128,128]{1,0:T(8,128)(2,1)S(1)}) custom-call(bf16[16,200,128]{2,1,0:T(8,128)(2,1)S(1)} %all-to-all-done.rows_ref.meta_ref, f32[4,256,128]{2,1,0:T(8,128)S(1)} %get-tuple-element.34.inner_ref, ...), custom_call_target="tpu_custom_call" | custom-call | flops 268435456 | bytes 1867776 | tf_op jit(solution)/shard_map/pallas_call | solution.py:54
  36.8 1.9 %shard_map.83 = (bf16[16,192,128]{2,1,0:T(8,128)(2,1)}, f32[2,4,256,128]{3,2,1,0:T(8,128)S(1)}) custom-call(bf16[16,200,128]{2,1,0:T(8,128)(2,1)S(1)} %all-to-all-done.rows_ref.meta_ref, f32[4,256,256]{2,1,0:T(8,128)S(1)} %get-tuple-element.31.mix_ref, bf16[4,256,256]{2,1,0:T(8,128)(2,1)S(1)} %get-tuple-element.32.weights_ref, ...), custom_call_target="tpu_custom_call" | custom-call | flops 268435456 | bytes 2916352 | tf_op jit(solution)/shard_map/pallas_call | solution.py:54
  38.7 2.9 %collective-permute-done.5.came_ref = bf16[128,128]{1,0:T(8,128)(2,1)S(1)} collective-permute-done((bf16[128,128]{1,0:T(8,128)(2,1)S(1)}, bf16[128,128]{1,0:T(8,128)(2,1)S(1)}, u32[]{:S(2)}, u32[]{:S(2)}) %collective-permute-start.5) | collective-permute-done | bytes 32800 | tf_op jit(solution)/shard_map/ppermute | solution.py:500
  41.6 1.0 %shard_map.84 = bf16[16,192,128]{2,1,0:T(8,128)(2,1)} custom-call(bf16[16,200,128]{2,1,0:T(8,128)(2,1)S(1)} %all-to-all-done.rows_ref.meta_ref, f32[4,256,128]{2,1,0:T(8,128)S(1)} %get-tuple-element.25.leave_ref, f32[2,4,256,128]{3,2,1,0:T(8,128)S(1)} %get-tuple-element.39.part_ref, ...), custom_call_target="tpu_custom_call", output_to_operand_aliasing={{}: (5, {})} | custom-call | flops 134217728 | bytes 1638400 | tf_op jit(solution)/shard_map/pallas_call | solution.py:54
  42.7 4.3 %all-to-all-start.1 = ((bf16[16,192,128]{2,1,0:T(8,128)(2,1)}), bf16[16,192,128]{2,1,0:T(8,128)(2,1)S(1)}, u32[]{:S(2)}, u32[]{:S(2)}) async-start(bf16[16,192,128]{2,1,0:T(8,128)(2,1)} %shard_map.84), calls=%async_computation.1 | async-start | bytes 1572864 | tf_op jit(solution)/shard_map/all_to_all | solution.py:534
  47.3 1.2 %collective-permute-done.6 = bf16[4,128,128]{2,1,0:T(8,128)(2,1)S(1)} collective-permute-done((bf16[4,128,128]{2,1,0:T(8,128)(2,1)S(1)}, bf16[4,128,128]{2,1,0:T(8,128)(2,1)S(1)}, u32[]{:S(2)}, u32[]{:S(2)}) %collective-permute-start.6) | collective-permute-done | bytes 131104 | tf_op jit(solution)/shard_map/ppermute | solution.py:548
  48.5 2.4 %collective-permute-start.8 = (bf16[2,128,128]{2,1,0:T(8,128)(2,1)S(1)}, bf16[2,128,128]{2,1,0:T(8,128)(2,1)S(1)}, u32[]{:S(2)}, u32[]{:S(2)}) collective-permute-start(bf16[2,128,128]{2,1,0:T(8,128)(2,1)S(1)} %pad_maximum_fusion.4), channel_id=1, source_target_pairs={{0,6},{1,7},{2,4},{3,5},{4,2},{5,3},{6,0},{7,1},{8,14},{9,15},{10,... | collective-permute-start | bytes 196616 | tf_op jit(solution)/shard_map/ppermute | solution.py:548
  51.0 0.6 collective-permute-start.9
  51.6 0.6 collective-permute-start.7
  52.2 1.3 %shard_map.87.refs_2_ = bf16[1024,2048]{1,0:T(8,128)(2,1)} custom-call(bf16[1,128,128]{2,1,0:T(8,128)(2,1)S(1)} %get-tuple-element.44.refs_0_, bf16[1,128,128]{2,1,0:T(8,128)(2,1)S(1)} %get-tuple-element.56.refs_1_, bf16[128,2048]{1,0:T(8,128)(2,1)S(1)} %get-tuple-element.43.refs_2_.refs_1_), custom_call_target="tpu_custom_call" | custom-call | flops 134217728 | bytes 1048576 | tf_op jit(solution)/shard_map/pallas_call | solution.py:54
  53.5 2.4 %collective-permute-done.9.refs_0_ = bf16[2,128,128]{2,1,0:T(8,128)(2,1)S(1)} collective-permute-done((bf16[2,128,128]{2,1,0:T(8,128)(2,1)S(1)}, bf16[2,128,128]{2,1,0:T(8,128)(2,1)S(1)}, u32[]{:S(2)}, u32[]{:S(2)}) %collective-permute-start.9) | collective-permute-done | bytes 65568 | tf_op jit(solution)/shard_map/ppermute | solution.py:548
  55.9 1.3 %shard_map.88.refs_2_ = bf16[1024,2048]{1,0:T(8,128)(2,1)} custom-call(bf16[2,128,128]{2,1,0:T(8,128)(2,1)S(1)} %collective-permute-done.9.refs_0_, bf16[128,2048]{1,0:T(8,128)(2,1)S(1)} %get-tuple-element.43.refs_2_.refs_1_, bf16[1024,2048]{1,0:T(8,128)(2,1)} %shard_map.87.refs_2_), custom_call_target="tpu_custom_call", output_to_operand_aliasing={{}: (2, {})} | custom-call | flops 134217728 | bytes 1048576 | tf_op jit(solution)/shard_map/pallas_call | solution.py:54
  57.2 8.1 %collective-permute-done.8.refs_0_ = bf16[2,128,128]{2,1,0:T(8,128)(2,1)S(1)} collective-permute-done((bf16[2,128,128]{2,1,0:T(8,128)(2,1)S(1)}, bf16[2,128,128]{2,1,0:T(8,128)(2,1)S(1)}, u32[]{:S(2)}, u32[]{:S(2)}) %collective-permute-start.8) | collective-permute-done | bytes 65568 | tf_op jit(solution)/shard_map/ppermute | solution.py:548
  65.2 1.3 %shard_map.89.refs_2_ = bf16[1024,2048]{1,0:T(8,128)(2,1)} custom-call(bf16[2,128,128]{2,1,0:T(8,128)(2,1)S(1)} %collective-permute-done.8.refs_0_, bf16[128,2048]{1,0:T(8,128)(2,1)S(1)} %get-tuple-element.43.refs_2_.refs_1_, bf16[1024,2048]{1,0:T(8,128)(2,1)} %shard_map.88.refs_2_), custom_call_target="tpu_custom_call", output_to_operand_aliasing={{}: (2, {})} | custom-call | flops 134217728 | bytes 1048576 | tf_op jit(solution)/shard_map/pallas_call | solution.py:54
  66.5 1.3 %shard_map.90 = bf16[1024,2048]{1,0:T(8,128)(2,1)} custom-call(bf16[2,128,128]{2,1,0:T(8,128)(2,1)S(1)} %collective-permute-done.7.refs_0_, bf16[128,2048]{1,0:T(8,128)(2,1)S(1)} %get-tuple-element.43.refs_2_.refs_1_, bf16[1024,2048]{1,0:T(8,128)(2,1)} %shard_map.89.refs_2_), custom_call_target="tpu_custom_call", output_to_operand_aliasing={{}: (2, {})} | custom-call | flops 134217728 | bytes 1048576 | tf_op jit(solution)/shard_map/pallas_call | solution.py:54
  67.8 1.0 %shard_map.85 = bf16[128,3072]{1,0:T(8,128)(2,1)} custom-call(bf16[16,192,128]{2,1,0:T(8,128)(2,1)S(1)} %all-to-all-done.1.in_ref), custom_call_target="tpu_custom_call" | custom-call | bytes 1572864 | tf_op jit(solution)/shard_map/pallas_call | solution.py:54
  (23 shorter events, 0.8 us)
Async XLA Ops:
  2.8 26.9 %all-to-all-start = ((bf16[16,200,128]{2,1,0:T(8,128)(2,1)}), bf16[16,200,128]{2,1,0:T(8,128)(2,1)S(1)}, u32[]{:S(2)}, u32[]{:S(2)}) async-start(bf16[16,200,128]{2,1,0:T(8,128)(2,1)} %shard_map.77), calls=%async_computation | async-start | bytes 1638400 | tf_op jit(solution)/shard_map/all_to_all | solution.py:534
  9.0 2.2 %copy-start = (bf16[1024,2048]{1,0:T(8,128)(2,1)S(1)}, bf16[1024,2048]{1,0:T(8,128)(2,1)}, u32[]{:S(2)}) copy-start(bf16[1024,2048]{1,0:T(8,128)(2,1)} %weight_ref.1) | copy-start | bytes 12582916
  11.2 1.0 %copy-start.1 = (bf16[128,2048]{1,0:T(8,128)(2,1)S(1)}, bf16[128,2048]{1,0:T(8,128)(2,1)}, u32[]{:S(2)}) copy-start(bf16[128,2048]{1,0:T(8,128)(2,1)} %up_ref.1) | copy-start | bytes 1572868
  12.3 0.7 copy-start.2
  14.4 1.6 %collective-permute-start = (f32[4,128,128]{2,1,0:T(8,128)S(1)}, f32[4,128,128]{2,1,0:T(8,128)S(1)}, u32[]{:S(2)}, u32[]{:S(2)}) collective-permute-start(f32[4,128,128]{2,1,0:T(8,128)S(1)} %get-tuple-element.30), channel_id=1, source_target_pairs={{0,1},{1,0},{2,3},{3,2},{4,5},{5,4},{6,7},{7,6},{8,9},{9,8},{10,11... | collective-permute-start | bytes 786440 | tf_op jit(solution)/shard_map/ppermute | solution.py:548
  16.1 15.1 %collective-permute-start.1 = (f32[2,128,128]{2,1,0:T(8,128)S(1)}, f32[2,128,128]{2,1,0:T(8,128)S(1)}, u32[]{:S(2)}, u32[]{:S(2)}) collective-permute-start(f32[2,128,128]{2,1,0:T(8,128)S(1)} %pad_maximum_fusion), channel_id=1, source_target_pairs={{0,2},{1,3},{2,0},{3,1},{4,6},{5,7},{6,4},{7,5},{8,10},{9,11},{10,... | collective-permute-start | bytes 393224 | tf_op jit(solution)/shard_map/ppermute | solution.py:548
  17.6 13.6 %collective-permute-start.2 = (f32[2,128,128]{2,1,0:T(8,128)S(1)}, f32[2,128,128]{2,1,0:T(8,128)S(1)}, u32[]{:S(2)}, u32[]{:S(2)}) collective-permute-start(f32[2,128,128]{2,1,0:T(8,128)S(1)} %pad_maximum_fusion.1), channel_id=1, source_target_pairs={{0,4},{1,5},{2,6},{3,7},{4,0},{5,1},{6,2},{7,3},{8,12},{9,13},{10,... | collective-permute-start | bytes 393224 | tf_op jit(solution)/shard_map/ppermute | solution.py:548
  19.2 12.7 %collective-permute-start.3 = (f32[2,128,128]{2,1,0:T(8,128)S(1)}, f32[2,128,128]{2,1,0:T(8,128)S(1)}, u32[]{:S(2)}, u32[]{:S(2)}) collective-permute-start(f32[2,128,128]{2,1,0:T(8,128)S(1)} %pad_maximum_fusion.2), channel_id=1, source_target_pairs={{0,6},{1,7},{2,4},{3,5},{4,2},{5,3},{6,0},{7,1},{8,14},{9,15},{10,... | collective-permute-start | bytes 393224 | tf_op jit(solution)/shard_map/ppermute | solution.py:548
  31.1 4.9 %collective-permute-start.4 = (bf16[128,128]{1,0:T(8,128)(2,1)S(1)}, bf16[128,128]{1,0:T(8,128)(2,1)S(1)}, u32[]{:S(2)}, u32[]{:S(2)}) collective-permute-start(bf16[128,128]{1,0:T(8,128)(2,1)S(1)} %get-tuple-element.36), channel_id=1, source_target_pairs={{0,8},{1,9},{2,10},{3,11},{4,12},{5,13},{6,14},{7,15},{8,0},{9,1},... | collective-permute-start | bytes 98312 | tf_op jit(solution)/shard_map/ppermute | solution.py:500
  36.8 4.9 %collective-permute-start.5 = (bf16[128,128]{1,0:T(8,128)(2,1)S(1)}, bf16[128,128]{1,0:T(8,128)(2,1)S(1)}, u32[]{:S(2)}, u32[]{:S(2)}) collective-permute-start(bf16[128,128]{1,0:T(8,128)(2,1)S(1)} %get-tuple-element.40), channel_id=1, source_target_pairs={{0,8},{1,9},{2,10},{3,11},{4,12},{5,13},{6,14},{7,15},{8,0},{9,1},... | collective-permute-start | bytes 98312 | tf_op jit(solution)/shard_map/ppermute | solution.py:500
  42.7 25.1 %all-to-all-start.1 = ((bf16[16,192,128]{2,1,0:T(8,128)(2,1)}), bf16[16,192,128]{2,1,0:T(8,128)(2,1)S(1)}, u32[]{:S(2)}, u32[]{:S(2)}) async-start(bf16[16,192,128]{2,1,0:T(8,128)(2,1)} %shard_map.84), calls=%async_computation.1 | async-start | bytes 1572864 | tf_op jit(solution)/shard_map/all_to_all | solution.py:534
  47.1 1.4 %collective-permute-start.6 = (bf16[4,128,128]{2,1,0:T(8,128)(2,1)S(1)}, bf16[4,128,128]{2,1,0:T(8,128)(2,1)S(1)}, u32[]{:S(2)}, u32[]{:S(2)}) collective-permute-start(bf16[4,128,128]{2,1,0:T(8,128)(2,1)S(1)} %slice.78), channel_id=1, source_target_pairs={{0,1},{1,0},{2,3},{3,2},{4,5},{5,4},{6,7},{7,6},{8,9},{9,8},{10,11... | collective-permute-start | bytes 393224 | tf_op jit(solution)/shard_map/ppermute | solution.py:548
  48.5 16.7 %collective-permute-start.8 = (bf16[2,128,128]{2,1,0:T(8,128)(2,1)S(1)}, bf16[2,128,128]{2,1,0:T(8,128)(2,1)S(1)}, u32[]{:S(2)}, u32[]{:S(2)}) collective-permute-start(bf16[2,128,128]{2,1,0:T(8,128)(2,1)S(1)} %pad_maximum_fusion.4), channel_id=1, source_target_pairs={{0,6},{1,7},{2,4},{3,5},{4,2},{5,3},{6,0},{7,1},{8,14},{9,15},{10,... | collective-permute-start | bytes 196616 | tf_op jit(solution)/shard_map/ppermute | solution.py:548
  51.0 4.9 %collective-permute-start.9 = (bf16[2,128,128]{2,1,0:T(8,128)(2,1)S(1)}, bf16[2,128,128]{2,1,0:T(8,128)(2,1)S(1)}, u32[]{:S(2)}, u32[]{:S(2)}) collective-permute-start(bf16[2,128,128]{2,1,0:T(8,128)(2,1)S(1)} %pad_maximum_fusion.5), channel_id=1, source_target_pairs={{0,2},{1,3},{2,0},{3,1},{4,6},{5,7},{6,4},{7,5},{8,10},{9,11},{10,... | collective-permute-start | bytes 196616 | tf_op jit(solution)/shard_map/ppermute | solution.py:548
  51.6 14.9 %collective-permute-start.7 = (bf16[2,128,128]{2,1,0:T(8,128)(2,1)S(1)}, bf16[2,128,128]{2,1,0:T(8,128)(2,1)S(1)}, u32[]{:S(2)}, u32[]{:S(2)}) collective-permute-start(bf16[2,128,128]{2,1,0:T(8,128)(2,1)S(1)} %pad_maximum_fusion.3), channel_id=1, source_target_pairs={{0,4},{1,5},{2,6},{3,7},{4,0},{5,1},{6,2},{7,3},{8,12},{9,13},{10,... | collective-permute-start | bytes 196616 | tf_op jit(solution)/shard_map/ppermute | solution.py:548
